TPU v7x, 32 devices: a whole 2x2x4 slice. The times are simulated.
32 devices in a mesh: fsdp: 4 (over x, core), ctx: 4 (over z), tp: 2 (over y).
Axes of the slice: x: 2, y: 2, z: 4, core: 2. Of those that a mesh axis runs over, the one named last changes fastest.
Arguments:
- tokens: float32 [8192, 1536], P(('fsdp', 'ctx')), may hold values from -6 to 6
- cotangent: float32 [8192, 1536], P(('fsdp', 'ctx')), may hold values from -6 to 6
- seq_lengths: int32 [4, 6], P('fsdp'), may hold values from 1 to 1280, as said below
- deal: int32 [4, 8], P('fsdp'), may hold values from 0 to 7, as said below
- norm_gains: bfloat16 [2, 2, 1536], P(None, None, 'fsdp'), may hold values from 0.5 to 1.5
- query_key_value: bfloat16 [2, 3, 1536, 1536], P(None, None, 'fsdp', 'tp'), may hold values from -0.15625 to 0.15625
- forget_weight: bfloat16 [2, 1536, 24], P(None, 'fsdp', 'tp'), may hold values from -0.078125 to 0.078125
- forget_bias: bfloat16 [2, 24], P(None, 'tp'), may hold values from 1.5 to 7
- out_weight: bfloat16 [2, 1536, 1536], P(None, 'tp', 'fsdp'), may hold values from -0.75 to 0.75
- gate_up_weight: bfloat16 [2, 2, 1536, 4096], P(None, None, 'fsdp', 'tp'), may hold values from -0.15625 to 0.15625
- down_weight: bfloat16 [2, 4096, 1536], P(None, 'tp', 'fsdp'), may hold values from -0.09375 to 0.09375
Outputs:
- mixed_out: float32 [8192, 1536], P(('fsdp', 'ctx'))
- grad_tokens: float32 [8192, 1536], P(('fsdp', 'ctx'))
- grad_norm_gains: float32 [2, 2, 1536], P(None, None, 'fsdp')
- grad_query_key_value: float32 [2, 3, 1536, 1536], P(None, None, 'fsdp', 'tp')
- grad_forget_weight: float32 [2, 1536, 24], P(None, 'fsdp', 'tp')
- grad_forget_bias: float32 [2, 24], P(None, 'tp')
- grad_out_weight: float32 [2, 1536, 1536], P(None, 'tp', 'fsdp')
- grad_gate_up_weight: float32 [2, 2, 1536, 4096], P(None, None, 'fsdp', 'tp')
- grad_down_weight: float32 [2, 4096, 1536], P(None, 'tp', 'fsdp')
- rms_values: float32 [2, 3], replicated
Inputs may be any that keep to these rules, and one draw needn't show every extreme that they name: `seq_lengths`: the first sequence of each pack has 1280 tokens; each row sums to 2048. `deal`: each row is a permutation; entry 2 c lies below 4 and entry 2 c + 1 does not.
All inputs are finite; a program needn't handle non-finite values.
Results may differ from a plain program's by a relative error of at most 0.038.
Values may be sent and summed in bfloat16 or wider, within the bound.
A program may use at most 448 MiB of HBM per device.

v0:
```python
import math

import jax
import jax.numpy as jnp
from jax import lax
from jax.sharding import PartitionSpec as P

EPSILON = 1e-06
NEG_BIG = -1e30


def rms_factor(values):
    return lax.rsqrt(jnp.mean(values * values, axis=-1, keepdims=True) + EPSILON)


def norm_back(grad_normed, values, factor, gain_row):
    unit_rows = values * factor
    grad_gain = jnp.sum(grad_normed * unit_rows, axis=0)
    grad_unit = grad_normed * gain_row.astype(jnp.float32)
    inner_mean = jnp.mean(grad_unit * unit_rows, axis=-1, keepdims=True)
    return (factor * (grad_unit - unit_rows * inner_mean), grad_gain)


def by_blocks(values, index, block_rows):
    block_count = index.shape[0]
    shaped = values.reshape((block_count, block_rows) + values.shape[1:])
    return jnp.take(shaped, index, axis=0).reshape(values.shape)


def fetch_layer(
    layer_index, norm_gains, query_key_value, forget_weight, out_weight, gate_up_weight, down_weight
):
    return (
        lax.all_gather(norm_gains[layer_index], "fsdp", axis=1, tiled=True),
        lax.all_gather(query_key_value[layer_index], "fsdp", axis=1, tiled=True),
        lax.all_gather(forget_weight[layer_index], "fsdp", axis=0, tiled=True),
        lax.all_gather(out_weight[layer_index], "fsdp", axis=1, tiled=True),
        lax.all_gather(gate_up_weight[layer_index], "fsdp", axis=1, tiled=True),
        lax.all_gather(down_weight[layer_index], "fsdp", axis=1, tiled=True),
    )


def fetch_pack(keys_here, values_here, forget_here):
    return (
        lax.all_gather(keys_here, "ctx", axis=0, tiled=True),
        lax.all_gather(values_here, "ctx", axis=0, tiled=True),
        lax.all_gather(forget_here, "ctx", axis=0, tiled=True),
    )


def tp_combine(values):
    return lax.psum(values.astype(jnp.bfloat16), "tp").astype(jnp.float32)


def decay_of(forget_pack, deal_order, inverse, block_rows):
    initial = by_blocks(forget_pack.astype(jnp.float32), inverse, block_rows)
    return by_blocks(jnp.cumsum(initial, axis=0), deal_order, block_rows)


def score_block(queries, key_heads, decay_query, decay_key, allowed, score_scale):
    raw_scores = jnp.einsum("qhd,khd->hqk", queries, key_heads, preferred_element_type=jnp.float32)
    scores = raw_scores * score_scale + decay_query.T[:, :, None] - decay_key.T[:, None, :]
    return jnp.where(allowed[None], scores, NEG_BIG)


def attend_forward(queries, key_heads, value_heads, decay_query, decay_key, allowed, score_scale):
    scores = score_block(queries, key_heads, decay_query, decay_key, allowed, score_scale)
    peak_score = jnp.max(scores, axis=2, keepdims=True)
    exponent = jnp.exp(scores - peak_score)
    exp_total = jnp.sum(exponent, axis=2, keepdims=True)
    probabilities = (exponent / exp_total).astype(jnp.bfloat16)
    attended = jnp.einsum(
        "hqk,khd->qhd", probabilities, value_heads, preferred_element_type=jnp.float32
    )
    return (attended, peak_score + jnp.log(exp_total))


def attend_backward(
    queries,
    key_heads,
    value_heads,
    decay_query,
    decay_key,
    allowed,
    log_total,
    grad_attended,
    score_scale,
):
    scores = score_block(queries, key_heads, decay_query, decay_key, allowed, score_scale)
    probabilities = jnp.exp(scores - log_total)
    grad_probs = jnp.einsum(
        "qhd,khd->hqk", grad_attended, value_heads, preferred_element_type=jnp.float32
    )
    inner_sum = jnp.sum(probabilities * grad_probs, axis=2, keepdims=True)
    grad_scores = (probabilities * (grad_probs - inner_sum)).astype(jnp.bfloat16)
    grad_queries = (
        jnp.einsum("hqk,khd->qhd", grad_scores, key_heads, preferred_element_type=jnp.float32)
        * score_scale
    )
    grad_keys = (
        jnp.einsum("hqk,qhd->khd", grad_scores, queries, preferred_element_type=jnp.float32)
        * score_scale
    )
    grad_values = jnp.einsum(
        "hqk,qhd->khd",
        probabilities.astype(jnp.bfloat16),
        grad_attended,
        preferred_element_type=jnp.float32,
    )
    wide_scores = grad_scores.astype(jnp.float32)
    return (
        grad_queries,
        grad_keys,
        grad_values,
        jnp.sum(wide_scores, axis=2).T,
        jnp.sum(wide_scores, axis=1).T,
    )


def shards(
    tokens,
    cotangent,
    seq_lengths,
    deal,
    norm_gains,
    query_key_value,
    forget_weight,
    forget_bias,
    out_weight,
    gate_up_weight,
    down_weight,
):
    layer_count = query_key_value.shape[0]
    row_count, model_width = tokens.shape
    heads_here = forget_weight.shape[2]
    head_size = query_key_value.shape[3] // heads_here
    block_count = deal.shape[1]
    block_rows = row_count // 2
    pack_rows = block_count * block_rows
    score_scale = 1.0 / math.sqrt(head_size)
    deal_order = deal[0]
    inverse = (
        jnp.zeros((block_count,), jnp.int32)
        .at[deal_order]
        .set(jnp.arange(block_count, dtype=jnp.int32))
    )
    anchor = (
        deal_order[:, None] * block_rows + jnp.arange(block_rows, dtype=jnp.int32)[None, :]
    ).reshape(pack_rows)
    seq_ends = jnp.cumsum(seq_lengths[0])
    seq_of = jnp.sum((anchor[:, None] >= seq_ends[None, :]).astype(jnp.int32), axis=1)
    ctx_index = lax.axis_index("ctx")
    row_start = ctx_index * row_count
    allowed_blocks = []
    for half_index in range(2):
        first_row = row_start + half_index * block_rows
        anchor_query = lax.dynamic_slice_in_dim(anchor, first_row, block_rows)
        seq_query = lax.dynamic_slice_in_dim(seq_of, first_row, block_rows)
        allowed_blocks.append(
            (seq_query[:, None] == seq_of[None, :]) & (anchor[None, :] <= anchor_query[:, None])
        )
    residual = tokens
    kept_states = []
    stat_terms = []
    for layer_index in range(layer_count):
        fetched = fetch_layer(
            layer_index,
            norm_gains,
            query_key_value,
            forget_weight,
            out_weight,
            gate_up_weight,
            down_weight,
        )
        gain_rows, qkv_rows, forget_rows, out_rows, gate_up_rows, down_rows = fetched
        factor_one = rms_factor(residual)
        normed_local = (residual * factor_one * gain_rows[0].astype(jnp.float32)).astype(
            jnp.bfloat16
        )
        normed_one = normed_local
        projected = jnp.einsum(
            "td,jde->jte", normed_one, qkv_rows, preferred_element_type=jnp.float32
        ).astype(jnp.bfloat16)
        logits = jnp.dot(normed_one, forget_rows, preferred_element_type=jnp.float32) + forget_bias[
            layer_index
        ].astype(jnp.float32)
        forget_log = jax.nn.log_sigmoid(logits).astype(jnp.bfloat16)
        key_pack, value_pack, forget_pack = fetch_pack(projected[1], projected[2], forget_log)
        decay_pack = decay_of(forget_pack, deal_order, inverse, block_rows)
        key_heads = key_pack.reshape(pack_rows, heads_here, head_size)
        value_heads = value_pack.reshape(pack_rows, heads_here, head_size)
        query_heads = projected[0].reshape(row_count, heads_here, head_size)
        attended_parts = []
        log_totals = []
        for half_index in range(2):
            first_row = half_index * block_rows
            decay_query = lax.dynamic_slice_in_dim(decay_pack, row_start + first_row, block_rows)
            attended, log_total = attend_forward(
                query_heads[first_row : first_row + block_rows],
                key_heads,
                value_heads,
                decay_query,
                decay_pack,
                allowed_blocks[half_index],
                score_scale,
            )
            attended_parts.append(attended)
            log_totals.append(log_total)
        attended_all = (
            jnp.concatenate(attended_parts, axis=0)
            .reshape(row_count, heads_here * head_size)
            .astype(jnp.bfloat16)
        )
        branch_part = jnp.dot(attended_all, out_rows, preferred_element_type=jnp.float32)
        branch = tp_combine(branch_part)
        middle = residual + branch
        factor_two = rms_factor(middle)
        normed_two_local = (middle * factor_two * gain_rows[1].astype(jnp.float32)).astype(
            jnp.bfloat16
        )
        gate_up = jnp.einsum(
            "td,jdf->jtf", normed_two_local, gate_up_rows, preferred_element_type=jnp.float32
        )
        hidden = (jax.nn.silu(gate_up[0]) * gate_up[1]).astype(jnp.bfloat16)
        ffn_part = jnp.dot(hidden, down_rows, preferred_element_type=jnp.float32)
        ffn_branch = tp_combine(ffn_part)
        stat_terms.append(
            jnp.stack(
                [
                    jnp.sum(residual * residual),
                    jnp.sum(branch * branch),
                    jnp.sum(ffn_branch * ffn_branch),
                ]
            )
        )
        layer_state = {
            "residual": residual,
            "factor_one": factor_one,
            "normed_one": normed_one,
            "projected": projected,
            "logits": logits,
            "forget_log": forget_log,
            "log_totals": log_totals,
            "attended": attended_all,
            "middle": middle,
            "factor_two": factor_two,
            "normed_two": normed_two_local,
            "gate_up": gate_up,
            "hidden": hidden,
        }
        kept_states.append(layer_state)
        residual = middle + ffn_branch
    final_dealt, initial_grad = (
        lax.all_gather(residual.astype(jnp.bfloat16), "ctx", axis=0, tiled=True).astype(
            residual.dtype
        ),
        lax.all_gather(cotangent.astype(jnp.bfloat16), "ctx", axis=0, tiled=True).astype(
            cotangent.dtype
        ),
    )
    own_blocks = 2 * ctx_index + jnp.arange(2, dtype=jnp.int32)
    mixed_out = jnp.take(
        final_dealt.reshape(block_count, block_rows, model_width), inverse[own_blocks], axis=0
    ).reshape(row_count, model_width)
    grad_residual = jnp.take(
        initial_grad.reshape(block_count, block_rows, model_width), deal_order[own_blocks], axis=0
    ).reshape(row_count, model_width)
    grad_layers = [None] * layer_count
    bias_grads = [None] * layer_count
    for layer_index in reversed(range(layer_count)):
        layer_state = kept_states[layer_index]
        projected = layer_state["projected"]
        fetched = fetch_layer(
            layer_index,
            norm_gains,
            query_key_value,
            forget_weight,
            out_weight,
            gate_up_weight,
            down_weight,
        )
        key_pack, value_pack, forget_pack = fetch_pack(
            projected[1], projected[2], layer_state["forget_log"]
        )
        key_heads = key_pack.reshape(pack_rows, heads_here, head_size)
        value_heads = value_pack.reshape(pack_rows, heads_here, head_size)
        decay_pack = decay_of(forget_pack, deal_order, inverse, block_rows)
        gain_rows, qkv_rows, forget_rows, out_rows, gate_up_rows, down_rows = fetched
        grad_ffn = grad_residual.astype(jnp.bfloat16)
        grad_hidden = jnp.einsum(
            "td,fd->tf", grad_ffn, down_rows, preferred_element_type=jnp.float32
        )
        gate_values = layer_state["gate_up"][0]
        up_values = layer_state["gate_up"][1]
        gate_sigmoid = jax.nn.sigmoid(gate_values)
        grad_gate = (
            grad_hidden * up_values * gate_sigmoid * (1.0 + gate_values * (1.0 - gate_sigmoid))
        ).astype(jnp.bfloat16)
        grad_up = (grad_hidden * gate_values * gate_sigmoid).astype(jnp.bfloat16)
        grad_gate_up = jnp.stack([grad_gate, grad_up])
        two_part = jnp.einsum(
            "jtf,jdf->td", grad_gate_up, gate_up_rows, preferred_element_type=jnp.float32
        )
        grad_normed_two = tp_combine(two_part)
        grad_w_gate_up = jnp.einsum(
            "td,jtf->jdf",
            layer_state["normed_two"],
            grad_gate_up,
            preferred_element_type=jnp.float32,
        )
        grad_w_down = jnp.einsum(
            "tf,td->fd", layer_state["hidden"], grad_ffn, preferred_element_type=jnp.float32
        )
        grad_from_two, grad_gain_two = norm_back(
            grad_normed_two, layer_state["middle"], layer_state["factor_two"], gain_rows[1]
        )
        grad_residual = grad_residual + grad_from_two
        grad_branch = grad_residual.astype(jnp.bfloat16)
        grad_w_out = jnp.einsum(
            "te,td->ed", layer_state["attended"], grad_branch, preferred_element_type=jnp.float32
        )
        grad_attended = jnp.einsum(
            "td,ed->te", grad_branch, out_rows, preferred_element_type=jnp.float32
        ).astype(jnp.bfloat16)
        grad_attended = grad_attended.reshape(row_count, heads_here, head_size)
        query_heads = projected[0].reshape(row_count, heads_here, head_size)
        grad_key_pack = jnp.zeros((pack_rows, heads_here, head_size), jnp.float32)
        grad_value_pack = jnp.zeros((pack_rows, heads_here, head_size), jnp.float32)
        decay_grad = jnp.zeros((pack_rows, heads_here), jnp.float32)
        query_parts = []
        row_parts = []
        for half_index in range(2):
            first_row = half_index * block_rows
            decay_query = lax.dynamic_slice_in_dim(decay_pack, row_start + first_row, block_rows)
            grad_queries, grad_keys, grad_values, row_part, column_part = attend_backward(
                query_heads[first_row : first_row + block_rows],
                key_heads,
                value_heads,
                decay_query,
                decay_pack,
                allowed_blocks[half_index],
                layer_state["log_totals"][half_index],
                grad_attended[first_row : first_row + block_rows],
                score_scale,
            )
            grad_key_pack = grad_key_pack + grad_keys
            grad_value_pack = grad_value_pack + grad_values
            decay_grad = decay_grad - column_part
            query_parts.append(grad_queries)
            row_parts.append(row_part)
        own_decay = lax.dynamic_slice_in_dim(decay_grad, row_start, row_count) + jnp.concatenate(
            row_parts, axis=0
        )
        decay_grad = lax.dynamic_update_slice_in_dim(decay_grad, own_decay, row_start, 0)
        decay_initial = by_blocks(decay_grad, inverse, block_rows)
        forget_initial = jnp.flip(jnp.cumsum(jnp.flip(decay_initial, 0), axis=0), 0)
        forget_grad_pack = by_blocks(forget_initial, deal_order, block_rows)
        grad_keys_here, grad_values_here, grad_forget = (
            lax.psum_scatter(
                grad_key_pack.reshape(pack_rows, heads_here * head_size).astype(jnp.bfloat16),
                "ctx",
                scatter_dimension=0,
                tiled=True,
            ).astype(jnp.float32),
            lax.psum_scatter(
                grad_value_pack.reshape(pack_rows, heads_here * head_size).astype(jnp.bfloat16),
                "ctx",
                scatter_dimension=0,
                tiled=True,
            ).astype(jnp.float32),
            lax.psum_scatter(
                forget_grad_pack.astype(jnp.bfloat16), "ctx", scatter_dimension=0, tiled=True
            ).astype(jnp.float32),
        )
        grad_logits = (grad_forget * jax.nn.sigmoid(-layer_state["logits"])).astype(jnp.bfloat16)
        grad_queries_here = jnp.concatenate(query_parts, axis=0).reshape(
            row_count, heads_here * head_size
        )
        grad_qkv = jnp.stack([grad_queries_here, grad_keys_here, grad_values_here]).astype(
            jnp.bfloat16
        )
        normed_one = layer_state["normed_one"]
        one_part = jnp.einsum(
            "jte,jde->td", grad_qkv, qkv_rows, preferred_element_type=jnp.float32
        ) + jnp.einsum("th,dh->td", grad_logits, forget_rows, preferred_element_type=jnp.float32)
        grad_normed_one = tp_combine(one_part)
        grad_w_qkv = jnp.einsum(
            "td,jte->jde", normed_one, grad_qkv, preferred_element_type=jnp.float32
        )
        grad_w_forget = jnp.einsum(
            "td,th->dh", normed_one, grad_logits, preferred_element_type=jnp.float32
        )
        bias_grads[layer_index] = jnp.sum(grad_logits.astype(jnp.float32), axis=0)
        grad_from_one, grad_gain_one = norm_back(
            grad_normed_one, layer_state["residual"], layer_state["factor_one"], gain_rows[0]
        )
        grad_residual = grad_residual + grad_from_one
        row_shards = (
            lax.psum_scatter(
                jnp.stack([grad_gain_one, grad_gain_two]).astype(jnp.bfloat16),
                "fsdp",
                scatter_dimension=1,
                tiled=True,
            ).astype(jnp.float32),
            lax.psum_scatter(
                grad_w_qkv.astype(jnp.bfloat16), "fsdp", scatter_dimension=1, tiled=True
            ).astype(jnp.float32),
            lax.psum_scatter(
                grad_w_forget.astype(jnp.bfloat16), "fsdp", scatter_dimension=0, tiled=True
            ).astype(jnp.float32),
            lax.psum_scatter(
                grad_w_out.astype(jnp.bfloat16), "fsdp", scatter_dimension=1, tiled=True
            ).astype(jnp.float32),
            lax.psum_scatter(
                grad_w_gate_up.astype(jnp.bfloat16), "fsdp", scatter_dimension=1, tiled=True
            ).astype(jnp.float32),
            lax.psum_scatter(
                grad_w_down.astype(jnp.bfloat16), "fsdp", scatter_dimension=1, tiled=True
            ).astype(jnp.float32),
        )
        grad_layers[layer_index] = (
            lax.psum(row_shards[0].astype(jnp.bfloat16), "ctx").astype(jnp.float32),
            lax.psum(row_shards[1].astype(jnp.bfloat16), "ctx").astype(jnp.float32),
            lax.psum(row_shards[2].astype(jnp.bfloat16), "ctx").astype(jnp.float32),
            lax.psum(row_shards[3].astype(jnp.bfloat16), "ctx").astype(jnp.float32),
            lax.psum(row_shards[4].astype(jnp.bfloat16), "ctx").astype(jnp.float32),
            lax.psum(row_shards[5].astype(jnp.bfloat16), "ctx").astype(jnp.float32),
        )
    stat_sums, bias_sums = lax.psum((jnp.stack(stat_terms), jnp.stack(bias_grads)), ("fsdp", "ctx"))
    grad_gains = jnp.stack([item[0] for item in grad_layers])
    rms_values = jnp.sqrt(
        stat_sums / (row_count * model_width * lax.axis_size("fsdp") * lax.axis_size("ctx"))
    )
    grad_qkv_all = jnp.stack([item[1] for item in grad_layers])
    grad_forget_all = jnp.stack([item[2] for item in grad_layers])
    grad_out_all = jnp.stack([item[3] for item in grad_layers])
    grad_gate_up_all = jnp.stack([item[4] for item in grad_layers])
    grad_down_all = jnp.stack([item[5] for item in grad_layers])
    return (
        mixed_out,
        grad_residual,
        grad_gains,
        grad_qkv_all,
        grad_forget_all,
        bias_sums,
        grad_out_all,
        grad_gate_up_all,
        grad_down_all,
        rms_values,
    )


def solution(mesh):
    in_specs = (
        P(("fsdp", "ctx"), None),
        P(("fsdp", "ctx"), None),
        P("fsdp", None),
        P("fsdp", None),
        P(None, None, "fsdp"),
        P(None, None, "fsdp", "tp"),
        P(None, "fsdp", "tp"),
        P(None, "tp"),
        P(None, "tp", "fsdp"),
        P(None, None, "fsdp", "tp"),
        P(None, "tp", "fsdp"),
    )
    out_specs = (
        P(("fsdp", "ctx"), None),
        P(("fsdp", "ctx"), None),
        P(None, None, "fsdp"),
        P(None, None, "fsdp", "tp"),
        P(None, "fsdp", "tp"),
        P(None, "tp"),
        P(None, "tp", "fsdp"),
        P(None, None, "fsdp", "tp"),
        P(None, "tp", "fsdp"),
        P(),
    )
    return jax.shard_map(shards, mesh=mesh, in_specs=in_specs, out_specs=out_specs, check_vma=False)
```

profile of v0, /device:TPU:0, one launch (start us, length us, event | category | flops | bytes accessed | tf_op | source)
XLA Modules:
  0.0 3116.6 jit_solution(13313253531841158501)
XLA Ops:
  20.0 45.1 %all-gather.35.cloned.1.call-done = bf16[1,3,1536,768]{3,2,1,0:T(8,128)(2,1)} async-done(((bf16[1,3,384,768]{3,2,1,0:T(8,128)(2,1)}), bf16[1,3,1536,768]{3,2,1,0:T(8,128)(2,1)}) %all-gather.35.cloned.1.call-update) | async-done | bytes 7077904 | tf_op jit(solution)/shard_map/all_gather | solution.py:35
  111.0 28.8 all-gather.39.cloned.1.call-done
  167.5 36.7 %all-gather.37.cloned.1.call-done = bf16[1,2048,768]{2,1,0:T(8,128)(2,1)} async-done(((bf16[1,512,768]{2,1,0:T(8,128)(2,1)}), bf16[1,2048,768]{2,1,0:T(8,128)(2,1)}) %all-gather.37.cloned.1.call-update) | async-done | bytes 3145744 | tf_op jit(solution)/shard_map/all_gather | solution.py:46
  268.9 39.6 %all-reduce.13.cloned.1.call-done = bf16[512,1536]{1,0:T(8,128)(2,1)} async-done(((bf16[512,1536]{1,0:T(8,128)(2,1)}), bf16[512,1536]{1,0:T(8,128)(2,1)}) %all-reduce.13.cloned.1.call-update) | async-done | bytes 1572880 | tf_op jit(solution)/shard_map/psum | solution.py:52
  312.6 80.2 %all-gather.43.cloned.1.call-done = bf16[1,2,1536,2048]{3,2,1,0:T(8,128)(2,1)} async-done(((bf16[1,2,384,2048]{3,2,1,0:T(8,128)(2,1)}), bf16[1,2,1536,2048]{3,2,1,0:T(8,128)(2,1)}) %all-gather.43.cloned.1.call-update) | async-done | bytes 12582928 | tf_op jit(solution)/shard_map/all_gather | solution.py:38
  409.4 31.9 %all-gather.45.cloned.1.call-done = bf16[1,2048,1536]{2,1,0:T(8,128)(2,1)} async-done(((bf16[1,2048,384]{2,1,0:T(8,128)(2,1)}), bf16[1,2048,1536]{2,1,0:T(8,128)(2,1)}) %all-gather.45.cloned.1.call-update) | async-done | bytes 6291472 | tf_op jit(solution)/shard_map/all_gather | solution.py:39
  455.3 45.6 %all-reduce.15.cloned.1.call-done = bf16[512,1536]{1,0:T(8,128)(2,1)} async-done(((bf16[512,1536]{1,0:T(8,128)(2,1)}), bf16[512,1536]{1,0:T(8,128)(2,1)}) %all-reduce.15.cloned.1.call-update) | async-done | bytes 1572880 | tf_op jit(solution)/shard_map/psum | solution.py:52
  506.1 47.9 %all-gather.47.cloned.1.call-done = bf16[1,3,1536,768]{3,2,1,0:T(8,128)(2,1)} async-done(((bf16[1,3,384,768]{3,2,1,0:T(8,128)(2,1)}), bf16[1,3,1536,768]{3,2,1,0:T(8,128)(2,1)}) %all-gather.47.cloned.1.call-update) | async-done | bytes 7077904 | tf_op jit(solution)/shard_map/all_gather | solution.py:35
  597.5 30.8 all-gather.51.cloned.1.call-done
  656.6 35.5 %all-gather.49.cloned.1.call-done = bf16[1,2048,768]{2,1,0:T(8,128)(2,1)} async-done(((bf16[1,512,768]{2,1,0:T(8,128)(2,1)}), bf16[1,2048,768]{2,1,0:T(8,128)(2,1)}) %all-gather.49.cloned.1.call-update) | async-done | bytes 3145744 | tf_op jit(solution)/shard_map/all_gather | solution.py:46
  752.0 81.7 %all-gather.33.cloned.1.call-done = bf16[2048,1536]{1,0:T(8,128)(2,1)} async-done(((bf16[512,1536]{1,0:T(8,128)(2,1)}), bf16[2048,1536]{1,0:T(8,128)(2,1)}) %all-gather.33.cloned.1.call-update) | async-done | bytes 6291472 | tf_op jit(solution)/shard_map/all_gather | solution.py:257
  853.1 33.1 %all-reduce.17.cloned.1.call-done = bf16[512,1536]{1,0:T(8,128)(2,1)} async-done(((bf16[512,1536]{1,0:T(8,128)(2,1)}), bf16[512,1536]{1,0:T(8,128)(2,1)}) %all-reduce.17.cloned.1.call-update) | async-done | bytes 1572880 | tf_op jit(solution)/shard_map/psum | solution.py:52
  890.2 80.2 %all-gather.55.cloned.1.call-done = bf16[1,2,1536,2048]{3,2,1,0:T(8,128)(2,1)} async-done(((bf16[1,2,384,2048]{3,2,1,0:T(8,128)(2,1)}), bf16[1,2,1536,2048]{3,2,1,0:T(8,128)(2,1)}) %all-gather.55.cloned.1.call-update) | async-done | bytes 12582928 | tf_op jit(solution)/shard_map/all_gather | solution.py:38
  982.5 35.8 %all-gather.57.cloned.1.call-done = bf16[1,2048,1536]{2,1,0:T(8,128)(2,1)} async-done(((bf16[1,2048,384]{2,1,0:T(8,128)(2,1)}), bf16[1,2048,1536]{2,1,0:T(8,128)(2,1)}) %all-gather.57.cloned.1.call-update) | async-done | bytes 6291472 | tf_op jit(solution)/shard_map/all_gather | solution.py:39
  1041.6 50.4 %all-reduce.19.cloned.1.call-done = bf16[512,1536]{1,0:T(8,128)(2,1)} async-done(((bf16[512,1536]{1,0:T(8,128)(2,1)}), bf16[512,1536]{1,0:T(8,128)(2,1)}) %all-reduce.19.cloned.1.call-update) | async-done | bytes 1572880 | tf_op jit(solution)/shard_map/psum | solution.py:52
  1154.6 22.9 convert_reduce_fusion.6
  1261.3 26.0 reduce-scatter.45.cloned.1.call-done
  1287.3 62.6 %reduce-scatter.43.cloned.1.call-done = bf16[512,768]{1,0:T(8,128)(2,1)} async-done(((bf16[2048,768]{1,0:T(8,128)(2,1)}), bf16[512,768]{1,0:T(8,128)(2,1)}) %reduce-scatter.43.cloned.1.call-update) | async-done | bytes 786448 | tf_op jit(solution)/shard_map/reduce_scatter | solution.py:359
  1358.7 51.2 %all-reduce.21.cloned.1.call-done = bf16[512,1536]{1,0:T(8,128)(2,1)} async-done(((bf16[512,1536]{1,0:T(8,128)(2,1)}), bf16[512,1536]{1,0:T(8,128)(2,1)}) %all-reduce.21.cloned.1.call-update) | async-done | bytes 1572880 | tf_op jit(solution)/shard_map/psum | solution.py:52
  1439.4 50.8 %all-reduce.23.cloned.1.call-done = bf16[512,1536]{1,0:T(8,128)(2,1)} async-done(((bf16[512,1536]{1,0:T(8,128)(2,1)}), bf16[512,1536]{1,0:T(8,128)(2,1)}) %all-reduce.23.cloned.1.call-update) | async-done | bytes 1572880 | tf_op jit(solution)/shard_map/psum | solution.py:52
  1552.7 22.9 convert_reduce_fusion.2
  1685.0 62.6 %reduce-scatter.49.cloned.1.call-done = bf16[512,768]{1,0:T(8,128)(2,1)} async-done(((bf16[2048,768]{1,0:T(8,128)(2,1)}), bf16[512,768]{1,0:T(8,128)(2,1)}) %reduce-scatter.49.cloned.1.call-update) | async-done | bytes 786448 | tf_op jit(solution)/shard_map/reduce_scatter | solution.py:359
  1856.0 31.8 %copy.291 = bf16[2,1536,2048]{2,0,1:T(2,128)(2,1)} copy(bf16[2,1536,2048]{1,2,0:T(8,128)(2,1)} %convert_bitcast_fusion) | data formatting | bytes 25165824
  1948.6 31.9 %copy.289 = bf16[2,1536,2048]{2,0,1:T(2,128)(2,1)} copy(bf16[2,1536,2048]{1,2,0:T(8,128)(2,1)} %convert_bitcast_fusion.1) | data formatting | bytes 25165824
  2038.5 64.4 %reduce-scatter.61.cloned.1.call-done = bf16[384,2304]{1,0:T(8,128)(2,1)} async-done(((bf16[1536,2304]{1,0:T(8,128)(2,1)}), bf16[384,2304]{1,0:T(8,128)(2,1)}) %reduce-scatter.61.cloned.1.call-update) | async-done | bytes 1769488
  2109.9 95.2 %reduce-scatter.73.cloned.1.call-done = bf16[384,4096]{1,0:T(8,128)(2,1)} async-done(((bf16[1536,4096]{1,0:T(8,128)(2,1)}), bf16[384,4096]{1,0:T(8,128)(2,1)}) %reduce-scatter.73.cloned.1.call-update) | async-done | bytes 3145744
  2215.7 55.5 %reduce-scatter.59.cloned.1.call-done = bf16[384,2304]{1,0:T(8,128)(2,1)} async-done(((bf16[1536,2304]{1,0:T(8,128)(2,1)}), bf16[384,2304]{1,0:T(8,128)(2,1)}) %reduce-scatter.59.cloned.1.call-update) | async-done | bytes 1769488
  2278.2 94.8 %reduce-scatter.71.cloned.1.call-done = bf16[384,4096]{1,0:T(8,128)(2,1)} async-done(((bf16[1536,4096]{1,0:T(8,128)(2,1)}), bf16[384,4096]{1,0:T(8,128)(2,1)}) %reduce-scatter.71.cloned.1.call-update) | async-done | bytes 3145744
  2444.2 33.1 %all-reduce = (f32[2,12]{1,0:T(2,128)}, f32[2,3]{1,0:T(2,128)S(1)}) all-reduce(f32[2,12]{1,0:T(2,128)S(1)} %pad_maximum_fusion.18, f32[2,3]{1,0:T(2,128)S(1)} %pad_maximum_fusion.19), channel_id=1, replica_groups=mesh['fsdp'=4,'ctx'=4,'tp'=2] {'fsdp','ctx'}, use_global_device_ids=true, to_apply=%region_71.74 | all-reduce | flops 30 | bytes 240 | tf_op jit(solution)/shard_map/psum | solution.py:429
  2484.1 24.8 all-reduce.1
  2510.1 75.1 %all-gather.31.cloned.1.call-done = bf16[2048,1536]{1,0:T(8,128)(2,1)} async-done(((bf16[512,1536]{1,0:T(8,128)(2,1)}), bf16[2048,1536]{1,0:T(8,128)(2,1)}) %all-gather.31.cloned.1.call-update) | async-done | bytes 6291472 | tf_op jit(solution)/shard_map/all_gather | solution.py:254
  2602.7 467.4 %all-reduce.25.cloned.1.call-done = (bf16[1,3,384,768]{2,3,1,0:T(8,128)(2,1)}, bf16[1,3,384,768]{2,3,1,0:T(8,128)(2,1)}, bf16[1,768,384]{2,1,0:T(8,128)(2,1)}, b...) async-done(((bf16[1,3,384,768]{2,3,1,0:T(8,128)(2,1)}, ...) | async-done | bytes 14155792 | tf_op jit(solution)/shard_map/psum | solution.py:423
  (745 shorter events, 1122.9 us)
Async XLA Ops:
  75.2 129.0 %all-gather.37.cloned.1.call-start = ((), (), s32[]{:S(2)}) async-start(), calls=%async_computation.33 | async-start | bytes 3932160 | tf_op jit(solution)/shard_map/all_gather | solution.py:46
  75.9 177.8 %all-gather.41.cloned.1.call-start = ((), (), s32[]{:S(2)}) async-start(), calls=%async_computation.35 | async-start | bytes 2949120 | tf_op jit(solution)/shard_map/all_gather | solution.py:37
  77.1 231.4 %all-reduce.13.cloned.1.call-start = ((), (), s32[]{:S(2)}) async-start(), calls=%async_computation.18 | async-start | bytes 3145728 | tf_op jit(solution)/shard_map/psum | solution.py:52
  258.2 134.5 %all-gather.43.cloned.1.call-start = ((), (), s32[]{:S(2)}) async-start(), calls=%async_computation.36 | async-start | bytes 15728640 | tf_op jit(solution)/shard_map/all_gather | solution.py:38
  265.0 176.3 %all-gather.45.cloned.1.call-start = ((), (), s32[]{:S(2)}) async-start(), calls=%async_computation.37 | async-start | bytes 7864320 | tf_op jit(solution)/shard_map/all_gather | solution.py:39
  268.8 232.1 %all-reduce.15.cloned.1.call-start = ((), (), s32[]{:S(2)}) async-start(), calls=%async_computation.19 | async-start | bytes 3145728 | tf_op jit(solution)/shard_map/psum | solution.py:52
  450.0 178.3 %all-gather.51.cloned.1.call-start = ((), (), s32[]{:S(2)}) async-start(), calls=%async_computation.40 | async-start | bytes 3932160 | tf_op jit(solution)/shard_map/all_gather | solution.py:45
  564.4 179.9 %all-gather.53.cloned.1.call-start = ((), (), s32[]{:S(2)}) async-start(), calls=%async_computation.41 | async-start | bytes 2949120 | tf_op jit(solution)/shard_map/all_gather | solution.py:37
  565.0 268.7 %all-gather.33.cloned.1.call-start = ((), (), s32[]{:S(2)}) async-start(), calls=%async_computation.22 | async-start | bytes 7864320 | tf_op jit(solution)/shard_map/all_gather | solution.py:257
  568.3 317.9 %all-reduce.17.cloned.1.call-start = ((), (), s32[]{:S(2)}) async-start(), calls=%async_computation.20 | async-start | bytes 3145728 | tf_op jit(solution)/shard_map/psum | solution.py:52
  748.9 221.5 %all-gather.55.cloned.1.call-start = ((), (), s32[]{:S(2)}) async-start(), calls=%async_computation.42 | async-start | bytes 15728640 | tf_op jit(solution)/shard_map/all_gather | solution.py:38
  749.5 268.8 %all-gather.57.cloned.1.call-start = ((), (), s32[]{:S(2)}) async-start(), calls=%async_computation.43 | async-start | bytes 7864320 | tf_op jit(solution)/shard_map/all_gather | solution.py:39
  750.0 341.9 %all-reduce.19.cloned.1.call-start = ((), (), s32[]{:S(2)}) async-start(), calls=%async_computation.23 | async-start | bytes 3145728 | tf_op jit(solution)/shard_map/psum | solution.py:52
  1040.3 219.3 %reduce-scatter.47.cloned.1.call-start = ((), (), s32[]{:S(2)}) async-start(), calls=%async_computation.26 | async-start | bytes 81920 | tf_op jit(solution)/shard_map/reduce_scatter | solution.py:371
  1240.2 169.8 %all-reduce.21.cloned.1.call-start = ((), (), s32[]{:S(2)}) async-start(), calls=%async_computation.27 | async-start | bytes 3145728 | tf_op jit(solution)/shard_map/psum | solution.py:52
  1358.2 131.9 %all-reduce.23.cloned.1.call-start = ((), (), s32[]{:S(2)}) async-start(), calls=%async_computation.28 | async-start | bytes 3145728 | tf_op jit(solution)/shard_map/psum | solution.py:52
  1438.5 227.7 %reduce-scatter.53.cloned.1.call-start = ((), (), s32[]{:S(2)}) async-start(), calls=%async_computation.31 | async-start | bytes 81920 | tf_op jit(solution)/shard_map/reduce_scatter | solution.py:371
  1638.6 361.1 %all-reduce.27.cloned.1.call-start = ((), (), s32[]{:S(2)}) async-start(), calls=%async_computation.57 | async-start | bytes 6291456 | tf_op jit(solution)/shard_map/psum | solution.py:52
  1756.0 253.8 %reduce-scatter.69.cloned.1.call-start = ((), (), s32[]{:S(2)}) async-start(), calls=%async_computation.51 | async-start | bytes 2949120
  1765.3 246.6 %reduce-scatter.77.cloned.1.call-start = ((), (), s32[]{:S(2)}) async-start(), calls=%async_computation.55 | async-start | bytes 7864320
  1783.4 231.1 %reduce-scatter.67.cloned.1.call-start = ((), (), s32[]{:S(2)}) async-start(), calls=%async_computation.50 | async-start | bytes 2949120
  1793.7 242.2 %reduce-scatter.75.cloned.1.call-start = ((), (), s32[]{:S(2)}) async-start(), calls=%async_computation.54 | async-start | bytes 7864320
  1809.7 293.1 %reduce-scatter.61.cloned.1.call-start = ((), (), s32[]{:S(2)}) async-start(), calls=%async_computation.47 | async-start | bytes 8847360
  1841.9 363.3 %reduce-scatter.73.cloned.1.call-start = ((), (), s32[]{:S(2)}) async-start(), calls=%async_computation.53 | async-start | bytes 15728640
  1901.8 369.4 %reduce-scatter.59.cloned.1.call-start = ((), (), s32[]{:S(2)}) async-start(), calls=%async_computation.46 | async-start | bytes 8847360
  1934.5 438.6 %reduce-scatter.71.cloned.1.call-start = ((), (), s32[]{:S(2)}) async-start(), calls=%async_computation.52 | async-start | bytes 15728640
  1994.3 402.2 %reduce-scatter.65.cloned.1.call-start = ((), (), s32[]{:S(2)}) async-start(), calls=%async_computation.49 | async-start | bytes 491520
  1997.0 422.9 %reduce-scatter.57.cloned.1.call-start = ((), (), s32[]{:S(2)}) async-start(), calls=%async_computation.45 | async-start | bytes 491520
  1998.2 445.1 %reduce-scatter.63.cloned.1.call-start = ((), (), s32[]{:S(2)}) async-start(), calls=%async_computation.48 | async-start | bytes 491520
  1999.6 483.5 %reduce-scatter.55.cloned.1.call-start = ((), (), s32[]{:S(2)}) async-start(), calls=%async_computation.44 | async-start | bytes 491520
  2005.5 579.7 %all-gather.31.cloned.1.call-start = ((), (), s32[]{:S(2)}) async-start(), calls=%async_computation.21 | async-start | bytes 7864320 | tf_op jit(solution)/shard_map/all_gather | solution.py:254
  2009.5 1060.6 %all-reduce.25.cloned.1.call-start = ((), (), s32[]{:S(2)}) async-start(), calls=%async_computation.56 | async-start | bytes 28311552 | tf_op jit(solution)/shard_map/psum | solution.py:423
  (170 other events, 5027.7 us)
Sparse Core Ops, SparseCore 0:
  11.6 53.5 all-gather.34
  75.3 64.4 all-gather.38
  142.0 62.1 all-gather.36
  258.3 50.1 all-reduce.12
  310.6 82.0 all-gather.42
  395.0 46.2 all-gather.44
  449.4 51.4 all-reduce.14
  503.1 50.8 all-gather.46
  563.8 64.4 all-gather.50
  629.9 62.1 all-gather.48
  718.4 115.3 all-gather.32
  836.5 49.6 all-reduce.16
  888.3 82.0 all-gather.54
  971.9 46.2 all-gather.56
  1040.4 51.4 all-reduce.18
  1228.8 58.4 reduce-scatter.44
  1289.6 60.2 reduce-scatter.42
  1358.4 51.5 all-reduce.20
  1438.6 51.4 all-reduce.22
  1626.6 58.3 reduce-scatter.50
  1687.3 60.2 reduce-scatter.48
  1756.1 85.9 all-reduce.26
  1845.2 33.0 reduce-scatter.68
  1880.9 58.3 reduce-scatter.76
  1941.9 33.0 reduce-scatter.66
  1977.5 58.3 reduce-scatter.74
  2039.2 63.6 reduce-scatter.60
  2106.0 99.0 reduce-scatter.72
  2207.5 63.6 reduce-scatter.58
  2274.0 99.0 reduce-scatter.70
  2468.9 116.2 all-gather.30
  2590.2 479.8 all-reduce.24
  (8 shorter events, 166.2 us)
where the time goes:
time: 3130 us; the launch traced here: 3120 us
  waiting for transfers between devices  1900 us (61%)
  matrix products  488 us (16%)
  local copies, waits for them, and re-layouts  361 us (12%)
  other arithmetic  238 us (8%)
  blocking collectives  107 us (3%)
    psum x1, waiting for transfers between devices, shards(): lax.psum(row_shards[1].astype(jnp.bfloat16), 'ctx').astype(jnp.float32)  467 us
    unnamed x52, waiting for transfers between devices  386 us
    unnamed x400, local copies, waits for them, and re-layouts  284 us
    psum x7, waiting for transfers between devices, tp_combine(): return lax.psum(values.astype(jnp.bfloat16), 'tp').astype(jnp.float32)  271 us
    all_gather x2, waiting for transfers between devices, fetch_layer(): lax.all_gather(gate_up_weight[layer_index], 'fsdp', axis=1, tiled=True)  160 us
    reduce_scatter x2, waiting for transfers between devices, shards(): lax.psum_scatter(grad_key_pack.reshape(pack_rows, heads_here * head_size)...  125 us
    all_gather x2, waiting for transfers between devices, fetch_layer(): lax.all_gather(query_key_value[layer_index], 'fsdp', axis=1, tiled=True)  93 us
    all_gather x1, waiting for transfers between devices, shards(): lax.all_gather(cotangent.astype(jnp.bfloat16), 'ctx', axis=0, tiled=True)  81.7 us
  transfers between devices with their start and end apart: 40, of which 31 were waited for; matrix products, arithmetic and copies ran while one was open for 22% of the time, Pallas kernels for 0%

commit v1 on v0

v1 whole, which is shorter than its diff:
```python
import functools
import math

import jax
import jax.numpy as jnp
from jax import lax
from jax.experimental import pallas as pl
from jax.experimental.pallas import tpu as pltpu
from jax.sharding import PartitionSpec as P

EPSILON = 1e-06
NEG_BIG = -1e30
FIRST_LENGTH = 1280
BF16 = jnp.bfloat16
F32 = jnp.float32


def matmul(left, right):
    return jnp.dot(left, right, preferred_element_type=F32)


def split_three(values):
    high = values.astype(BF16).astype(F32)
    rest = values - high
    middle = rest.astype(BF16).astype(F32)
    return high, middle, rest - middle


def lanes_of(shape):
    return lax.broadcasted_iota(jnp.int32, shape, 1)


def with_lanes(base, first, columns):
    lane = lanes_of(base.shape)
    for offset, column in enumerate(columns):
        base = jnp.where(lane == first + offset, column, base)
    return base


def widen(values, width):
    rows, lanes = values.shape
    return jnp.concatenate([values, jnp.zeros((rows, width - lanes), values.dtype)], axis=1)


def key_range(block, block_rows):
    first_blocks = FIRST_LENGTH // block_rows
    return (0 if block < first_blocks else first_blocks), block + 1


def tile_mask(ends_ref, key_block, query_block, block_rows):
    shape = (block_rows, block_rows)
    mask = None
    if key_block == query_block:
        mask = lax.broadcasted_iota(jnp.int32, shape, 0) <= lax.broadcasted_iota(jnp.int32, shape, 1)
    if (query_block + 1) * block_rows > FIRST_LENGTH:
        key_pos = key_block * block_rows + lax.broadcasted_iota(jnp.int32, (block_rows, 1), 0)
        query_pos = query_block * block_rows + lax.broadcasted_iota(jnp.int32, (1, block_rows), 1)
        key_seq = jnp.zeros((block_rows, 1), jnp.int32)
        query_seq = jnp.zeros((1, block_rows), jnp.int32)
        for entry in range(ends_ref.shape[0]):
            key_seq = key_seq + (key_pos >= ends_ref[entry]).astype(jnp.int32)
            query_seq = query_seq + (query_pos >= ends_ref[entry]).astype(jnp.int32)
        same = key_seq == query_seq
        mask = same if mask is None else mask & same
    return mask


def place_pack(blk_ref, received, pack_ref, block_rows):
    for k, ref in enumerate(received):
        for half in range(2):
            start = pl.multiple_of(blk_ref[2 * k + half] * block_rows, block_rows)
            pack_ref[pl.ds(start, block_rows), :] = ref[half * block_rows : (half + 1) * block_rows, :]


def decay_blocks(pack_ref, forget_lane, block_count, block_rows):
    shape = (block_rows, block_rows)
    lower = (
        lax.broadcasted_iota(jnp.int32, shape, 0) >= lax.broadcasted_iota(jnp.int32, shape, 1)
    ).astype(BF16)
    carry = None
    out = []
    for block in range(block_count):
        rows = slice(block * block_rows, (block + 1) * block_rows)
        sums = matmul(lower, pack_ref[rows, forget_lane : forget_lane + 64])
        if carry is not None:
            sums = sums + carry
        carry = sums[block_rows - 1 : block_rows, :]
        out.append(sums)
    return out


def attend_kernel(hp, head_size, block_rows, blk_ref, ends_ref, *refs):
    count = (len(refs) - 6) // 2
    received, outs = refs[:count], refs[count : 2 * count]
    lse_ref, att_ref, pack_ref, key_ref, value_ref, out_ref = refs[2 * count :]
    block_count = 2 * count
    width = hp * head_size
    scale = 1.0 / math.sqrt(head_size)
    place_pack(blk_ref, received, pack_ref, block_rows)
    decays = decay_blocks(pack_ref, 3 * width, block_count, block_rows)
    masks = {}
    for block in range(block_count):
        for key_block in range(*key_range(block, block_rows)):
            if block not in masks or key_block != block:
                masks[block, key_block] = None
    for head in range(hp):
        query_tiles = []
        for block in range(block_count):
            rows = slice(block * block_rows, (block + 1) * block_rows)
            here = slice(head * head_size, (head + 1) * head_size)
            query = pack_ref[rows, here].astype(F32) * scale
            key = pack_ref[rows, width + here.start : width + here.stop].astype(F32)
            value = pack_ref[rows, 2 * width + here.start : 2 * width + here.stop].astype(F32)
            decay = decays[block][:, head : head + 1]
            high, middle, low = split_three(decay)
            key_ref[rows, :] = with_lanes(
                widen(key, 128), head_size, (-high, -middle, -low, 1.0, 1.0, 1.0)
            ).astype(BF16)
            value_ref[:, rows] = with_lanes(widen(value, 128), head_size, (1.0,)).T.astype(BF16)
            query_tiles.append(
                with_lanes(
                    widen(query, 128), head_size, (1.0, 1.0, 1.0, high, middle, low)
                ).T.astype(BF16)
            )
        for block in range(block_count):
            rows = slice(block * block_rows, (block + 1) * block_rows)
            first, last = key_range(block, block_rows)
            tiles = []
            peak = None
            for key_block in range(first, last):
                key_rows = slice(key_block * block_rows, (key_block + 1) * block_rows)
                scores = matmul(key_ref[key_rows, :], query_tiles[block])
                mask = tile_mask(ends_ref, key_block, block, block_rows)
                if mask is not None:
                    scores = jnp.where(mask, scores, NEG_BIG)
                top = jnp.max(scores, axis=0, keepdims=True)
                peak = top if peak is None else jnp.maximum(peak, top)
                tiles.append(scores)
            total = jnp.zeros((128, block_rows), F32)
            for key_block, scores in zip(range(first, last), tiles):
                key_rows = slice(key_block * block_rows, (key_block + 1) * block_rows)
                exponent = jnp.exp(scores - peak).astype(BF16)
                total = total + matmul(value_ref[:, key_rows], exponent)
            exp_total = total[head_size : head_size + 1, :]
            attended = total * (1.0 / exp_total)
            att_ref[head, :, rows] = attended[:head_size, :]
            lse_ref[head, :, rows] = peak + jnp.log(exp_total)
            out_ref[rows, head * head_size : (head + 1) * head_size] = attended.T[:, :head_size].astype(
                BF16
            )
    for k, ref in enumerate(outs):
        for half in range(2):
            start = pl.multiple_of(blk_ref[2 * k + half] * block_rows, block_rows)
            ref[:, half * width : (half + 1) * width] = out_ref[pl.ds(start, block_rows), :]


def attend_back_kernel(hp, head_size, block_rows, blk_ref, ends_ref, *refs):
    count = (len(refs) - 11) // 3
    received = refs[:count]
    grads = refs[count : 2 * count]
    lse_ref, att_ref = refs[2 * count : 2 * count + 2]
    outs = refs[2 * count + 2 : 3 * count + 2]
    (
        pack_ref,
        grad_ref,
        key_ref,
        value_ref,
        key_turned_ref,
        grad_key_ref,
        grad_value_ref,
        decay_ref,
        out_ref,
    ) = refs[3 * count + 2 :]
    block_count = 2 * count
    width = hp * head_size
    group = pack_ref.shape[1]
    scale = 1.0 / math.sqrt(head_size)
    place_pack(blk_ref, received, pack_ref, block_rows)
    for k, ref in enumerate(grads):
        for half in range(2):
            start = pl.multiple_of(blk_ref[2 * k + half] * block_rows, block_rows)
            grad_ref[pl.ds(start, block_rows), :] = ref[:, half * width : (half + 1) * width]
    decays = decay_blocks(pack_ref, 3 * width, block_count, block_rows)
    for head in range(hp):
        here = slice(head * head_size, (head + 1) * head_size)
        query_tiles = []
        query_plain = []
        grad_tiles = []
        for block in range(block_count):
            rows = slice(block * block_rows, (block + 1) * block_rows)
            query = pack_ref[rows, here].astype(F32) * scale
            key = pack_ref[rows, width + here.start : width + here.stop].astype(F32)
            value = pack_ref[rows, 2 * width + here.start : 2 * width + here.stop].astype(F32)
            grad = grad_ref[rows, here].astype(F32)
            high, middle, low = split_three(decays[block][:, head : head + 1])
            key_ref[rows, :] = with_lanes(
                widen(key, 128), head_size, (-high, -middle, -low, 1.0, 1.0, 1.0, 1.0, 1.0, 1.0)
            ).astype(BF16)
            key_turned_ref[:, rows] = with_lanes(widen(key, 128), head_size, (1.0,)).T.astype(BF16)
            value_ref[rows, :] = with_lanes(widen(value, 128), head_size, (1.0, 1.0, 1.0)).astype(BF16)
            query_wide = with_lanes(widen(query, 128), head_size, (1.0, 1.0, 1.0, high, middle, low)).T
            query_plain.append(with_lanes(widen(query, 128), head_size, (1.0,)).astype(BF16))
            row_index = lax.broadcasted_iota(jnp.int32, query_wide.shape, 0)
            for offset, part in enumerate(split_three(lse_ref[head, :, rows])):
                query_wide = jnp.where(row_index == head_size + 6 + offset, -part, query_wide)
            query_tiles.append(query_wide.astype(BF16))
            grad_turned = widen(grad, 128).T
            inner = jnp.sum(grad_turned[:head_size, :] * att_ref[head, :, rows], axis=0, keepdims=True)
            for offset, part in enumerate(split_three(inner)):
                grad_turned = jnp.where(row_index == head_size + offset, -part, grad_turned)
            grad_tiles.append(grad_turned.astype(BF16))
        for block in range(block_count):
            rows = slice(block * block_rows, (block + 1) * block_rows)
            first, last = key_range(block, block_rows)
            grad_query = jnp.zeros((128, block_rows), F32)
            for key_block in range(first, last):
                key_rows = slice(key_block * block_rows, (key_block + 1) * block_rows)
                scores = matmul(key_ref[key_rows, :], query_tiles[block])
                mask = tile_mask(ends_ref, key_block, block, block_rows)
                if mask is not None:
                    scores = jnp.where(mask, scores, NEG_BIG)
                probs = jnp.exp(scores)
                grad_scores = (probs * matmul(value_ref[key_rows, :], grad_tiles[block])).astype(BF16)
                grad_query = grad_query + matmul(key_turned_ref[:, key_rows], grad_scores)
                add_key = matmul(grad_scores, query_plain[block])
                add_value = matmul(probs.astype(BF16), grad_ref[rows, here])
                if key_block == block:
                    grad_key_ref[key_rows, :] = add_key
                    grad_value_ref[key_rows, :] = add_value
                else:
                    grad_key_ref[key_rows, :] += add_key
                    grad_value_ref[key_rows, :] += add_value
            turned = grad_query.T
            out_ref[rows, here] = (turned[:, :head_size] * scale).astype(BF16)
            decay_ref[rows, head : head + 1] = turned[:, head_size : head_size + 1]
        out_ref[:, width + here.start : width + here.stop] = grad_key_ref[:, :head_size].astype(BF16)
        out_ref[:, 2 * width + here.start : 2 * width + here.stop] = grad_value_ref[...].astype(BF16)
        decay_ref[:, head : head + 1] -= grad_key_ref[:, head_size : head_size + 1]
    shape = (block_rows, block_rows)
    upper = (
        lax.broadcasted_iota(jnp.int32, shape, 0) <= lax.broadcasted_iota(jnp.int32, shape, 1)
    ).astype(BF16)
    carry = None
    tail = group - 3 * width
    for block in reversed(range(block_count)):
        rows = slice(block * block_rows, (block + 1) * block_rows)
        sums = jnp.zeros((block_rows, 128), F32)
        values = jnp.where(lanes_of((block_rows, 128)) < hp, decay_ref[rows, :], 0.0)
        for part in split_three(values):
            sums = sums + matmul(upper, part.astype(BF16))
        if carry is not None:
            sums = sums + carry
        carry = sums[0:1, :]
        out_ref[rows, 3 * width : group] = sums[:, :tail].astype(BF16)
    for k, ref in enumerate(outs):
        for half in range(2):
            start = pl.multiple_of(blk_ref[2 * k + half] * block_rows, block_rows)
            ref[half * block_rows : (half + 1) * block_rows, :] = out_ref[pl.ds(start, block_rows), :]


def vmem_spec():
    return pl.BlockSpec(memory_space=pltpu.VMEM)


def smem_spec():
    return pl.BlockSpec(memory_space=pltpu.SMEM)


def attend(blk, ends, received, hp, head_size, block_rows):
    count = len(received)
    pack_rows = 2 * count * block_rows
    width = hp * head_size
    group = received[0].shape[1]
    out = pl.pallas_call(
        functools.partial(attend_kernel, hp, head_size, block_rows),
        out_shape=[jax.ShapeDtypeStruct((block_rows, 2 * width), BF16)] * count
        + [
            jax.ShapeDtypeStruct((hp, 1, pack_rows), F32),
            jax.ShapeDtypeStruct((hp, head_size, pack_rows), F32),
        ],
        in_specs=[smem_spec(), smem_spec()] + [vmem_spec()] * count,
        out_specs=[vmem_spec()] * (count + 2),
        scratch_shapes=[
            pltpu.VMEM((pack_rows, group), BF16),
            pltpu.VMEM((pack_rows, 128), BF16),
            pltpu.VMEM((128, pack_rows), BF16),
            pltpu.VMEM((pack_rows, width), BF16),
        ],
        compiler_params=pltpu.CompilerParams(vmem_limit_bytes=48 << 20),
        name="attend",
    )(blk, ends, *received)
    return out[:count], out[count], out[count + 1]


def attend_back(blk, ends, received, grads, lse, att, hp, head_size, block_rows):
    count = len(received)
    pack_rows = 2 * count * block_rows
    width = hp * head_size
    group = received[0].shape[1]
    return pl.pallas_call(
        functools.partial(attend_back_kernel, hp, head_size, block_rows),
        out_shape=[jax.ShapeDtypeStruct((2 * block_rows, group), BF16)] * count,
        in_specs=[smem_spec(), smem_spec()] + [vmem_spec()] * (2 * count + 2),
        out_specs=[vmem_spec()] * count,
        scratch_shapes=[
            pltpu.VMEM((pack_rows, group), BF16),
            pltpu.VMEM((pack_rows, width), BF16),
            pltpu.VMEM((pack_rows, 128), BF16),
            pltpu.VMEM((pack_rows, 128), BF16),
            pltpu.VMEM((128, pack_rows), BF16),
            pltpu.VMEM((pack_rows, 128), F32),
            pltpu.VMEM((pack_rows, head_size), F32),
            pltpu.VMEM((pack_rows, 128), F32),
            pltpu.VMEM((pack_rows, group), BF16),
        ],
        compiler_params=pltpu.CompilerParams(vmem_limit_bytes=48 << 20),
        name="attend_back",
    )(blk, ends, *received, *grads, lse, att)


def rms_factor(values):
    return lax.rsqrt(jnp.mean(values * values, axis=-1, keepdims=True) + EPSILON)


def norm_back(grad_normed, values, factor, gain_row):
    unit_rows = values * factor
    grad_gain = jnp.sum(grad_normed * unit_rows, axis=0)
    grad_unit = grad_normed * gain_row.astype(F32)
    inner_mean = jnp.mean(grad_unit * unit_rows, axis=-1, keepdims=True)
    return (factor * (grad_unit - unit_rows * inner_mean), grad_gain)


def swap(values, axis, size, step):
    return lax.ppermute(values, axis, [(i, i ^ step) for i in range(size)])


def halving(size):
    steps = []
    while size > 1:
        size //= 2
        steps.append(size)
    return steps


def shards(
    sizes,
    tokens,
    cotangent,
    seq_lengths,
    deal,
    norm_gains,
    query_key_value,
    forget_weight,
    forget_bias,
    out_weight,
    gate_up_weight,
    down_weight,
):
    fsdp, ctx, tp = sizes
    layer_count = query_key_value.shape[0]
    row_count, model_width = tokens.shape
    heads_here = forget_weight.shape[2]
    head_size = query_key_value.shape[3] // heads_here
    block_rows = row_count // 2
    piece = model_width // fsdp
    half_width = model_width // 2
    hp = -(-heads_here // ctx)
    heads_padded = hp * ctx
    width = hp * head_size
    group = -(-(3 * width + hp) // 128) * 128
    f_index = lax.axis_index("fsdp")
    c_index = lax.axis_index("ctx")
    fsdp_steps = halving(fsdp)
    offsets = [0]
    for step in fsdp_steps:
        offsets = offsets + [item ^ step for item in offsets]

    def gather(values, axis):
        for step in fsdp_steps:
            values = jnp.concatenate([values, swap(values, "fsdp", fsdp, step)], axis=axis)
        return values

    def add_low(left, right):
        return (left.astype(F32) + right.astype(F32)).astype(BF16)

    def scatter(near, far, axis):
        for step in reversed(fsdp_steps):
            near = add_low(near, swap(far, "fsdp", fsdp, step))
            if step != fsdp_steps[0]:
                size = near.shape[axis] // 2
                near, far = (
                    lax.slice_in_dim(near, 0, size, axis=axis),
                    lax.slice_in_dim(near, size, 2 * size, axis=axis),
                )
        return near

    def sum_ctx(values, kind):
        if ctx != 4:
            return lax.psum(values, "ctx")
        inward = (values + lax.ppermute(values, "ctx", [(0, 1), (3, 2)])).astype(kind)
        total = (inward + lax.ppermute(inward, "ctx", [(1, 2), (2, 1)])).astype(kind)
        outward = lax.ppermute(total, "ctx", [(1, 0), (2, 3)])
        return jnp.where((c_index == 0) | (c_index == 3), outward, total)

    def sum_tp(values):
        values = values.astype(BF16)
        step = 1
        while step < tp:
            values = values.astype(F32) + swap(values, "tp", tp, step).astype(F32)
            step *= 2
            if step < tp:
                values = values.astype(BF16)
        return values.astype(F32)

    def exchange(sends):
        return [sends[0]] + [swap(sends[k], "ctx", ctx, k) for k in range(1, ctx)]

    def to_local(values):
        return jnp.concatenate(
            [
                lax.dynamic_slice_in_dim(values, (f_index ^ item) * piece, piece, axis=1)
                for item in offsets
            ],
            axis=1,
        )

    def from_local(values):
        places = jnp.asarray([offsets.index(item) for item in range(fsdp)], jnp.int32)
        return jnp.concatenate(
            [
                lax.dynamic_slice_in_dim(values, places[f_index ^ item] * piece, piece, axis=1)
                for item in range(fsdp)
            ],
            axis=1,
        )

    def pick(items, index):
        out = items[0]
        for entry in range(1, len(items)):
            out = jnp.where(index == entry, items[entry], out)
        return out

    deal_order = deal[0]
    inverse = (
        jnp.zeros((2 * ctx,), jnp.int32).at[deal_order].set(jnp.arange(2 * ctx, dtype=jnp.int32))
    )
    seq_ends = jnp.cumsum(seq_lengths[0]).astype(jnp.int32)
    peers = jnp.bitwise_xor(jnp.arange(ctx, dtype=jnp.int32), c_index)
    blk = jnp.take(deal_order.reshape(ctx, 2), peers, axis=0).reshape(2 * ctx)

    def arrange_qkv(layer):
        weights = query_key_value[layer].reshape(3, piece, heads_here, head_size)
        forget = forget_weight[layer]
        if heads_padded != heads_here:
            more = heads_padded - heads_here
            weights = jnp.pad(weights, ((0, 0), (0, 0), (0, more), (0, 0)))
            forget = jnp.pad(forget, ((0, 0), (0, more)))
        weights = weights.reshape(3, piece, ctx, width).transpose(1, 2, 0, 3)
        parts = [
            weights.reshape(piece, ctx, 3 * width),
            forget.reshape(piece, ctx, hp),
            jnp.zeros((piece, ctx, group - 3 * width - hp), BF16),
        ]
        return jnp.concatenate(parts, axis=2).reshape(piece, ctx * group)

    gains = gather(norm_gains.reshape(2 * layer_count, piece), 1)
    weights = []
    for layer in range(layer_count):
        weights.append(
            (
                gather(arrange_qkv(layer), 0),
                gather(out_weight[layer], 1),
                gather(gate_up_weight[layer], 1),
                gather(down_weight[layer], 1),
            )
        )

    cot_blocks = cotangent.astype(BF16).reshape(2, block_rows, model_width)
    late_side = (c_index >= ctx // 2).astype(jnp.int32)
    cot_sends = []
    for k in range(ctx):
        wanted = deal_order[2 * (c_index ^ k) + late_side]
        cot_sends.append(lax.dynamic_index_in_dim(cot_blocks, wanted % 2, 0, keepdims=False))
    cot_got = exchange(cot_sends)
    cot_dealt = jnp.concatenate(
        [pick(cot_got, (deal_order[2 * c_index + half] // 2) ^ c_index) for half in range(2)], axis=0
    )
    grad_residual = to_local(cot_dealt).astype(F32)

    bias_all = forget_bias.astype(F32)
    if heads_padded != heads_here:
        bias_all = jnp.pad(bias_all, ((0, 0), (0, heads_padded - heads_here)))
    bias_all = bias_all.reshape(layer_count, ctx, hp)

    residual = to_local(tokens)
    kept = []
    stat_terms = []
    for layer in range(layer_count):
        qkv_rows, out_rows, gate_up_rows, down_rows = weights[layer]
        gain_one, gain_two = gains[2 * layer], gains[2 * layer + 1]
        factor_one = rms_factor(residual)
        normed_one = (residual * factor_one * gain_one.astype(F32)).astype(BF16)
        projected = matmul(normed_one, qkv_rows).reshape(row_count, ctx, group)
        logits = projected[:, :, 3 * width : 3 * width + hp] + bias_all[layer][None]
        forget_log = jax.nn.log_sigmoid(logits).astype(BF16)
        packed = jnp.concatenate(
            [
                projected[:, :, : 3 * width].astype(BF16),
                forget_log,
                jnp.zeros((row_count, ctx, group - 3 * width - hp), BF16),
            ],
            axis=2,
        )
        sends = [
            lax.dynamic_index_in_dim(packed, c_index ^ k, 1, keepdims=False) for k in range(ctx)
        ]
        received = exchange(sends)
        att_sends, lse, att_turned = attend(
            blk, seq_ends, received, hp, head_size, block_rows
        )
        att_got = jnp.stack(exchange(att_sends)).reshape(ctx, block_rows, 2, width)
        attended = jnp.take(att_got, peers, axis=0).transpose(2, 1, 0, 3)
        attended = attended.reshape(row_count, heads_padded * head_size)[:, : heads_here * head_size]
        branch = sum_tp(matmul(attended, out_rows))
        middle = residual + branch
        factor_two = rms_factor(middle)
        normed_two = (middle * factor_two * gain_two.astype(F32)).astype(BF16)
        gate_up = jnp.einsum("td,jdf->jtf", normed_two, gate_up_rows, preferred_element_type=F32)
        hidden = (jax.nn.silu(gate_up[0]) * gate_up[1]).astype(BF16)
        ffn_branch = sum_tp(matmul(hidden, down_rows))
        stat_terms += [
            jnp.sum(residual * residual),
            jnp.sum(branch * branch),
            jnp.sum(ffn_branch * ffn_branch),
        ]
        kept.append(
            dict(
                residual=residual,
                factor_one=factor_one,
                normed_one=normed_one,
                logits=logits,
                received=received,
                lse=lse,
                att_turned=att_turned,
                attended=attended,
                middle=middle,
                factor_two=factor_two,
                normed_two=normed_two,
                gate_up=gate_up,
                hidden=hidden,
            )
        )
        residual = middle + ffn_branch

    final_blocks = residual.astype(BF16).reshape(2, block_rows, model_width)
    out_got = exchange(
        [
            lax.dynamic_index_in_dim(
                final_blocks, ((c_index ^ k) >= ctx // 2).astype(jnp.int32), 0, keepdims=False
            )
            for k in range(ctx)
        ]
    )
    mixed_local = jnp.concatenate(
        [pick(out_got, (inverse[2 * c_index + half] // 2) ^ c_index) for half in range(2)], axis=0
    )
    mixed_out = from_local(mixed_local).astype(F32)

    grads = {}
    gain_grads = [None] * (2 * layer_count)
    bias_grads = [None] * layer_count
    for layer in reversed(range(layer_count)):
        state = kept[layer]
        qkv_rows, out_rows, gate_up_rows, down_rows = weights[layer]
        gain_one, gain_two = gains[2 * layer], gains[2 * layer + 1]
        grad_ffn = grad_residual.astype(BF16)
        grad_hidden = jnp.einsum("td,fd->tf", grad_ffn, down_rows, preferred_element_type=F32)
        gate_values, up_values = state["gate_up"][0], state["gate_up"][1]
        gate_sigmoid = jax.nn.sigmoid(gate_values)
        grad_gate = (
            grad_hidden * up_values * gate_sigmoid * (1.0 + gate_values * (1.0 - gate_sigmoid))
        ).astype(BF16)
        grad_up = (grad_hidden * gate_values * gate_sigmoid).astype(BF16)
        grad_gate_up = jnp.stack([grad_gate, grad_up])
        two_part = jnp.einsum("jtf,jdf->td", grad_gate_up, gate_up_rows, preferred_element_type=F32)
        grad_normed_two = sum_tp(two_part)

        def halves(values):
            return values[:, :half_width], values[:, half_width:]

        down_grad = scatter(
            *[
                jnp.einsum("tf,td->fd", state["hidden"], part, preferred_element_type=F32).astype(BF16)
                for part in halves(grad_ffn)
            ],
            1,
        )
        gate_up_grad = scatter(
            *[
                jnp.einsum("td,jtf->jdf", part, grad_gate_up, preferred_element_type=F32).astype(BF16)
                for part in halves(state["normed_two"])
            ],
            1,
        )
        grads["down", layer] = sum_ctx(down_grad, BF16).astype(F32)
        grads["gate_up", layer] = sum_ctx(gate_up_grad, BF16).astype(F32)
        grad_from_two, gain_grads[2 * layer + 1] = norm_back(
            grad_normed_two, state["middle"], state["factor_two"], gain_two
        )
        grad_residual = grad_residual + grad_from_two
        grad_branch = grad_residual.astype(BF16)
        grad_attended = jnp.einsum(
            "td,ed->te", grad_branch, out_rows, preferred_element_type=F32
        ).astype(BF16)
        out_grad = scatter(
            *[
                jnp.einsum("te,td->ed", state["attended"], part, preferred_element_type=F32).astype(BF16)
                for part in halves(grad_branch)
            ],
            1,
        )
        grads["out", layer] = sum_ctx(out_grad, BF16).astype(F32)
        if heads_padded != heads_here:
            more = (heads_padded - heads_here) * head_size
            grad_attended = jnp.pad(grad_attended, ((0, 0), (0, more)))
        grad_attended = grad_attended.reshape(2, block_rows, ctx, width).transpose(2, 1, 0, 3)
        grad_attended = grad_attended.reshape(ctx, block_rows, 2 * width)
        grad_got = exchange(
            [
                lax.dynamic_index_in_dim(grad_attended, c_index ^ k, 0, keepdims=False)
                for k in range(ctx)
            ]
        )
        back_sends = attend_back(
            blk,
            seq_ends,
            state["received"],
            grad_got,
            state["lse"],
            state["att_turned"],
            hp,
            head_size,
            block_rows,
        )
        back_got = jnp.take(jnp.stack(exchange(back_sends)), peers, axis=0).transpose(1, 0, 2)
        grad_forget = back_got[:, :, 3 * width : 3 * width + hp].astype(F32)
        grad_logits = (grad_forget * jax.nn.sigmoid(-state["logits"])).astype(BF16)
        grad_qkv = jnp.concatenate(
            [
                back_got[:, :, : 3 * width],
                grad_logits,
                jnp.zeros((row_count, ctx, group - 3 * width - hp), BF16),
            ],
            axis=2,
        ).reshape(row_count, ctx * group)
        bias_grads[layer] = jnp.sum(grad_logits.astype(F32), axis=0).reshape(heads_padded)[:heads_here]
        one_part = jnp.einsum("te,de->td", grad_qkv, qkv_rows, preferred_element_type=F32)
        grad_normed_one = sum_tp(one_part)
        qkv_grad = sum_ctx(
            scatter(
                *[
                    jnp.einsum("td,te->de", part, grad_qkv, preferred_element_type=F32).astype(BF16)
                    for part in halves(state["normed_one"])
                ],
                0,
            ),
            BF16,
        ).reshape(piece, ctx, group)
        grads["qkv", layer] = (
            qkv_grad[:, :, : 3 * width]
            .reshape(piece, ctx, 3, width)
            .transpose(2, 0, 1, 3)
            .reshape(3, piece, heads_padded * head_size)[:, :, : heads_here * head_size]
            .astype(F32)
        )
        grads["forget", layer] = (
            qkv_grad[:, :, 3 * width : 3 * width + hp]
            .reshape(piece, heads_padded)[:, :heads_here]
            .astype(F32)
        )
        grad_from_one, gain_grads[2 * layer] = norm_back(
            grad_normed_one, state["residual"], state["factor_one"], gain_one
        )
        grad_residual = grad_residual + grad_from_one
    grad_tokens = from_local(grad_residual)

    small = jnp.concatenate(
        [from_local(jnp.stack(gain_grads)).reshape(-1), jnp.stack(stat_terms)] + bias_grads
    )
    used = small.shape[0]
    small = jnp.pad(small, (0, -used % 1024)).reshape(-1, 128)
    for step in reversed(fsdp_steps):
        small = small + swap(small, "fsdp", fsdp, step)
    small = sum_ctx(small, F32).reshape(-1)
    gain_size = 2 * layer_count * model_width
    grad_gains = lax.dynamic_slice_in_dim(
        small[:gain_size].reshape(layer_count, 2, model_width), f_index * piece, piece, axis=2
    )
    stat_sums = small[gain_size : gain_size + 3 * layer_count].reshape(layer_count, 3)
    bias_sums = small[gain_size + 3 * layer_count : used].reshape(layer_count, heads_here)
    rms_values = jnp.sqrt(stat_sums / (row_count * model_width * fsdp * ctx))

    def both(name):
        return jnp.stack([grads[name, layer] for layer in range(layer_count)])

    return (
        mixed_out,
        grad_tokens,
        grad_gains,
        both("qkv"),
        both("forget"),
        bias_sums,
        both("out"),
        both("gate_up"),
        both("down"),
        rms_values,
    )


def solution(mesh):
    in_specs = (
        P(("fsdp", "ctx"), None),
        P(("fsdp", "ctx"), None),
        P("fsdp", None),
        P("fsdp", None),
        P(None, None, "fsdp"),
        P(None, None, "fsdp", "tp"),
        P(None, "fsdp", "tp"),
        P(None, "tp"),
        P(None, "tp", "fsdp"),
        P(None, None, "fsdp", "tp"),
        P(None, "tp", "fsdp"),
    )
    out_specs = (
        P(("fsdp", "ctx"), None),
        P(("fsdp", "ctx"), None),
        P(None, None, "fsdp"),
        P(None, None, "fsdp", "tp"),
        P(None, "fsdp", "tp"),
        P(None, "tp"),
        P(None, "tp", "fsdp"),
        P(None, None, "fsdp", "tp"),
        P(None, "tp", "fsdp"),
        P(),
    )
    sizes = (mesh.shape["fsdp"], mesh.shape["ctx"], mesh.shape["tp"])
    return jax.shard_map(
        functools.partial(shards, sizes),
        mesh=mesh,
        in_specs=in_specs,
        out_specs=out_specs,
        check_vma=False,
    )
```

time: 3130 us -> 1930 us (0.62)
  waiting for transfers between devices: 1900 us -> 986 us
  matrix products: 488 us -> 200 us
  starting transfers between devices: 3.81 us -> 226 us
  local copies, waits for them, and re-layouts: 361 us -> 187 us
  blocking collectives: 107 us -> 0 us
  Pallas kernels: 0 us -> 78.3 us
    ppermute x0 -> x101, waiting for transfers between devices: none -> 986 us  [the longest x74 599 us: swap(): return lax.ppermute(values, axis, [(i, i ^ step) for i in range(size)])]
    psum x8 -> x0, waiting for transfers between devices: 738 us -> none  [the longest x1 467 us: shards(): lax.psum(row_shards[1].astype(jnp.bfloat16), 'ctx').astype(jnp.float32)]
    all_gather x14 -> x0, waiting for transfers between devices: 610 us -> none  [the longest x2 160 us: fetch_layer(): lax.all_gather(gate_up_weight[layer_index], 'fsdp', axis=1, tiled=True)]
    unnamed x52 -> x0, waiting for transfers between devices: 386 us -> none
    dot_general x52 -> x30, matrix products: 469 us -> 174 us  [the longest x6 37 us: matmul(): return jnp.dot(left, right, preferred_element_type=F32)]
    ppermute x0 -> x101, starting transfers between devices: none -> 226 us  [the longest x74 148 us: swap(): return lax.ppermute(values, axis, [(i, i ^ step) for i in range(size)])]
    unnamed x400 -> x318, local copies, waits for them, and re-layouts: 284 us -> 60.5 us
    reduce_scatter x6 -> x0, waiting for transfers between devices: 168 us -> none  [the longest x2 125 us: shards(): lax.psum_scatter(grad_key_pack.reshape(pack_rows, heads_here * head_size)...]
  transfers between devices with their start and end apart: 40 -> 101, of which waited for: 31 -> 37; matrix products, arithmetic and copies ran while one was open for 22% -> 26% of each run, Pallas kernels for 0% -> 3%
where the time goes in v1:
time: 1930 us; the launch traced here: 1920 us
  waiting for transfers between devices  986 us (51%)
  starting transfers between devices  226 us (12%)
  other arithmetic  222 us (12%)
  matrix products  200 us (10%)
  local copies, waits for them, and re-layouts  187 us (10%)
  Pallas kernels  78.3 us (4%)
  between operations  23.5 us (1%)
    ppermute x74, waiting for transfers between devices, swap(): return lax.ppermute(values, axis, [(i, i ^ step) for i in range(size)])  599 us
    ppermute x9, waiting for transfers between devices, sum_ctx(): outward = lax.ppermute(total, 'ctx', [(1, 0), (2, 3)])  211 us
    ppermute x9, waiting for transfers between devices, sum_ctx(): lax.ppermute(values, 'ctx', [(0, 1), (3, 2)])  176 us
    ppermute x74, starting transfers between devices, swap(): return lax.ppermute(values, axis, [(i, i ^ step) for i in range(size)])  148 us
    unnamed x318, local copies, waits for them, and re-layouts  60.5 us
    ppermute x9, starting transfers between devices, sum_ctx(): lax.ppermute(values, 'ctx', [(0, 1), (3, 2)])  51.3 us
    pallas_call x2, Pallas kernels, attend_back(): pl.pallas_call(functools.partial(attend_back_kernel, hp, head_size, block...  50.6 us
  transfers between devices with their start and end apart: 101, of which 37 were waited for; matrix products, arithmetic and copies ran while one was open for 26% of the time, Pallas kernels for 3%

profile of v1, /device:TPU:0, one launch (start us, length us, event | category | flops | bytes accessed | tf_op | source)
XLA Modules:
  0.0 1922.7 jit_solution(15170684571695348032)
XLA Ops:
  23.8 42.8 %collective-permute-done.2 = bf16[384,2560]{0,1:T(8,128)(2,1)S(1)} collective-permute-done((bf16[384,2560]{0,1:T(8,128)(2,1)S(1)}, bf16[384,2560]{0,1:T(8,128)(2,1)S(1)}, u32[]{:S(2)}, u32[]{:S(2)}) %collective-permute-start.2) | collective-permute-done | bytes 1966112 | tf_op jit(solution)/shard_map/ppermute | solution.py:334
  87.1 61.4 %collective-permute-done = bf16[4,384]{1,0:T(4,128)(2,1)S(1)} collective-permute-done((bf16[4,384]{1,0:T(4,128)(2,1)S(1)}, bf16[4,384]{1,0:T(4,128)(2,1)S(1)}, u32[]{:S(2)}, u32[]{:S(2)}) %collective-permute-start) | collective-permute-done | bytes 3104 | tf_op jit(solution)/shard_map/ppermute | solution.py:334
  176.3 19.9 %collective-permute-done.4.refs_1_ = bf16[512,640]{1,0:T(8,128)(2,1)S(1)} collective-permute-done((bf16[512,640]{1,0:T(8,128)(2,1)}, bf16[512,640]{1,0:T(8,128)(2,1)S(1)}, u32[]{:S(2)}, u32[]{:S(2)}) %collective-permute-start.4) | collective-permute-done | bytes 655392 | tf_op jit(solution)/shard_map/ppermute | solution.py:334
  196.2 19.6 %collective-permute-done.5.refs_2_ = bf16[512,640]{1,0:T(8,128)(2,1)S(1)} collective-permute-done((bf16[512,640]{1,0:T(8,128)(2,1)}, bf16[512,640]{1,0:T(8,128)(2,1)S(1)}, u32[]{:S(2)}, u32[]{:S(2)}) %collective-permute-start.5) | collective-permute-done | bytes 655392 | tf_op jit(solution)/shard_map/ppermute | solution.py:334
  281.0 41.4 %collective-permute-done.15 = bf16[2048,384]{1,0:T(8,128)(2,1)} collective-permute-done((bf16[2048,384]{1,0:T(8,128)(2,1)}, bf16[2048,384]{1,0:T(8,128)(2,1)}, u32[]{:S(2)}, u32[]{:S(2)}) %collective-permute-start.15) | collective-permute-done | bytes 1572896 | tf_op jit(solution)/shard_map/ppermute | solution.py:334
  361.9 27.9 %collective-permute-done.29 = bf16[2,384,2048]{1,2,0:T(8,128)(2,1)} collective-permute-done((bf16[2,384,2048]{1,2,0:T(8,128)(2,1)}, bf16[2,384,2048]{1,2,0:T(8,128)(2,1)}, u32[]{:S(2)}, u32[]{:S(2)}) %collective-permute-start.29) | collective-permute-done | bytes 3145760 | tf_op jit(solution)/shard_map/ppermute | solution.py:334
  422.2 19.0 collective-permute-done.20.refs_1_
  444.1 17.3 collective-permute-done.21.refs_2_
  461.4 14.7 attend.3
  477.2 14.2 collective-permute-start.23
  555.3 43.2 %collective-permute-done.38 = bf16[256,1536]{1,0:T(8,128)(2,1)} collective-permute-done((bf16[256,1536]{1,0:T(8,128)(2,1)}, bf16[256,1536]{1,0:T(8,128)(2,1)}, u32[]{:S(2)}, u32[]{:S(2)}) %collective-permute-start.38) | collective-permute-done | bytes 786464 | tf_op jit(solution)/shard_map/ppermute | solution.py:334
  655.6 24.8 %collective-permute-done.40 = bf16[512,1536]{1,0:T(8,128)(2,1)} collective-permute-done((bf16[512,1536]{1,0:T(8,128)(2,1)}, bf16[512,1536]{1,0:T(8,128)(2,1)}, u32[]{:S(2)}, u32[]{:S(2)}) %collective-permute-start.40) | collective-permute-done | bytes 1572896 | tf_op jit(solution)/shard_map/ppermute | solution.py:334
  684.8 24.2 %collective-permute-done.33 = bf16[512,1536]{1,0:T(8,128)(2,1)} collective-permute-done((bf16[512,1536]{1,0:T(8,128)(2,1)}, bf16[512,1536]{1,0:T(8,128)(2,1)}, u32[]{:S(2)}, u32[]{:S(2)}) %collective-permute-start.33) | collective-permute-done | bytes 1572896 | tf_op jit(solution)/shard_map/ppermute | solution.py:334
  746.1 25.5 %attend_back.2 = (bf16[512,640]{1,0:T(8,128)(2,1)S(1)}, bf16[512,640]{1,0:T(8,128)(2,1)S(1)}, bf16[512,640]{1,0:T(8,128)(2,1)S(1)}, bf16[512,640]{1,0:T(8,128)(2,1)S(1)}) custom-call(s32[8]{0:T(128)S(1)} %select_n.371.blk_ref, s32[6]{0:T(128)S(1)} %bitcast.306, bf16[512,640]{1,0:T(8,128)(2,1)S(1)} %bitcast.299, ...), custom_call_target="tpu_custom_call" | custom-call | tf_op jit(solution)/shard_map/attend_back/pallas_call | solution.py:300
  781.9 15.3 collective-permute-done.44
  797.2 23.0 %collective-permute-done.45 = bf16[512,640]{1,0:T(8,128)(2,1)S(1)} collective-permute-done((bf16[512,640]{1,0:T(8,128)(2,1)S(1)}, bf16[512,640]{1,0:T(8,128)(2,1)S(1)}, u32[]{:S(2)}, u32[]{:S(2)}) %collective-permute-start.45) | collective-permute-done | bytes 655392 | tf_op jit(solution)/shard_map/ppermute | solution.py:334
  865.7 14.1 collective-permute-start.78
  980.2 25.1 %attend_back.3 = (bf16[512,640]{1,0:T(8,128)(2,1)S(1)}, bf16[512,640]{1,0:T(8,128)(2,1)S(1)}, bf16[512,640]{1,0:T(8,128)(2,1)S(1)}, bf16[512,640]{1,0:T(8,128)(2,1)S(1)}) custom-call(s32[8]{0:T(128)S(1)} %select_n.371.blk_ref, s32[6]{0:T(128)S(1)} %bitcast.307, bf16[512,640]{1,0:T(8,128)(2,1)S(1)} %bitcast.297, bf16[512,640]{1,0:T(8,128)(2,1)S(1)} %copy-done.1, ...), custom_call_target="tpu_custom_call" | custom-call | tf_op jit(solution)/shard_map/attend_back/pallas_call | solution.py:300
  1016.9 16.8 collective-permute-done.52
  1033.7 20.8 %collective-permute-done.53 = bf16[512,640]{1,0:T(8,128)(2,1)S(1)} collective-permute-done((bf16[512,640]{1,0:T(8,128)(2,1)S(1)}, bf16[512,640]{1,0:T(8,128)(2,1)S(1)}, u32[]{:S(2)}, u32[]{:S(2)}) %collective-permute-start.53) | collective-permute-done | bytes 655392 | tf_op jit(solution)/shard_map/ppermute | solution.py:334
  1054.6 14.6 collective-permute-start.98
  1159.7 90.8 %collective-permute-done.72 = bf16[768,384]{1,0:T(8,128)(2,1)S(1)} collective-permute-done((bf16[768,384]{1,0:T(8,128)(2,1)}, bf16[768,384]{1,0:T(8,128)(2,1)S(1)}, u32[]{:S(2)}, u32[]{:S(2)}) %collective-permute-start.72) | collective-permute-done | bytes 589856 | tf_op jit(solution)/shard_map/ppermute | solution.py:334
  1275.6 32.3 %collective-permute-start.36 = (bf16[256,1536]{1,0:T(8,128)(2,1)S(1)}, bf16[256,1536]{1,0:T(8,128)(2,1)S(1)}, u32[]{:S(2)}, u32[]{:S(2)}) collective-permute-start(bf16[256,1536]{1,0:T(8,128)(2,1)S(1)} %copy-done.106), channel_id=1, source_target_pairs={{0,2},{2,0},{4,6},{6,4},{1,3},{3,1},{5,7},{7,5},{8,10},{10,8},{12,... | collective-permute-start | bytes 2359304 | tf_op jit(solution)/shard_map/ppermute | solution.py:334
  1307.9 16.3 collective-permute-done.35
  1329.7 24.0 %collective-permute-done.92 = bf16[2048,384]{1,0:T(8,128)(2,1)} collective-permute-done((bf16[2048,384]{1,0:T(8,128)(2,1)}, bf16[2048,384]{1,0:T(8,128)(2,1)}, u32[]{:S(2)}, u32[]{:S(2)}) %collective-permute-start.92) | collective-permute-done | bytes 1572896 | tf_op jit(solution)/shard_map/ppermute | solution.py:334
  1380.1 29.1 %collective-permute-done.73 = bf16[768,384]{1,0:T(8,128)(2,1)S(1)} collective-permute-done((bf16[768,384]{1,0:T(8,128)(2,1)S(1)}, bf16[768,384]{1,0:T(8,128)(2,1)S(1)}, u32[]{:S(2)}, u32[]{:S(2)}) %collective-permute-start.73) | collective-permute-done | bytes 589856 | tf_op jit(solution)/shard_map/ppermute | solution.py:400
  1422.6 63.1 %collective-permute-done.93 = bf16[2048,384]{1,0:T(8,128)(2,1)S(1)} collective-permute-done((bf16[2048,384]{1,0:T(8,128)(2,1)S(1)}, bf16[2048,384]{1,0:T(8,128)(2,1)S(1)}, u32[]{:S(2)}, u32[]{:S(2)}) %collective-permute-start.93) | collective-permute-done | bytes 1572896 | tf_op jit(solution)/shard_map/ppermute | solution.py:400
  1512.1 81.9 %collective-permute-done.63 = bf16[384,2560]{1,0:T(8,128)(2,1)} collective-permute-done((bf16[384,2560]{1,0:T(8,128)(2,1)}, bf16[384,2560]{1,0:T(8,128)(2,1)}, u32[]{:S(2)}, u32[]{:S(2)}) %collective-permute-start.63) | collective-permute-done | bytes 1966112 | tf_op jit(solution)/shard_map/ppermute | solution.py:400
  1651.6 40.6 %collective-permute-done.95 = bf16[2048,384]{1,0:T(8,128)(2,1)} collective-permute-done((bf16[2048,384]{1,0:T(8,128)(2,1)}, bf16[2048,384]{1,0:T(8,128)(2,1)}, u32[]{:S(2)}, u32[]{:S(2)}) %collective-permute-start.95) | collective-permute-done | bytes 1572896 | tf_op jit(solution)/shard_map/ppermute | solution.py:402
  1703.5 30.9 %collective-permute-done.70 = bf16[384,2560]{1,0:T(8,128)(2,1)} collective-permute-done((bf16[384,2560]{1,0:T(8,128)(2,1)}, bf16[384,2560]{1,0:T(8,128)(2,1)}, u32[]{:S(2)}, u32[]{:S(2)}) %collective-permute-start.70) | collective-permute-done | bytes 1966112 | tf_op jit(solution)/shard_map/ppermute | solution.py:402
  1747.8 96.1 %collective-permute-done.65 = bf16[384,2560]{1,0:T(8,128)(2,1)} collective-permute-done((bf16[384,2560]{1,0:T(8,128)(2,1)S(1)}, bf16[384,2560]{1,0:T(8,128)(2,1)}, u32[]{:S(2)}, u32[]{:S(2)}) %collective-permute-start.65) | collective-permute-done | bytes 1966112 | tf_op jit(solution)/shard_map/ppermute | solution.py:402
  1867.2 35.0 %collective-permute-done.85 = bf16[2,384,2048]{1,2,0:T(8,128)(2,1)} collective-permute-done((bf16[2,384,2048]{1,2,0:T(8,128)(2,1)}, bf16[2,384,2048]{1,2,0:T(8,128)(2,1)}, u32[]{:S(2)}, u32[]{:S(2)}) %collective-permute-start.85) | collective-permute-done | bytes 3145760 | tf_op jit(solution)/shard_map/ppermute | solution.py:402
  (763 shorter events, 833.6 us)
Async XLA Ops:
  69.2 88.0 %collective-permute-start.3 = (bf16[768,2560]{0,1:T(8,128)(2,1)}, bf16[768,2560]{0,1:T(8,128)(2,1)}, u32[]{:S(2)}, u32[]{:S(2)}) collective-permute-start(bf16[768,2560]{0,1:T(8,128)(2,1)} %pad_maximum_fusion.18), channel_id=1, source_target_pairs={{0,8},{8,0},{16,24},{24,16},{1,9},{9,1},{17,25},{25,17},{2,10},{10... | collective-permute-start | bytes 11796488 | tf_op jit(solution)/shard_map/ppermute | solution.py:334
  80.5 92.8 %collective-permute-start.10 = (bf16[768,384]{1,0:T(8,128)(2,1)}, bf16[768,384]{1,0:T(8,128)(2,1)}, u32[]{:S(2)}, u32[]{:S(2)}) collective-permute-start(bf16[768,384]{1,0:T(8,128)(2,1)} %get-tuple-element.179), channel_id=1, source_target_pairs={{0,16},{8,24},{16,0},{24,8},{1,17},{9,25},{17,1},{25,9},{2,18},{10... | collective-permute-start | bytes 1769480 | tf_op jit(solution)/shard_map/ppermute | solution.py:334
  157.0 180.7 %collective-permute-start.14 = (bf16[2,768,2048]{1,2,0:T(8,128)(2,1)}, bf16[2,768,2048]{1,2,0:T(8,128)(2,1)}, u32[]{:S(2)}, u32[]{:S(2)}) collective-permute-start(bf16[2,768,2048]{1,2,0:T(8,128)(2,1)} %pad_maximum_fusion.4), channel_id=1, source_target_pairs={{0,8},{8,0},{16,24},{24,16},{1,9},{9,1},{17,25},{25,17},{2,10},{10... | collective-permute-start | bytes 18874376 | tf_op jit(solution)/shard_map/ppermute | solution.py:334
  175.6 92.9 %collective-permute-start.11 = (bf16[768,768]{1,0:T(8,128)(2,1)}, bf16[768,768]{1,0:T(8,128)(2,1)}, u32[]{:S(2)}, u32[]{:S(2)}) collective-permute-start(bf16[768,768]{1,0:T(8,128)(2,1)} %pad_maximum_fusion.55), channel_id=1, source_target_pairs={{0,8},{8,0},{16,24},{24,16},{1,9},{9,1},{17,25},{25,17},{2,10},{10... | collective-permute-start | bytes 3538952 | tf_op jit(solution)/shard_map/ppermute | solution.py:334
  279.1 110.7 %collective-permute-start.29 = (bf16[2,384,2048]{1,2,0:T(8,128)(2,1)}, bf16[2,384,2048]{1,2,0:T(8,128)(2,1)}, u32[]{:S(2)}, u32[]{:S(2)}) collective-permute-start(bf16[2,384,2048]{1,2,0:T(8,128)(2,1)} %bitcast.318), channel_id=1, source_target_pairs={{0,16},{8,24},{16,0},{24,8},{1,17},{9,25},{17,1},{25,9},{2,18},{10... | collective-permute-start | bytes 9437192 | tf_op jit(solution)/shard_map/ppermute | solution.py:334
  395.9 211.2 %collective-permute-start.30 = (bf16[2,768,2048]{1,2,0:T(8,128)(2,1)}, bf16[2,768,2048]{1,2,0:T(8,128)(2,1)}, u32[]{:S(2)}, u32[]{:S(2)}) collective-permute-start(bf16[2,768,2048]{1,2,0:T(8,128)(2,1)} %pad_maximum_fusion.6), channel_id=1, source_target_pairs={{0,8},{8,0},{16,24},{24,16},{1,9},{9,1},{17,25},{25,17},{2,10},{10... | collective-permute-start | bytes 18874376 | tf_op jit(solution)/shard_map/ppermute | solution.py:334
  422.2 102.9 %collective-permute-start.27 = (bf16[768,768]{1,0:T(8,128)(2,1)}, bf16[768,768]{1,0:T(8,128)(2,1)}, u32[]{:S(2)}, u32[]{:S(2)}) collective-permute-start(bf16[768,768]{1,0:T(8,128)(2,1)} %pad_maximum_fusion.56), channel_id=1, source_target_pairs={{0,8},{8,0},{16,24},{24,16},{1,9},{9,1},{17,25},{25,17},{2,10},{10... | collective-permute-start | bytes 3538952 | tf_op jit(solution)/shard_map/ppermute | solution.py:334
  441.2 93.7 %collective-permute-start.31 = (bf16[2048,384]{1,0:T(8,128)(2,1)}, bf16[2048,384]{1,0:T(8,128)(2,1)}, u32[]{:S(2)}, u32[]{:S(2)}) collective-permute-start(bf16[2048,384]{1,0:T(8,128)(2,1)} %get-tuple-element.150), channel_id=1, source_target_pairs={{0,16},{8,24},{16,0},{24,8},{1,17},{9,25},{17,1},{25,9},{2,18},{10... | collective-permute-start | bytes 4718600 | tf_op jit(solution)/shard_map/ppermute | solution.py:334
  779.5 130.8 %collective-permute-start.96 = (bf16[2048,768]{1,0:T(8,128)(2,1)}, bf16[2048,768]{1,0:T(8,128)(2,1)}, u32[]{:S(2)}, u32[]{:S(2)}) collective-permute-start(bf16[2048,768]{1,0:T(8,128)(2,1)} %convolution_convert_fusion.4), channel_id=1, source_target_pairs={{0,8},{8,0},{16,24},{24,16},{1,9},{9,1},{17,25},{25,17},{2,10},{10... | collective-permute-start | bytes 9437192 | tf_op jit(solution)/shard_map/ppermute | solution.py:334
  779.5 318.1 %collective-permute-start.86 = (bf16[2,768,2048]{1,2,0:T(8,128)(2,1)}, bf16[2,768,2048]{1,2,0:T(8,128)(2,1)}, u32[]{:S(2)}, u32[]{:S(2)}) collective-permute-start(bf16[2,768,2048]{1,2,0:T(8,128)(2,1)} %convert_bitcast_fusion), channel_id=1, source_target_pairs={{0,8},{8,0},{16,24},{24,16},{1,9},{9,1},{17,25},{25,17},{2,10},{10... | collective-permute-start | bytes 18874376 | tf_op jit(solution)/shard_map/ppermute | solution.py:334
  916.4 91.5 %collective-permute-start.97 = (bf16[2048,384]{1,0:T(8,128)(2,1)}, bf16[2048,384]{1,0:T(8,128)(2,1)}, u32[]{:S(2)}, u32[]{:S(2)}) collective-permute-start(bf16[2048,384]{1,0:T(8,128)(2,1)} %slice.338), channel_id=1, source_target_pairs={{0,16},{8,24},{16,0},{24,8},{1,17},{9,25},{17,1},{25,9},{2,18},{10... | collective-permute-start | bytes 4718600 | tf_op jit(solution)/shard_map/ppermute | solution.py:334
  979.4 137.5 %collective-permute-start.66 = (bf16[768,2560]{1,0:T(8,128)(2,1)}, bf16[768,2560]{1,0:T(8,128)(2,1)}, u32[]{:S(2)}, u32[]{:S(2)}) collective-permute-start(bf16[768,2560]{1,0:T(8,128)(2,1)} %convolution_convert_fusion), channel_id=1, source_target_pairs={{0,8},{8,0},{16,24},{24,16},{1,9},{9,1},{17,25},{25,17},{2,10},{10... | collective-permute-start | bytes 11796488 | tf_op jit(solution)/shard_map/ppermute | solution.py:334
  1033.7 110.9 %collective-permute-start.91 = (bf16[2048,768]{1,0:T(8,128)(2,1)}, bf16[2048,768]{1,0:T(8,128)(2,1)}, u32[]{:S(2)}, u32[]{:S(2)}) collective-permute-start(bf16[2048,768]{1,0:T(8,128)(2,1)} %convolution_convert_fusion.6), channel_id=1, source_target_pairs={{0,8},{8,0},{16,24},{24,16},{1,9},{9,1},{17,25},{25,17},{2,10},{10... | collective-permute-start | bytes 9437192 | tf_op jit(solution)/shard_map/ppermute | solution.py:334
  1054.5 95.8 %collective-permute-start.81 = (bf16[2,768,2048]{1,2,0:T(8,128)(2,1)}, bf16[2,768,2048]{1,2,0:T(8,128)(2,1)}, u32[]{:S(2)}, u32[]{:S(2)}) collective-permute-start(bf16[2,768,2048]{1,2,0:T(8,128)(2,1)} %convert_bitcast_fusion.1), channel_id=1, source_target_pairs={{0,8},{8,0},{16,24},{24,16},{1,9},{9,1},{17,25},{25,17},{2,10},{10... | collective-permute-start | bytes 18874376 | tf_op jit(solution)/shard_map/ppermute | solution.py:334
  1116.8 137.8 %collective-permute-start.61 = (bf16[768,2560]{1,0:T(8,128)(2,1)}, bf16[768,2560]{1,0:T(8,128)(2,1)}, u32[]{:S(2)}, u32[]{:S(2)}) collective-permute-start(bf16[768,2560]{1,0:T(8,128)(2,1)} %convolution_convert_fusion.2), channel_id=1, source_target_pairs={{0,8},{8,0},{16,24},{24,16},{1,9},{9,1},{17,25},{25,17},{2,10},{10... | collective-permute-start | bytes 11796488 | tf_op jit(solution)/shard_map/ppermute | solution.py:334
  1124.7 128.1 %collective-permute-start.87 = (bf16[2,384,2048]{1,2,0:T(8,128)(2,1)}, bf16[2,384,2048]{1,2,0:T(8,128)(2,1)}, u32[]{:S(2)}, u32[]{:S(2)}) collective-permute-start(bf16[2,384,2048]{1,2,0:T(8,128)(2,1)} %slice.332), channel_id=1, source_target_pairs={{0,16},{8,24},{16,0},{24,8},{1,17},{9,25},{17,1},{25,9},{2,18},{10... | collective-permute-start | bytes 9437192 | tf_op jit(solution)/shard_map/ppermute | solution.py:334
  1134.7 191.3 %collective-permute-start.67 = (bf16[384,2560]{1,0:T(8,128)(2,1)}, bf16[384,2560]{1,0:T(8,128)(2,1)}, u32[]{:S(2)}, u32[]{:S(2)}) collective-permute-start(bf16[384,2560]{1,0:T(8,128)(2,1)} %slice.312), channel_id=1, source_target_pairs={{0,16},{8,24},{16,0},{24,8},{1,17},{9,25},{17,1},{25,9},{2,18},{10... | collective-permute-start | bytes 5898248 | tf_op jit(solution)/shard_map/ppermute | solution.py:334
  1149.8 100.8 %collective-permute-start.72 = (bf16[768,384]{1,0:T(8,128)(2,1)}, bf16[768,384]{1,0:T(8,128)(2,1)S(1)}, u32[]{:S(2)}, u32[]{:S(2)}) collective-permute-start(bf16[768,384]{1,0:T(8,128)(2,1)} %slice.320), channel_id=1, source_target_pairs={{0,16},{8,24},{16,0},{24,8},{1,17},{9,25},{17,1},{25,9},{2,18},{10... | collective-permute-start | bytes 1769480 | tf_op jit(solution)/shard_map/ppermute | solution.py:334
  1150.3 102.0 %collective-permute-start.57 = (f32[56,128]{1,0:T(8,128)S(1)}, f32[56,128]{1,0:T(8,128)S(1)}, u32[]{:S(2)}, u32[]{:S(2)}) collective-permute-start(f32[56,128]{1,0:T(8,128)S(1)} %fusion.102), channel_id=1, source_target_pairs={{0,16},{8,24},{16,0},{24,8},{1,17},{9,25},{17,1},{25,9},{2,18},{10... | collective-permute-start | bytes 86024 | tf_op jit(solution)/shard_map/ppermute | solution.py:334
  1250.5 111.4 %collective-permute-start.82 = (bf16[2,384,2048]{1,2,0:T(8,128)(2,1)S(1)}, bf16[2,384,2048]{1,2,0:T(8,128)(2,1)}, u32[]{:S(2)}, u32[]{:S(2)}) collective-permute-start(bf16[2,384,2048]{1,2,0:T(8,128)(2,1)S(1)} %slice.328), channel_id=1, source_target_pairs={{0,16},{8,24},{16,0},{24,8},{1,17},{9,25},{17,1},{25,9},{2,18},{10... | collective-permute-start | bytes 9437192 | tf_op jit(solution)/shard_map/ppermute | solution.py:334
  1252.3 101.4 %collective-permute-start.92 = (bf16[2048,384]{1,0:T(8,128)(2,1)}, bf16[2048,384]{1,0:T(8,128)(2,1)}, u32[]{:S(2)}, u32[]{:S(2)}) collective-permute-start(bf16[2048,384]{1,0:T(8,128)(2,1)} %slice.336), channel_id=1, source_target_pairs={{0,16},{8,24},{16,0},{24,8},{1,17},{9,25},{17,1},{25,9},{2,18},{10... | collective-permute-start | bytes 4718600 | tf_op jit(solution)/shard_map/ppermute | solution.py:334
  1326.0 163.6 %collective-permute-start.88 = (bf16[2,384,2048]{1,2,0:T(8,128)(2,1)S(1)}, bf16[2,384,2048]{1,2,0:T(8,128)(2,1)}, u32[]{:S(2)}, u32[]{:S(2)}) collective-permute-start(bf16[2,384,2048]{1,2,0:T(8,128)(2,1)S(1)} %add_convert_fusion.4), channel_id=1, source_target_pairs={{0,2},{6,4},{1,3},{7,5},{8,10},{14,12},{9,11},{15,13},{16,18},{22,... | collective-permute-start | bytes 9437192 | tf_op jit(solution)/shard_map/ppermute | solution.py:400
  1377.6 125.7 %collective-permute-start.68 = (bf16[384,2560]{1,0:T(8,128)(2,1)}, bf16[384,2560]{1,0:T(8,128)(2,1)}, u32[]{:S(2)}, u32[]{:S(2)}) collective-permute-start(bf16[384,2560]{1,0:T(8,128)(2,1)} %add_convert_fusion.6), channel_id=1, source_target_pairs={{0,2},{6,4},{1,3},{7,5},{8,10},{14,12},{9,11},{15,13},{16,18},{22,... | collective-permute-start | bytes 5898248 | tf_op jit(solution)/shard_map/ppermute | solution.py:400
  1413.7 186.8 %collective-permute-start.83 = (bf16[2,384,2048]{1,2,0:T(8,128)(2,1)}, bf16[2,384,2048]{1,2,0:T(8,128)(2,1)}, u32[]{:S(2)}, u32[]{:S(2)}) collective-permute-start(bf16[2,384,2048]{1,2,0:T(8,128)(2,1)} %add_convert_fusion.5), channel_id=1, source_target_pairs={{0,2},{6,4},{1,3},{7,5},{8,10},{14,12},{9,11},{15,13},{16,18},{22,... | collective-permute-start | bytes 9437192 | tf_op jit(solution)/shard_map/ppermute | solution.py:400
  1420.0 174.0 %collective-permute-start.63 = (bf16[384,2560]{1,0:T(8,128)(2,1)}, bf16[384,2560]{1,0:T(8,128)(2,1)}, u32[]{:S(2)}, u32[]{:S(2)}) collective-permute-start(bf16[384,2560]{1,0:T(8,128)(2,1)} %add_convert_fusion.7), channel_id=1, source_target_pairs={{0,2},{6,4},{1,3},{7,5},{8,10},{14,12},{9,11},{15,13},{16,18},{22,... | collective-permute-start | bytes 5898248 | tf_op jit(solution)/shard_map/ppermute | solution.py:400
  1489.6 124.9 %collective-permute-start.94 = (bf16[2048,384]{1,0:T(8,128)(2,1)}, bf16[2048,384]{1,0:T(8,128)(2,1)}, u32[]{:S(2)}, u32[]{:S(2)}) collective-permute-start(bf16[2048,384]{1,0:T(8,128)(2,1)} %add.563), channel_id=1, source_target_pairs={{2,4},{4,2},{3,5},{5,3},{10,12},{12,10},{11,13},{13,11},{18,20},{2... | collective-permute-start | bytes 4718600 | tf_op jit(solution)/shard_map/ppermute | solution.py:401
  1503.3 126.8 %collective-permute-start.89 = (bf16[2,384,2048]{1,2,0:T(8,128)(2,1)}, bf16[2,384,2048]{1,2,0:T(8,128)(2,1)}, u32[]{:S(2)}, u32[]{:S(2)}) collective-permute-start(bf16[2,384,2048]{1,2,0:T(8,128)(2,1)} %add.559), channel_id=1, source_target_pairs={{2,4},{4,2},{3,5},{5,3},{10,12},{12,10},{11,13},{13,11},{18,20},{2... | collective-permute-start | bytes 9437192 | tf_op jit(solution)/shard_map/ppermute | solution.py:401
  1509.8 113.5 %collective-permute-start.69 = (bf16[384,2560]{1,0:T(8,128)(2,1)S(1)}, bf16[384,2560]{1,0:T(8,128)(2,1)S(1)}, u32[]{:S(2)}, u32[]{:S(2)}) collective-permute-start(bf16[384,2560]{1,0:T(8,128)(2,1)S(1)} %add.543), channel_id=1, source_target_pairs={{2,4},{4,2},{3,5},{5,3},{10,12},{12,10},{11,13},{13,11},{18,20},{2... | collective-permute-start | bytes 5898248 | tf_op jit(solution)/shard_map/ppermute | solution.py:401
  1630.1 104.2 %collective-permute-start.70 = (bf16[384,2560]{1,0:T(8,128)(2,1)}, bf16[384,2560]{1,0:T(8,128)(2,1)}, u32[]{:S(2)}, u32[]{:S(2)}) collective-permute-start(bf16[384,2560]{1,0:T(8,128)(2,1)} %add.544), channel_id=1, source_target_pairs={{2,0},{4,6},{3,1},{5,7},{10,8},{12,14},{11,9},{13,15},{18,16},{20,... | collective-permute-start | bytes 5898248 | tf_op jit(solution)/shard_map/ppermute | solution.py:402
  1641.3 223.6 %collective-permute-start.90 = (bf16[2,384,2048]{1,2,0:T(8,128)(2,1)}, bf16[2,384,2048]{1,2,0:T(8,128)(2,1)}, u32[]{:S(2)}, u32[]{:S(2)}) collective-permute-start(bf16[2,384,2048]{1,2,0:T(8,128)(2,1)} %add.560), channel_id=1, source_target_pairs={{2,0},{4,6},{3,1},{5,7},{10,8},{12,14},{11,9},{13,15},{18,16},{20,... | collective-permute-start | bytes 9437192 | tf_op jit(solution)/shard_map/ppermute | solution.py:402
  1648.7 195.2 %collective-permute-start.65 = (bf16[384,2560]{1,0:T(8,128)(2,1)S(1)}, bf16[384,2560]{1,0:T(8,128)(2,1)}, u32[]{:S(2)}, u32[]{:S(2)}) collective-permute-start(bf16[384,2560]{1,0:T(8,128)(2,1)S(1)} %add.540), channel_id=1, source_target_pairs={{2,0},{4,6},{3,1},{5,7},{10,8},{12,14},{11,9},{13,15},{18,16},{20,... | collective-permute-start | bytes 5898248 | tf_op jit(solution)/shard_map/ppermute | solution.py:402
  1699.1 203.2 %collective-permute-start.85 = (bf16[2,384,2048]{1,2,0:T(8,128)(2,1)}, bf16[2,384,2048]{1,2,0:T(8,128)(2,1)}, u32[]{:S(2)}, u32[]{:S(2)}) collective-permute-start(bf16[2,384,2048]{1,2,0:T(8,128)(2,1)} %add.556), channel_id=1, source_target_pairs={{2,0},{4,6},{3,1},{5,7},{10,8},{12,14},{11,9},{13,15},{18,16},{20,... | collective-permute-start | bytes 9437192 | tf_op jit(solution)/shard_map/ppermute | solution.py:402
  (222 other events, 6145.8 us)

commit v2 on v1

v2 whole, which is shorter than its diff:
```python
import functools
import math

import jax
import jax.numpy as jnp
from jax import lax
from jax.experimental import pallas as pl
from jax.experimental.layout import Layout, with_layout_constraint
from jax.experimental.pallas import tpu as pltpu
from jax.sharding import PartitionSpec as P

EPSILON = 1e-06
NEG_BIG = -1e30
FIRST_LENGTH = 1280
BF16 = jnp.bfloat16
F32 = jnp.float32


def matmul(left, right):
    return jnp.dot(left, right, preferred_element_type=F32)


def split_three(values):
    high = values.astype(BF16).astype(F32)
    rest = values - high
    middle = rest.astype(BF16).astype(F32)
    return high, middle, rest - middle


def iota(shape, dim):
    return lax.broadcasted_iota(jnp.int32, shape, dim)


def with_lanes(base, first, columns):
    lane = iota(base.shape, 1)
    for offset, column in enumerate(columns):
        base = jnp.where(lane == first + offset, column, base)
    return base


def with_rows(base, first, rows):
    row = iota(base.shape, 0)
    for offset, item in enumerate(rows):
        base = jnp.where(row == first + offset, item, base)
    return base


def first_lanes(values, lanes):
    return jnp.where(iota(values.shape, 1) < lanes, values, 0.0)


def widen(values, width=128):
    rows, lanes = values.shape
    return jnp.concatenate([values, jnp.zeros((rows, width - lanes), values.dtype)], axis=1)


class Pack:
    def __init__(self, hp, head_size):
        self.hp, self.head_size = hp, head_size
        self.value_tiles = (hp + 2) // 2
        self.tiles = hp + self.value_tiles

    def value_place(self, head):
        return self.hp + head // 2, (head % 2) * self.head_size


def peer(c, k):
    out, bit = c, 1
    while bit <= k:
        if k & bit:
            out = out + bit * (1 - 2 * ((c // bit) % 2))
        bit *= 2
    return out


def key_range(block, block_rows):
    first_blocks = FIRST_LENGTH // block_rows
    return (0 if block < first_blocks else first_blocks), block + 1


def score_tiles(block, block_rows, ends_ref):
    first, last = key_range(block, block_rows)
    if (block + 1) * block_rows <= FIRST_LENGTH:
        shape = (block_rows, block_rows)
        diagonal = (slice(block * block_rows, last * block_rows), iota(shape, 0) <= iota(shape, 1))
        if first == block:
            return [diagonal]
        return [(slice(first * block_rows, block * block_rows), None), diagonal]
    rows = (last - first) * block_rows
    key_pos = first * block_rows + iota((rows, 1), 0)
    query_pos = block * block_rows + iota((1, block_rows), 1)
    key_seq = jnp.zeros((rows, 1), jnp.int32)
    query_seq = jnp.zeros((1, block_rows), jnp.int32)
    for entry in range(ends_ref.shape[0]):
        key_seq = key_seq + (key_pos >= ends_ref[entry]).astype(jnp.int32)
        query_seq = query_seq + (query_pos >= ends_ref[entry]).astype(jnp.int32)
    mask = (key_pos <= query_pos) & (key_seq == query_seq)
    return [(slice(first * block_rows, last * block_rows), mask)]


def decay_blocks(load, block_count, block_rows):
    shape = (block_rows, block_rows)
    lower = (iota(shape, 0) >= iota(shape, 1)).astype(BF16)
    carry = None
    out = []
    for block in range(block_count):
        sums = matmul(lower, load(block))
        if carry is not None:
            sums = sums + carry
        carry = sums[block_rows - 1 : block_rows, :]
        out.append(sums)
    return out


def greet(count):
    c = lax.axis_index("ctx")
    barrier = pltpu.get_barrier_semaphore()
    for k in range(1, count):
        pl.semaphore_signal(
            barrier, inc=1, device_id={"ctx": peer(c, k)}, device_id_type=pl.DeviceIdType.MESH
        )
    pl.semaphore_wait(barrier, count - 1)
    return c


def move(k, c, source, target, send_sem, recv_sem):
    if k == 0:
        copy = pltpu.make_async_copy(source, target, recv_sem)
    else:
        copy = pltpu.make_async_remote_copy(
            src_ref=source,
            dst_ref=target,
            send_sem=send_sem,
            recv_sem=recv_sem,
            device_id={"ctx": peer(c, k)},
            device_id_type=pl.DeviceIdType.MESH,
        )
    copy.start()
    return copy


def arrive(k, copy):
    if k == 0:
        copy.wait()
    else:
        copy.wait_recv()


def attend_kernel(
    pack,
    place_ref,
    blk_ref,
    ends_ref,
    send_ref,
    out_ref,
    kept_ref,
    lse_ref,
    att_ref,
    key_ref,
    value_ref,
    block_ref,
    back_ref,
    in_send,
    in_recv,
    out_send,
    out_recv,
    keep_sem,
    *recv_refs,
):
    count = send_ref.shape[0]
    block_rows = send_ref.shape[3]
    block_count = 2 * count
    hp, head_size = pack.hp, pack.head_size
    scale = 1.0 / math.sqrt(head_size)
    c = greet(count)
    copies = {}
    order = [pack.value_place(hp)[0]]
    for head in range(hp):
        order += [item for item in (head, pack.value_place(head)[0]) if item not in order]
    for tile in order:
        for k in reversed(range(count)):
            copies[tile, k] = move(
                k,
                c,
                send_ref.at[k, tile],
                recv_refs[tile].at[pl.ds(2 * k, 2)],
                in_send.at[tile, k],
                in_recv.at[tile, k],
            )
    keeps = []
    here = set()

    def need(tile):
        if tile not in here:
            here.add(tile)
            for k in range(count):
                arrive(k, copies[tile, k])
            keep = pltpu.make_async_copy(recv_refs[tile], kept_ref.at[tile], keep_sem.at[tile])
            keep.start()
            keeps.append(keep)

    tile, lane = pack.value_place(hp)
    need(tile)
    decays = decay_blocks(
        lambda block: recv_refs[tile][place_ref[block]][:, lane : lane + head_size], block_count, block_rows
    )
    returns = []
    for head in range(hp):
        need(head)
        value_tile, value_lane = pack.value_place(head)
        need(value_tile)
        query_tiles = []
        for block in range(block_count):
            rows = slice(block * block_rows, (block + 1) * block_rows)
            pair = recv_refs[head][place_ref[block]].astype(F32)
            value = recv_refs[value_tile][place_ref[block]].astype(F32)
            value = value[:, value_lane : value_lane + head_size]
            high, middle, low = split_three(decays[block][:, head : head + 1])
            key_ref[rows, :] = with_lanes(
                widen(pair[:, head_size:]), head_size, (-high, -middle, -low, 1.0, 1.0, 1.0)
            ).astype(BF16)
            value_ref[:, rows] = with_lanes(widen(value), head_size, (1.0,)).T.astype(BF16)
            query_tiles.append(
                with_lanes(first_lanes(pair * scale, head_size), head_size, (1.0, 1.0, 1.0, high, middle, low))
                .T.astype(BF16)
            )
        for block in range(block_count):
            rows = slice(block * block_rows, (block + 1) * block_rows)
            tiles = []
            peak = None
            for key_rows, mask in score_tiles(block, block_rows, ends_ref):
                scores = matmul(key_ref[key_rows, :], query_tiles[block])
                if mask is not None:
                    scores = jnp.where(mask, scores, NEG_BIG)
                top = jnp.max(scores, axis=0, keepdims=True)
                peak = top if peak is None else jnp.maximum(peak, top)
                tiles.append((key_rows, scores))
            total = jnp.zeros((128, block_rows), F32)
            for key_rows, scores in tiles:
                total = total + matmul(value_ref[:, key_rows], jnp.exp(scores - peak).astype(BF16))
            exp_total = total[head_size : head_size + 1, :]
            attended = total * (1.0 / exp_total)
            att_ref[head, :, rows] = attended[:head_size, :]
            lse_ref[head, :, rows] = peak + jnp.log(exp_total)
            block_ref[head, block] = attended.T.astype(BF16)
        for k in range(count):
            back_ref[k, head] = jnp.concatenate(
                [
                    block_ref[head, blk_ref[2 * k]][:, :head_size],
                    block_ref[head, blk_ref[2 * k + 1]][:, :head_size],
                ],
                axis=1,
            )
        for k in reversed(range(count)):
            returns.append(
                (
                    k,
                    move(
                        k,
                        c,
                        back_ref.at[k, head],
                        out_ref.at[k, head],
                        out_send.at[k, head],
                        out_recv.at[k, head],
                    ),
                )
            )
    for k, copy in returns:
        copy.wait()
    for (tile, k), copy in copies.items():
        if k:
            copy.wait_send()
    for keep in keeps:
        keep.wait()


def attend_back_kernel(
    pack,
    place_ref,
    blk_ref,
    ends_ref,
    kept_ref,
    lse_ref,
    att_ref,
    send_ref,
    out_ref,
    key_ref,
    value_ref,
    turned_ref,
    plain_ref,
    grad_key_ref,
    grad_value_ref,
    decay_ref,
    block_ref,
    back_ref,
    in_send,
    in_recv,
    out_send,
    out_recv,
    *grad_refs,
):
    count = send_ref.shape[0]
    block_rows = send_ref.shape[2]
    block_count = 2 * count
    hp, head_size = pack.hp, pack.head_size
    scale = 1.0 / math.sqrt(head_size)
    c = greet(count)
    copies = {}
    for head in range(hp):
        for k in reversed(range(count)):
            copies[head, k] = move(
                k,
                c,
                send_ref.at[k, head],
                grad_refs[head].at[k],
                in_send.at[head, k],
                in_recv.at[head, k],
            )
    tile, lane = pack.value_place(hp)
    decays = decay_blocks(
        lambda block: kept_ref[tile, place_ref[block]][:, lane : lane + head_size], block_count, block_rows
    )
    returns = []

    def give(tile):
        for k in range(count):
            for half in range(2):
                back_ref[tile, k, half] = block_ref[tile, blk_ref[2 * k + half]]
        for k in reversed(range(count)):
            returns.append(
                move(
                    k,
                    c,
                    back_ref.at[tile, k],
                    out_ref.at[k, tile],
                    out_send.at[tile, k],
                    out_recv.at[tile, k],
                )
            )

    for head in range(hp):
        value_tile, value_lane = pack.value_place(head)
        query_tiles = []
        for block in range(block_count):
            rows = slice(block * block_rows, (block + 1) * block_rows)
            pair = kept_ref[head, place_ref[block]].astype(F32)
            value = kept_ref[value_tile, place_ref[block]].astype(F32)
            value = value[:, value_lane : value_lane + head_size]
            key = pair[:, head_size:]
            query = first_lanes(pair * scale, head_size)
            high, middle, low = split_three(decays[block][:, head : head + 1])
            key_ref[rows, :] = with_lanes(
                widen(key), head_size, (-high, -middle, -low, 1.0, 1.0, 1.0, 1.0, 1.0, 1.0)
            ).astype(BF16)
            turned_ref[:, rows] = with_lanes(widen(key), head_size, (1.0,)).T.astype(BF16)
            value_ref[rows, :] = with_lanes(widen(value), head_size, (1.0, 1.0, 1.0)).astype(BF16)
            plain_ref[rows, :] = with_lanes(query, head_size, (1.0,)).astype(BF16)
            query_wide = with_lanes(query, head_size, (1.0, 1.0, 1.0, high, middle, low)).T
            log_parts = [-part for part in split_three(lse_ref[head, :, rows])]
            query_tiles.append(with_rows(query_wide, head_size + 6, log_parts).astype(BF16))
        for k in range(count):
            arrive(k, copies[head, k])
        grad_plain = []
        grad_tiles = []
        for block in range(block_count):
            rows = slice(block * block_rows, (block + 1) * block_rows)
            place = place_ref[block]
            both = grad_refs[head][place // 2].astype(F32)
            grad = jnp.where(place % 2 == 0, both[:, :head_size], both[:, head_size:])
            grad_plain.append(grad.astype(BF16))
            grad_turned = widen(grad).T
            inner = jnp.sum(grad_turned[:head_size, :] * att_ref[head, :, rows], axis=0, keepdims=True)
            inner_parts = [-part for part in split_three(inner)]
            grad_tiles.append(with_rows(grad_turned, head_size, inner_parts).astype(BF16))
        query_grads = []
        for block in range(block_count):
            rows = slice(block * block_rows, (block + 1) * block_rows)
            grad_query = jnp.zeros((128, block_rows), F32)
            for key_rows, mask in score_tiles(block, block_rows, ends_ref):
                scores = matmul(key_ref[key_rows, :], query_tiles[block])
                if mask is not None:
                    scores = jnp.where(mask, scores, NEG_BIG)
                probs = jnp.exp(scores)
                grad_scores = (probs * matmul(value_ref[key_rows, :], grad_tiles[block])).astype(BF16)
                grad_query = grad_query + matmul(turned_ref[:, key_rows], grad_scores)
                add_key = matmul(grad_scores, plain_ref[rows, :])
                add_value = matmul(probs.astype(BF16), grad_plain[block])
                old = slice(key_rows.start, max(key_rows.start, rows.start))
                split = old.stop - old.start
                if split:
                    grad_key_ref[old, :] += add_key[:split]
                    grad_value_ref[old, :] += add_value[:split]
                if key_rows.stop == rows.stop:
                    grad_key_ref[rows, :] = add_key[split:]
                    grad_value_ref[rows, :] = add_value[split:]
            turned = grad_query.T
            query_grads.append((turned[:, :head_size] * scale).astype(BF16))
            decay_ref[rows, head : head + 1] = turned[:, head_size : head_size + 1]
        for block in range(block_count):
            rows = slice(block * block_rows, (block + 1) * block_rows)
            key_wide = grad_key_ref[rows, :]
            block_ref[head, block] = jnp.concatenate(
                [query_grads[block], key_wide[:, :head_size].astype(BF16)], axis=1
            )
            block_ref[value_tile, block, :, value_lane : value_lane + head_size] = grad_value_ref[
                rows, :
            ].astype(BF16)
            decay_ref[rows, head : head + 1] -= key_wide[:, head_size : head_size + 1]
        give(head)
        if value_lane and value_tile != tile:
            give(value_tile)
    shape = (block_rows, block_rows)
    upper = (iota(shape, 0) <= iota(shape, 1)).astype(BF16)
    carry = None
    for block in reversed(range(block_count)):
        rows = slice(block * block_rows, (block + 1) * block_rows)
        sums = jnp.zeros((block_rows, 128), F32)
        values = jnp.where(iota((block_rows, 128), 1) < hp, decay_ref[rows, :], 0.0)
        for part in split_three(values):
            sums = sums + matmul(upper, part.astype(BF16))
        if carry is not None:
            sums = sums + carry
        carry = sums[0:1, :]
        if lane == 0:
            block_ref[tile, block] = sums.astype(BF16)
        else:
            block_ref[tile, block, :, lane : lane + head_size] = sums[:, :head_size].astype(BF16)
    give(tile)
    for copy in returns:
        copy.wait()
    for (head, k), copy in copies.items():
        if k:
            copy.wait_send()


def spec(space):
    return pl.BlockSpec(memory_space=space)


def attend(pack, place, blk, ends, sends):
    count, tiles, _, block_rows, _ = sends.shape
    hp, head_size = pack.hp, pack.head_size
    pack_rows = 2 * count * block_rows
    dma = pltpu.SemaphoreType.DMA
    return pl.pallas_call(
        functools.partial(attend_kernel, pack),
        out_shape=[
            jax.ShapeDtypeStruct((count, hp, block_rows, 128), BF16),
            jax.ShapeDtypeStruct((tiles, 2 * count, block_rows, 128), BF16),
            jax.ShapeDtypeStruct((hp, 1, pack_rows), F32),
            jax.ShapeDtypeStruct((hp, head_size, pack_rows), F32),
        ],
        in_specs=[spec(pltpu.SMEM)] * 3 + [spec(pl.ANY)],
        out_specs=[spec(pl.ANY), spec(pl.ANY), spec(pltpu.VMEM), spec(pltpu.VMEM)],
        scratch_shapes=[
            pltpu.VMEM((pack_rows, 128), BF16),
            pltpu.VMEM((128, pack_rows), BF16),
            pltpu.VMEM((hp, 2 * count, block_rows, 128), BF16),
            pltpu.VMEM((count, hp, block_rows, 128), BF16),
            dma((tiles, count)),
            dma((tiles, count)),
            dma((count, hp)),
            dma((count, hp)),
            dma((tiles,)),
        ]
        + [pltpu.VMEM((2 * count, block_rows, 128), BF16)] * tiles,
        compiler_params=pltpu.CompilerParams(
            vmem_limit_bytes=40 << 20, collective_id=0, has_side_effects=True
        ),
        name="attend",
    )(place, blk, ends, sends)


def attend_back(pack, place, blk, ends, kept, lse, att, sends):
    count, hp, block_rows, _ = sends.shape
    tiles = kept.shape[0]
    head_size = pack.head_size
    pack_rows = 2 * count * block_rows
    dma = pltpu.SemaphoreType.DMA
    return pl.pallas_call(
        functools.partial(attend_back_kernel, pack),
        out_shape=jax.ShapeDtypeStruct((count, tiles, 2, block_rows, 128), BF16),
        in_specs=[spec(pltpu.SMEM)] * 3 + [spec(pltpu.VMEM)] * 3 + [spec(pl.ANY)],
        out_specs=spec(pl.ANY),
        scratch_shapes=[
            pltpu.VMEM((pack_rows, 128), BF16),
            pltpu.VMEM((pack_rows, 128), BF16),
            pltpu.VMEM((128, pack_rows), BF16),
            pltpu.VMEM((pack_rows, 128), BF16),
            pltpu.VMEM((pack_rows, 128), F32),
            pltpu.VMEM((pack_rows, head_size), F32),
            pltpu.VMEM((pack_rows, 128), F32),
            pltpu.VMEM((tiles, 2 * count, block_rows, 128), BF16),
            pltpu.VMEM((tiles, count, 2, block_rows, 128), BF16),
            dma((hp, count)),
            dma((hp, count)),
            dma((tiles, count)),
            dma((tiles, count)),
        ]
        + [pltpu.VMEM((count, block_rows, 128), BF16)] * hp,
        compiler_params=pltpu.CompilerParams(
            vmem_limit_bytes=40 << 20, collective_id=1, has_side_effects=True
        ),
        name="attend_back",
    )(place, blk, ends, kept, lse, att, sends)


VMEM_BYTES = 60 << 20


def turned_matmul(left, right):
    return lax.dot_general(left, right, (((1,), (1,)), ((), ())), preferred_element_type=F32)


def column_sums(values):
    return jnp.sum(values, axis=0, keepdims=True)


def unit_factor(values):
    return lax.rsqrt(jnp.mean(values * values, axis=-1, keepdims=True) + EPSILON)


def norm_rows_back(grad_normed, values, gain):
    factor = unit_factor(values)
    unit = values * factor
    grad_unit = grad_normed * gain
    inner = jnp.mean(grad_unit * unit, axis=-1, keepdims=True)
    return factor * (grad_unit - unit * inner), column_sums(grad_normed * unit)


class Refs:
    def __init__(self, names, refs):
        for name, ref in zip(names, refs, strict=True):
            setattr(self, name, ref)

    def pieces(self, name):
        out = []
        while hasattr(self, f"{name}_{len(out)}"):
            out.append(getattr(self, f"{name}_{len(out)}"))
        return out


def named_call(kernel, name, inputs, outputs, scratch, collective_id):
    names = list(inputs) + list(outputs) + list(scratch)

    def body(*refs):
        kernel(Refs(names, refs))

    params = dict(vmem_limit_bytes=VMEM_BYTES)
    if collective_id is not None:
        params.update(collective_id=collective_id, has_side_effects=True)
    out = pl.pallas_call(
        body,
        out_shape=[jax.ShapeDtypeStruct(shape, kind) for shape, kind, _ in outputs.values()],
        in_specs=[spec(space) for _, space in inputs.values()],
        out_specs=[spec(space) for _, _, space in outputs.values()],
        scratch_shapes=list(scratch.values()),
        compiler_params=pltpu.CompilerParams(**params),
        name=name,
    )(*[array for array, _ in inputs.values()])
    return dict(zip(outputs, out))


class Copies:
    def __init__(self, sems):
        self.sems, self.used, self.saves = sems, 0, []

    def load(self, source, target):
        copy = pltpu.make_async_copy(source, target, self.sems.at[self.used])
        self.used += 1
        copy.start()
        return copy

    def load_down(self, pieces, target, columns=None):
        rows = pieces[0].shape[0]
        out = []
        for index, item in enumerate(pieces):
            place = target.at[pl.ds(index * rows, rows)]
            if columns is not None:
                place = target.at[pl.ds(index * rows, rows), pl.ds(0, columns)]
            out.append(self.load(item, place))
        return out

    def load_beside(self, pieces, target):
        columns = pieces[0].shape[1]
        return [
            self.load(item, target.at[:, pl.ds(index * columns, columns)])
            for index, item in enumerate(pieces)
        ]

    def save(self, source, target):
        self.saves.append(self.load(source, target))

    def finish(self):
        for copy in self.saves:
            copy.wait()


class PairSums:
    def __init__(self, steps, send_refs, recv_refs, send_sem, recv_sem):
        self.steps, self.send_refs, self.recv_refs = steps, send_refs, recv_refs
        self.send_sem, self.recv_sem = send_sem, recv_sem
        self.t = lax.axis_index("tp")
        self.started = []

    def greet(self):
        barrier = pltpu.get_barrier_semaphore()
        for step in self.steps:
            pl.semaphore_signal(
                barrier, inc=1, device_id={"tp": peer(self.t, step)}, device_id_type=pl.DeviceIdType.MESH
            )
        pl.semaphore_wait(barrier, len(self.steps))

    def copy(self, index):
        copy = pltpu.make_async_remote_copy(
            src_ref=self.send_refs[index],
            dst_ref=self.recv_refs[index],
            send_sem=self.send_sem.at[index],
            recv_sem=self.recv_sem.at[index],
            device_id={"tp": peer(self.t, self.steps[index % len(self.steps)])},
            device_id_type=pl.DeviceIdType.MESH,
        )
        copy.start()
        self.started.append(copy)
        return copy

    def start(self, place):
        self.first = getattr(self, "first", {})
        self.first[place] = self.copy(place * len(self.steps))

    def finish(self, place):
        copy = self.first[place]
        base = place * len(self.steps)
        for offset in range(len(self.steps)):
            if offset:
                self.send_refs[base + offset][...] = total.astype(BF16)
                copy = self.copy(base + offset)
            copy.wait_recv()
            total = self.send_refs[base + offset][...].astype(F32) + self.recv_refs[base + offset][
                ...
            ].astype(F32)
        return total

    def end(self):
        for copy in self.started:
            copy.wait_send()


def pair_scratch(places, steps, rows, columns):
    count = places * len(steps)
    buffers = {f"send{index}": pltpu.VMEM((rows, columns), BF16) for index in range(count)}
    buffers.update({f"recv{index}": pltpu.VMEM((rows, columns), BF16) for index in range(count)})
    buffers["pair_send"] = pltpu.SemaphoreType.DMA((count,))
    buffers["pair_recv"] = pltpu.SemaphoreType.DMA((count,))
    return buffers


def pair_sums(r, places, steps):
    count = places * len(steps)
    return PairSums(
        steps,
        [getattr(r, f"send{index}") for index in range(count)],
        [getattr(r, f"recv{index}") for index in range(count)],
        r.pair_send,
        r.pair_recv,
    )


def over_units(units, block, body):
    def step(index, carry):
        body(pl.ds(pl.multiple_of(index * block, block), block))
        return carry

    lax.fori_loop(0, units // block, step, 0)


def tile_columns(pack, item, head):
    first = (item * pack.hp + head) * pack.head_size
    return slice(first, first + pack.head_size)


def write_tiles(pack, count, packed_ref, half, query, key, value, forget):
    size = pack.head_size
    forget_tile, forget_lane = pack.value_place(pack.hp)
    lane = iota(forget.shape, 1)
    for item in range(count):
        target = peer(lax.axis_index("ctx"), item)
        for head in range(pack.hp):
            columns = tile_columns(pack, item, head)
            packed_ref[target, head, half] = jnp.concatenate([query[:, columns], key[:, columns]], axis=1)
        shift = (forget_lane - item * pack.hp) % 128
        moved = pltpu.roll(forget, shift, 1) if shift else forget
        moved = jnp.where((lane >= forget_lane) & (lane < forget_lane + pack.hp), moved, 0.0)
        for tile in range(pack.hp, pack.tiles):
            parts = []
            for slot in range(2):
                head = 2 * (tile - pack.hp) + slot
                if head < pack.hp:
                    parts.append(value[:, tile_columns(pack, item, head)])
                else:
                    parts.append(moved[:, slot * size : (slot + 1) * size].astype(BF16))
            packed_ref[target, tile, half] = jnp.concatenate(parts, axis=1)


def project_rows(pack, r, count, width, half, rows, normed):
    def part(first, size):
        return matmul(normed, r.w_mix[:, first : first + size])

    query, key, value = [part(index * width, width).astype(BF16) for index in range(3)]
    logits = part(3 * width, 128) + r.bias[...]
    r.logits[rows, :] = logits
    forget = jnp.minimum(logits, 0.0) - jnp.log1p(jnp.exp(-jnp.abs(logits)))
    forget = forget.astype(BF16).astype(F32)
    write_tiles(pack, count, r.packed, half, query, key, value, forget)


def first_kernel(pack, count, width, r):
    copies = Copies(r.sems)
    c = lax.axis_index("ctx")
    block_rows = r.packed.shape[3]
    for copy in copies.load_down(r.pieces("w_qkv"), r.w_mix):
        copy.wait()
    for half in range(2):
        rows = slice(half * block_rows, (half + 1) * block_rows)
        residual = r.residual[rows, :]
        normed = (residual * unit_factor(residual) * r.gain[...]).astype(BF16)
        r.normed[rows, :] = normed
        add = column_sums(residual * residual)
        r.stat[...] = jnp.broadcast_to(add if half == 0 else add + r.stat[0:1, :], r.stat.shape)
        project_rows(pack, r, count, width, half, rows, normed)


def middle_kernel(pack, count, units, unit_block, steps, r):
    copies = Copies(r.sems)
    c = lax.axis_index("ctx")
    sums = pair_sums(r, 4, steps)
    block_rows = r.attended.shape[0] // 2
    load_out = copies.load_beside([item.at[pl.ds(0, r.w_o.shape[0])] for item in r.pieces("w_back")], r.w_o)
    load_base = copies.load(r.residual, r.base)
    load_units = copies.load_down([item.at[0] for item in r.pieces("w_units")], r.w_g)
    load_units += copies.load_down([item.at[1] for item in r.pieces("w_units")], r.w_mix, units)
    load_units += copies.load_beside(
        [item.at[pl.ds(r.w_o.shape[0], units)] for item in r.pieces("w_back")], r.w_d
    )
    sums.greet()
    for copy in load_out:
        copy.wait()
    halves = [slice(half * block_rows, (half + 1) * block_rows) for half in range(2)]
    size = pack.head_size
    for half, rows in enumerate(halves):
        columns = []
        for item in range(count):
            for head in range(pack.hp):
                columns.append(r.att[peer(c, item), head][:, half * size : (half + 1) * size])
        attended = jnp.concatenate(columns, axis=1)
        r.attended[rows, :] = attended
        sums.send_refs[half * len(steps)][...] = matmul(attended, r.w_o[...]).astype(BF16)
        sums.start(half)
    load_base.wait()
    for copy in load_units:
        copy.wait()
    for half, rows in enumerate(halves):
        branch = sums.finish(half)
        add = column_sums(branch * branch)
        r.stat[0:1, :] = add if half == 0 else r.stat[0:1, :] + add
        middle = r.base[rows, :] + branch
        r.base[rows, :] = middle
        copies.save(r.base.at[rows], r.middle.at[rows])
        normed = (middle * unit_factor(middle) * r.gain_two[...]).astype(BF16)
        r.normed_keep[rows, :] = normed
        copies.save(r.normed_keep.at[rows], r.normed_two.at[rows])
        r.total[...] = jnp.zeros(r.total.shape, F32)

        def block(columns, rows=rows):
            gate = matmul(r.normed_keep[rows, :], r.w_g[:, columns])
            up = matmul(r.normed_keep[rows, :], r.w_mix[:, columns])
            hidden = (gate * jax.nn.sigmoid(gate) * up).astype(BF16)
            r.gate_keep[rows, columns] = gate.astype(BF16)
            r.up_keep[rows, columns] = up.astype(BF16)
            r.hidden_keep[rows, columns] = hidden
            r.total[...] += matmul(hidden, r.w_d[columns, :])

        over_units(units, unit_block, block)
        sums.send_refs[(2 + half) * len(steps)][...] = r.total[...].astype(BF16)
        sums.start(2 + half)
        copies.save(r.gate_keep.at[rows], r.gate.at[rows])
        copies.save(r.up_keep.at[rows], r.up.at[rows])
        copies.save(r.hidden_keep.at[rows], r.hidden.at[rows])
    for half, rows in enumerate(halves):
        branch = sums.finish(2 + half)
        add = column_sums(branch * branch)
        r.stat[1:2, :] = add if half == 0 else r.stat[1:2, :] + add
        residual = r.base[rows, :] + branch
        r.after_keep[rows, :] = residual
        copies.save(r.after_keep.at[rows], r.after.at[rows])
    copies.finish()
    sums.end()


def back_kernel(pack, count, width, units, unit_block, steps, upper, feed, r):
    copies = Copies(r.sems)
    c = lax.axis_index("ctx")
    size = pack.head_size
    forget_tile, forget_lane = pack.value_place(pack.hp)
    if feed:
        sums = pair_sums(r, 4 if upper else 2, steps)
        second = 2 if upper else 0
    block_rows = r.total.shape[0]
    halves = [slice(half * block_rows, (half + 1) * block_rows) for half in range(2)]
    if upper:
        load_qkv = copies.load_down(r.pieces("w_qkv"), r.w_mix, 3 * width + 128)
    if feed:
        if upper:
            load_value = [copies.load(r.residual.at[rows], r.values.at[rows]) for rows in halves]
        load_base = copies.load(r.base_in, r.base)
        waits = [copies.load(r.gate, r.gate_keep), copies.load(r.up, r.up_keep)]
        waits += copies.load_beside(
        [item.at[pl.ds(r.w_o.shape[0], units)] for item in r.pieces("w_back")], r.w_d
    )
        waits += copies.load_down([item.at[0] for item in r.pieces("w_units")], r.w_g)
        load_out = copies.load_beside([item.at[pl.ds(0, r.w_o.shape[0])] for item in r.pieces("w_back")], r.w_o)
        sums.greet()

    if upper:
        for copy in load_qkv:
            copy.wait()
        for half, rows in enumerate(halves):
            columns = [[], [], []]
            forget = jnp.zeros((block_rows, 128), F32)
            lane = iota(forget.shape, 1)
            for item in range(count):
                source = peer(c, item)
                for head in range(pack.hp):
                    pair = r.back[source, head, half]
                    columns[0].append(pair[:, :size])
                    columns[1].append(pair[:, size:])
                    value_tile, value_lane = pack.value_place(head)
                    columns[2].append(r.back[source, value_tile, half][:, value_lane : value_lane + size])
                wide = r.back[source, forget_tile, half].astype(F32)
                shift = (item * pack.hp - forget_lane) % 128
                moved = pltpu.roll(wide, shift, 1) if shift else wide
                first = item * pack.hp
                forget = jnp.where((lane >= first) & (lane < first + pack.hp), moved, forget)
            grad_logits = (forget * jax.nn.sigmoid(-r.logits[rows, :])).astype(BF16)
            add = column_sums(grad_logits.astype(F32))
            r.bias_grad[...] = jnp.broadcast_to(
                add if half == 0 else add + r.bias_grad[0:1, :], r.bias_grad.shape
            )
            for index in range(3):
                r.grads_keep[rows, index * width : (index + 1) * width] = jnp.concatenate(
                    columns[index], axis=1
                )
            r.grads_keep[rows, 3 * width :] = grad_logits
            copies.save(r.grads_keep.at[rows], r.grads.at[rows])
            grads = r.grads_keep[rows, :]
            part = turned_matmul(grads, r.w_mix[:, : 3 * width + 128]).astype(BF16)
            if feed:
                sums.send_refs[half * len(steps)][...] = part
                sums.start(half)
            else:
                r.one_part[rows, :] = part
    if feed:
        waits += copies.load_down([item.at[1] for item in r.pieces("w_units")], r.w_mix, units)
        load_base.wait()
        load_middle = []
        for half, rows in enumerate(halves):
            grad = r.base[rows, :].astype(F32)
            if upper:
                load_value[half].wait()
                back, add = norm_rows_back(sums.finish(half), r.values[rows, :], r.gain_one[...])
                r.gain_grad[0:1, :] = add if half == 0 else r.gain_grad[0:1, :] + add
                grad = grad + back
            load_middle.append(copies.load(r.middle.at[rows], r.values.at[rows]))
            r.grad_keep[rows, :] = grad
            r.low_keep[rows, :] = grad.astype(BF16)
            copies.save(r.low_keep.at[rows], r.low.at[rows])
            for copy in waits:
                copy.wait()
            waits = []
            r.total[...] = jnp.zeros(r.total.shape, F32)

            def block(columns, rows=rows):
                grad_hidden = turned_matmul(r.low_keep[rows, :], r.w_d[columns, :])
                gate = r.gate_keep[rows, columns].astype(F32)
                up = r.up_keep[rows, columns].astype(F32)
                sigmoid = jax.nn.sigmoid(gate)
                grad_gate = (grad_hidden * up * sigmoid * (1.0 + gate * (1.0 - sigmoid))).astype(BF16)
                grad_up = (grad_hidden * gate * sigmoid).astype(BF16)
                r.gate_keep[rows, columns] = grad_gate
                r.up_keep[rows, columns] = grad_up
                r.total[...] += turned_matmul(grad_gate, r.w_g[:, columns]) + turned_matmul(
                    grad_up, r.w_mix[:, columns]
                )

            over_units(units, unit_block, block)
            sums.send_refs[(second + half) * len(steps)][...] = r.total[...].astype(BF16)
            sums.start(second + half)
            copies.save(r.gate_keep.at[rows], r.grad_gate.at[rows])
            copies.save(r.up_keep.at[rows], r.grad_up.at[rows])
        for copy in load_out:
            copy.wait()
        for half, rows in enumerate(halves):
            load_middle[half].wait()
            back, add = norm_rows_back(sums.finish(second + half), r.values[rows, :], r.gain_two[...])
            r.gain_grad[1:2, :] = add if half == 0 else r.gain_grad[1:2, :] + add
            grad = r.grad_keep[rows, :] + back
            r.grad_keep[rows, :] = grad
            copies.save(r.grad_keep.at[rows], r.grad.at[rows])
            low = grad.astype(BF16)
            r.branch[rows, :] = low
            r.turned[rows, :] = turned_matmul(low, r.w_o[...]).astype(BF16)
        for item in range(count):
            for head in range(pack.hp):
                columns = tile_columns(pack, item, head)
                r.sends[peer(c, item), head] = jnp.concatenate(
                    [r.turned[rows, columns] for rows in halves], axis=1
                )
    copies.finish()
    if feed:
        sums.end()


def tail_kernel(chunks, halved, fsdp_step, fsdp_axis, counts, *refs):
    units = counts
    own = refs[:units]
    far = refs[units : units + len(halved)]
    outs = refs[units + len(halved) : 2 * units + len(halved)]
    rest = refs[2 * units + len(halved) :]
    inward = rest[:units]
    crossed = rest[units : units + len(halved)]
    x_send, x_recv, a_send, a_recv, b_send, b_recv, c_send, c_recv = rest[units + len(halved) :]
    c = lax.axis_index("ctx")
    f = lax.axis_index(fsdp_axis)
    mesh_id = pl.DeviceIdType.MESH
    barrier = pltpu.get_barrier_semaphore()
    pl.semaphore_signal(
        barrier, inc=1, device_id={fsdp_axis: peer(f, fsdp_step)}, device_id_type=mesh_id
    )
    for k in range(1, 4):
        pl.semaphore_signal(barrier, inc=1, device_id={"ctx": peer(c, k)}, device_id_type=mesh_id)
    pl.semaphore_wait(barrier, 4)
    is_end = c * (3 - c) == 0
    is_middle = c * (3 - c) != 0

    def remote(source, target, send, recv, where):
        return pltpu.make_async_remote_copy(
            src_ref=source,
            dst_ref=target,
            send_sem=send,
            recv_sem=recv,
            device_id=where,
            device_id_type=mesh_id,
        )

    def mine(unit):
        return crossed[halved.index(unit)] if unit in halved else own[unit]

    def rows_of(index):
        unit, first, count = chunks[index]
        return unit, pl.ds(first, count)

    def x_copy(index):
        unit, rows = rows_of(index)
        place = halved.index(unit)
        return remote(
            far[place].at[rows],
            crossed[place].at[rows],
            x_send.at[index],
            x_recv.at[index],
            {fsdp_axis: peer(f, fsdp_step)},
        )

    def a_copy(index):
        unit, rows = rows_of(index)
        return remote(
            mine(unit).at[rows], inward[unit].at[rows], a_send.at[index], a_recv.at[index], {"ctx": 1 + c // 2}
        )

    def b_copy(index):
        unit, rows = rows_of(index)
        return remote(
            inward[unit].at[rows], outs[unit].at[rows], b_send.at[index], b_recv.at[index], {"ctx": 3 - c}
        )

    def c_copy(index):
        unit, rows = rows_of(index)
        return remote(
            outs[unit].at[rows], outs[unit].at[rows], c_send.at[index], c_recv.at[index], {"ctx": 3 * (c - 1)}
        )

    def add(left, right, kind):
        return (left.astype(F32) + right.astype(F32)).astype(kind)

    total = len(chunks)
    for index in range(total):
        if chunks[index][0] in halved:
            x_copy(index).start()

    def from_x(index):
        unit, rows = rows_of(index)
        if unit in halved:
            place = halved.index(unit)
            x_copy(index).wait_recv()
            crossed[place][rows, :] = add(own[unit][rows, :], crossed[place][rows, :], own[unit].dtype)

    @pl.when(is_end)
    def _():
        for index in range(total):
            from_x(index)
            a_copy(index).start()
        for index in range(total):
            a_copy(index).wait_send()

    @pl.when(is_middle)
    def _():
        lag = 2
        for index in range(total + lag):
            if index < total:
                unit, rows = rows_of(index)
                from_x(index)
                a_copy(index).wait_recv()
                inward[unit][rows, :] = add(mine(unit)[rows, :], inward[unit][rows, :], own[unit].dtype)
                b_copy(index).start()
            if index >= lag:
                late = index - lag
                unit, rows = rows_of(late)
                b_copy(late).wait_recv()
                outs[unit][rows, :] = add(inward[unit][rows, :], outs[unit][rows, :], outs[unit].dtype)
                c_copy(late).start()
        for index in range(total):
            b_copy(index).wait_send()
            c_copy(index).wait_send()

    @pl.when(is_end)
    def _():
        for index in range(total):
            c_copy(index).wait_recv()

    for index in range(total):
        if chunks[index][0] in halved:
            x_copy(index).wait_send()


def tail(arrays, far, fsdp_step, chunk_bytes=200 << 10):
    halved = tuple(sorted(far))
    chunks = []
    for unit, item in enumerate(arrays):
        rows, row_bytes = item.shape[0], item.shape[1] * item.dtype.itemsize
        pieces = 1
        while rows % (2 * pieces) == 0 and (rows // (2 * pieces)) % 16 == 0 and (
            rows // pieces * row_bytes > chunk_bytes
        ):
            pieces *= 2
        chunks += [(unit, step * (rows // pieces), rows // pieces) for step in range(pieces)]
    dma = pltpu.SemaphoreType.DMA
    buffers = [pltpu.VMEM(item.shape, item.dtype) for item in arrays]
    return pl.pallas_call(
        functools.partial(tail_kernel, tuple(chunks), halved, fsdp_step, "fsdp", len(arrays)),
        out_shape=[jax.ShapeDtypeStruct(item.shape, item.dtype) for item in arrays],
        in_specs=[spec(pltpu.VMEM)] * (len(arrays) + len(halved)),
        out_specs=[spec(pltpu.VMEM)] * len(arrays),
        scratch_shapes=buffers
        + [buffers[unit] for unit in halved]
        + [dma((len(chunks),))] * 8,
        compiler_params=pltpu.CompilerParams(
            vmem_limit_bytes=56 << 20, collective_id=2, has_side_effects=True
        ),
        name="tail",
    )(*arrays, *[far[unit] for unit in halved])


def small_sum_kernel(steps, fsdp_axis, value_ref, out_ref, held_ref, *refs):
    fsdp_refs, ctx_refs = refs[: len(steps)], refs[len(steps) : len(steps) + 3]
    send_sem, recv_sem = refs[len(steps) + 3 :]
    c = lax.axis_index("ctx")
    f = lax.axis_index(fsdp_axis)
    mesh_id = pl.DeviceIdType.MESH
    barrier = pltpu.get_barrier_semaphore()
    for step in steps:
        pl.semaphore_signal(barrier, inc=1, device_id={fsdp_axis: peer(f, step)}, device_id_type=mesh_id)
    for k in range(1, 4):
        pl.semaphore_signal(barrier, inc=1, device_id={"ctx": peer(c, k)}, device_id_type=mesh_id)
    pl.semaphore_wait(barrier, len(steps) + 3)
    total = value_ref[...]
    for index, step in enumerate(steps):
        held_ref[index] = total
        copy = pltpu.make_async_remote_copy(
            src_ref=held_ref.at[index],
            dst_ref=fsdp_refs[index],
            send_sem=send_sem.at[index],
            recv_sem=recv_sem.at[index],
            device_id={fsdp_axis: peer(f, step)},
            device_id_type=mesh_id,
        )
        copy.start()
        copy.wait()
        total = total + fsdp_refs[index][...]
    held_ref[len(steps)] = total
    copies = []
    for k in range(1, 4):
        copy = pltpu.make_async_remote_copy(
            src_ref=held_ref.at[len(steps)],
            dst_ref=ctx_refs[k - 1],
            send_sem=send_sem.at[len(steps) + k - 1],
            recv_sem=recv_sem.at[len(steps) + k - 1],
            device_id={"ctx": peer(c, k)},
            device_id_type=mesh_id,
        )
        copy.start()
        copies.append(copy)
    for copy in copies:
        copy.wait()
    near = total + ctx_refs[0][...]
    out_ref[...] = near + (ctx_refs[1][...] + ctx_refs[2][...])


def small_sum(values, steps):
    dma = pltpu.SemaphoreType.DMA
    return pl.pallas_call(
        functools.partial(small_sum_kernel, tuple(steps), "fsdp"),
        out_shape=jax.ShapeDtypeStruct(values.shape, values.dtype),
        in_specs=[spec(pltpu.VMEM)],
        out_specs=spec(pltpu.VMEM),
        scratch_shapes=[pltpu.VMEM((len(steps) + 1,) + values.shape, values.dtype)]
        + [pltpu.VMEM(values.shape, values.dtype)] * (len(steps) + 3)
        + [dma((len(steps) + 3,))] * 2,
        compiler_params=pltpu.CompilerParams(collective_id=3, has_side_effects=True),
        name="small_sum",
    )(values)


def norm_back(grad_normed, values, factor, gain_row):
    unit_rows = values * factor
    grad_gain = jnp.sum(grad_normed * unit_rows, axis=0)
    grad_unit = grad_normed * gain_row.astype(F32)
    inner_mean = jnp.mean(grad_unit * unit_rows, axis=-1, keepdims=True)
    return (factor * (grad_unit - unit_rows * inner_mean), grad_gain)


def swap(values, axis, size, step):
    return lax.ppermute(values, axis, [(i, i ^ step) for i in range(size)])


def halving(size):
    steps = []
    while size > 1:
        size //= 2
        steps.append(size)
    return steps


def shards(
    sizes,
    tokens,
    cotangent,
    seq_lengths,
    deal,
    norm_gains,
    query_key_value,
    forget_weight,
    forget_bias,
    out_weight,
    gate_up_weight,
    down_weight,
):
    fsdp, ctx, tp = sizes
    layer_count = query_key_value.shape[0]
    row_count, model_width = tokens.shape
    heads_here = forget_weight.shape[2]
    head_size = query_key_value.shape[3] // heads_here
    block_rows = row_count // 2
    piece = model_width // fsdp
    half_width = model_width // 2
    hp = -(-heads_here // ctx)
    heads_padded = hp * ctx
    width = heads_padded * head_size
    more_columns = (heads_padded - heads_here) * head_size
    qkv_columns = 3 * width + 128
    units = gate_up_weight.shape[3]
    unit_block = min(512, units)
    pack = Pack(hp, head_size)
    tiles = pack.tiles
    everything = (row_count, model_width)
    f_index = lax.axis_index("fsdp")
    c_index = lax.axis_index("ctx")
    t_index = lax.axis_index("tp")
    fsdp_steps = halving(fsdp)
    tp_steps = list(reversed(halving(tp)))
    offsets = [0]
    for step in fsdp_steps:
        offsets = offsets + [item ^ step for item in offsets]
    vmem, any_space = pltpu.VMEM, pltpu.HBM

    def add_low(left, right):
        return (left.astype(F32) + right.astype(F32)).astype(BF16)

    grads = {}
    tasks = {}
    pending = {}

    def gather_pieces(values):
        pieces = [values]
        for step in fsdp_steps[:-1]:
            for item in list(pieces):
                pieces.append((yield swap(item, "fsdp", fsdp, step)))
        return pieces

    def reduce_grad(near, far, axis, until):
        for step in reversed(fsdp_steps):
            near = add_low(near, (yield swap(far, "fsdp", fsdp, step)))
            if step != fsdp_steps[0]:
                size = near.shape[axis] // 2
                near, far = (
                    lax.slice_in_dim(near, 0, size, axis=axis),
                    lax.slice_in_dim(near, size, 2 * size, axis=axis),
                )
                if until == "core" and size == piece:
                    return near, far
        return near

    def begin(name, *args):
        tasks[name] = reduce_grad(*args)
        pending[name] = next(tasks[name])

    own_first = {}

    def begin_gather(name, values):
        tasks[name] = gather_pieces(values)
        own_first[name] = swap(values, "fsdp", fsdp, fsdp_steps[-1])
        pending[name] = next(tasks[name])

    def tick(values, names):
        names = [name for name in names if name in tasks]
        if not names:
            return values
        values, got = lax.optimization_barrier((values, [pending.pop(name) for name in names]))
        for name, item in zip(names, got):
            try:
                pending[name] = tasks[name].send(item)
            except StopIteration as end:
                grads[name] = end.value
                del tasks[name]
        return values

    def finished(name):
        while name in tasks:
            tick((), [name])
        return grads[name]

    def weight_pieces(name):
        pieces = finished(name)
        last = [own_first[name]] + [swap(item, "fsdp", fsdp, fsdp_steps[-1]) for item in pieces[1:]]
        return pieces + last

    def exchange(sends):
        return [sends[0]] + [swap(sends[k], "ctx", ctx, k) for k in range(1, ctx)]

    def to_local(values):
        return jnp.concatenate(
            [
                lax.dynamic_slice_in_dim(values, (f_index ^ item) * piece, piece, axis=1)
                for item in offsets
            ],
            axis=1,
        )

    def from_local(values):
        places = jnp.asarray([offsets.index(item) for item in range(fsdp)], jnp.int32)
        return jnp.concatenate(
            [
                lax.dynamic_slice_in_dim(values, places[f_index ^ item] * piece, piece, axis=1)
                for item in range(fsdp)
            ],
            axis=1,
        )

    def pick(items, index):
        out = items[0]
        for entry in range(1, len(items)):
            out = jnp.where(index == entry, items[entry], out)
        return out

    deal_order = deal[0]
    inverse = (
        jnp.zeros((2 * ctx,), jnp.int32).at[deal_order].set(jnp.arange(2 * ctx, dtype=jnp.int32))
    )
    seq_ends = jnp.cumsum(seq_lengths[0]).astype(jnp.int32)
    peers = jnp.bitwise_xor(jnp.arange(ctx, dtype=jnp.int32), c_index)
    blk = jnp.take(deal_order.reshape(ctx, 2), peers, axis=0).reshape(2 * ctx)
    place = 2 * jnp.bitwise_xor(inverse // 2, c_index) + inverse % 2

    def own_qkv(layer):
        parts = [jnp.pad(query_key_value[layer, j], ((0, 0), (0, more_columns))) for j in range(3)]
        last = jnp.concatenate(
            [
                jnp.pad(forget_weight[layer], ((0, 0), (0, heads_padded - heads_here))),
                norm_gains[layer].T,
                jnp.zeros((piece, 128 - heads_padded - 2), BF16),
            ],
            axis=1,
        )
        return with_layout_constraint(jnp.concatenate(parts + [last], axis=1), Layout((0, 1)))

    def gathered_gains(pieces):
        rows = jnp.concatenate(
            [item[:, 3 * width + heads_padded : 3 * width + heads_padded + 2] for item in pieces]
        )
        return [item[None] for item in rows.T.astype(F32)]

    share = model_width // tp

    def own_columns(values):
        values = lax.dynamic_slice_in_dim(values, t_index * share, share, axis=1).astype(BF16)
        return values.reshape(2, block_rows, share)

    def column_pieces(values):
        step = 1
        pieces = [values]
        while step < tp:
            pieces = pieces + [swap(item, "tp", tp, step) for item in pieces]
            step *= 2
        return pieces

    def all_columns(pieces):
        order = [0]
        step = 1
        while step < tp:
            order = order + [item ^ step for item in order]
            step *= 2
        stacked = jnp.concatenate(pieces, axis=1)
        places = jnp.asarray([order.index(item) for item in range(tp)], jnp.int32)
        return jnp.concatenate(
            [
                lax.dynamic_slice_in_dim(stacked, places[t_index ^ item] * share, share, axis=1)
                for item in range(tp)
            ],
            axis=1,
        )

    shard = own_qkv(0)
    begin_gather(("w_qkv", 0), shard)
    cot_blocks = own_columns(cotangent)
    late_side = (c_index >= ctx // 2).astype(jnp.int32)
    cot_sends = []
    for k in range(ctx):
        wanted = deal_order[2 * (c_index ^ k) + late_side]
        cot_sends.append(lax.dynamic_index_in_dim(cot_blocks, wanted % 2, 0, keepdims=False))
    cot_got = exchange(cot_sends)

    bias_all = jnp.pad(forget_bias.astype(F32), ((0, 0), (0, 128 - heads_here)))[:, None, :]
    own_weights = [
        {
            "w_units": gate_up_weight[layer],
            "w_back": jnp.concatenate(
                [jnp.pad(out_weight[layer], ((0, more_columns), (0, 0))), down_weight[layer]], axis=0
            ),
        }
        for layer in range(layer_count)
    ]
    for layer in range(1, layer_count):
        own_weights[layer]["w_qkv"] = own_qkv(layer)

    residual = to_local(tokens)
    own_weights, residual, cot_got = tick((own_weights, residual, cot_got), [("w_qkv", 0)])
    for name in ("w_back", "w_units"):
        begin_gather((name, 0), own_weights[0][name])
    cot_mine = jnp.concatenate(
        [pick(cot_got, (deal_order[2 * c_index + half] // 2) ^ c_index) for half in range(2)], axis=0
    )
    weights = [{"w_qkv": weight_pieces(("w_qkv", 0))}]
    gains = gathered_gains(weights[0]["w_qkv"])

    def piece_inputs(layer, *names):
        return {
            f"{name}_{index}": (item, any_space)
            for name in names
            for index, item in enumerate(weights[layer][name])
        }

    def packed_out():
        return ((ctx, tiles, 2, block_rows, 128), BF16, vmem)

    dma = pltpu.SemaphoreType.DMA
    mix = pltpu.VMEM((model_width, max(units, qkv_columns)), BF16)

    def project(layer, residual):
        out = named_call(
            functools.partial(first_kernel, pack, ctx, width),
            "project",
            {
                "residual": (residual, vmem),
                "gain": (gains[2 * layer], vmem),
                "bias": (bias_all[layer], vmem),
                **piece_inputs(layer, "w_qkv"),
            },
            {
                "normed": (everything, BF16, vmem),
                "packed": packed_out(),
                "logits": ((row_count, 128), F32, vmem),
                "stat": ((8, model_width), F32, vmem),
            },
            {"w_mix": pltpu.VMEM((model_width, qkv_columns), BF16), "sems": dma((fsdp,))},
            None,
        )
        stat_terms[layer][0] = jnp.sum(out["stat"][0])
        return out["normed"], out["packed"], out["logits"]

    stat_terms = [[None] * 3 for _ in range(layer_count)]
    normed_one, packed, logits = project(0, residual)
    kept = []
    for layer in range(layer_count):
        later = layer + 1
        last = later == layer_count
        rest = [(name, layer) for name in ("w_back", "w_units")]
        if layer == 0:
            packed, cot_mine = lax.optimization_barrier((packed, cot_mine))
        if last:
            cot_pieces = column_pieces(cot_mine)
        att, received, lse, att_turned = attend(pack, place, blk, seq_ends, packed)
        if last:
            att, cot_pieces = lax.optimization_barrier((att, cot_pieces))
            att = tick(att, rest)
        else:
            att, own_weights[later] = tick((att, own_weights[later]), rest)
            begin_gather(("w_qkv", later), own_weights[later]["w_qkv"])
            begin_gather(("w_back", later), own_weights[later]["w_back"])
        for item in rest:
            weights[layer][item[0]] = weight_pieces(item)
        inputs = {
            "att": (att, vmem),
            "residual": (residual, any_space),
            "gain_two": (gains[2 * layer + 1], vmem),
            **piece_inputs(layer, "w_back", "w_units"),
        }
        outputs = {
            "attended": ((row_count, width), BF16, vmem),
            "middle": (everything, F32, any_space),
            "normed_two": (everything, BF16, any_space),
            "gate": ((row_count, units), BF16, any_space),
            "up": ((row_count, units), BF16, any_space),
            "hidden": ((row_count, units), BF16, any_space),
            "after": (everything, F32, any_space),
            "stat": ((8, model_width), F32, vmem),
        }
        out = named_call(
            functools.partial(middle_kernel, pack, ctx, units, unit_block, tp_steps),
            "middle",
            inputs,
            outputs,
            {
                "w_o": pltpu.VMEM((width, model_width), BF16),
                "w_g": pltpu.VMEM((model_width, units), BF16),
                "w_mix": pltpu.VMEM((model_width, units), BF16),
                "w_d": pltpu.VMEM((units, model_width), BF16),
                "base": pltpu.VMEM(everything, F32),
                "after_keep": pltpu.VMEM(everything, F32),
                "normed_keep": pltpu.VMEM(everything, BF16),
                "gate_keep": pltpu.VMEM((row_count, units), BF16),
                "up_keep": pltpu.VMEM((row_count, units), BF16),
                "hidden_keep": pltpu.VMEM((row_count, units), BF16),
                "total": pltpu.VMEM((block_rows, model_width), F32),
                "sems": dma((5 * fsdp + 16,)),
                **pair_scratch(4, tp_steps, block_rows, model_width),
            },
            4,
        )
        kept.append(
            dict(
                residual=residual,
                normed_one=normed_one,
                logits=logits,
                received=received,
                lse=lse,
                att_turned=att_turned,
                **{
                    name: out[name] for name in ("attended", "middle", "normed_two", "gate", "up", "hidden")
                },
            )
        )
        stat_terms[layer][1] = jnp.sum(out["stat"][0])
        stat_terms[layer][2] = jnp.sum(out["stat"][1])
        residual = out["after"]
        if not last:
            residual, own_weights[later] = tick((residual, own_weights[later]), [("w_qkv", later)])
            begin_gather(("w_units", later), own_weights[later]["w_units"])
            weights.append({"w_qkv": weight_pieces(("w_qkv", later))})
            gains += gathered_gains(weights[later]["w_qkv"])
            normed_one, packed, logits = project(later, residual)

    final_blocks = own_columns(residual)
    out_got = exchange(
        [
            lax.dynamic_index_in_dim(
                final_blocks, ((c_index ^ k) >= ctx // 2).astype(jnp.int32), 0, keepdims=False
            )
            for k in range(ctx)
        ]
    )

    def halves(values):
        return values[:, :half_width], values[:, half_width:]

    def weight_grad(left, right):
        return lax.dot_general(left, right, (((0,), (0,)), ((), ())), preferred_element_type=F32).astype(BF16)

    gain_grads = [None] * (2 * layer_count)
    bias_grads = [None] * layer_count

    def back_call(layer, upper, grad_base, back_got):
        inputs, outputs, scratch = {}, {}, {"w_mix": mix, "sems": dma((5 * fsdp + 20,))}
        scratch["total"] = pltpu.VMEM((block_rows, model_width), F32)
        if upper is not None:
            inputs.update(
                back=(back_got, vmem), logits=(kept[upper]["logits"], vmem), **piece_inputs(upper, "w_qkv")
            )
            outputs.update(
                grads=((row_count, qkv_columns), BF16, any_space), bias_grad=((8, 128), F32, vmem)
            )
            scratch.update(grads_keep=pltpu.VMEM((row_count, qkv_columns), BF16))
            if layer is None:
                outputs.update(one_part=(everything, BF16, vmem))
            else:
                inputs.update(
                    residual=(kept[upper]["residual"], any_space), gain_one=(gains[2 * upper], vmem)
                )
        if layer is not None:
            state = kept[layer]
            inputs.update(
                base_in=(grad_base, any_space),
                middle=(state["middle"], any_space),
                gate=(state["gate"], any_space),
                up=(state["up"], any_space),
                gain_two=(gains[2 * layer + 1], vmem),
                **piece_inputs(layer, "w_back", "w_units"),
            )
            outputs.update(
                low=(everything, BF16, any_space),
                grad_gate=((row_count, units), BF16, any_space),
                grad_up=((row_count, units), BF16, any_space),
                grad=(everything, F32, any_space),
                branch=(everything, BF16, vmem),
                sends=((ctx, hp, block_rows, 128), BF16, vmem),
                gain_grad=((8, model_width), F32, vmem),
            )
            scratch.update(
                base=pltpu.VMEM(everything, grad_base.dtype),
                values=pltpu.VMEM(everything, F32),
                grad_keep=pltpu.VMEM(everything, F32),
                low_keep=pltpu.VMEM(everything, BF16),
                gate_keep=pltpu.VMEM((row_count, units), BF16),
                up_keep=pltpu.VMEM((row_count, units), BF16),
                turned=pltpu.VMEM((row_count, width), BF16),
                w_o=pltpu.VMEM((width, model_width), BF16),
                w_g=pltpu.VMEM((model_width, units), BF16),
                w_d=pltpu.VMEM((units, model_width), BF16),
                **pair_scratch(2 if upper is None else 4, tp_steps, block_rows, model_width),
            )
        return named_call(
            functools.partial(
                back_kernel,
                pack,
                ctx,
                width,
                units,
                unit_block,
                tp_steps,
                upper is not None,
                layer is not None,
            ),
            "back_top" if upper is None else "back_end" if layer is None else "back",
            inputs,
            outputs,
            scratch,
            None if layer is None else 6 if upper is None else 7,
        )

    def begin_qkv(layer, out):
        bias_grads[layer] = out["bias_grad"][0, :heads_here]
        begin(
            ("qkv", layer),
            *[weight_grad(part, out["grads"]) for part in halves(kept[layer]["normed_one"])],
            0,
            "core",
        )

    ffn = ("down", "gate", "up", "out")
    grad_base = to_local(all_columns(cot_pieces))
    back_got, upper = None, None
    for layer in reversed(range(layer_count)):
        state = kept[layer]
        out = back_call(layer, upper, grad_base, back_got)
        if upper is None:
            out, out_got = lax.optimization_barrier((out, out_got))
        else:
            out, (grads["down", upper],) = lax.optimization_barrier((out, background_down))
            background_gate = lax.psum([grads["gate", upper]], "ctx")
        if upper is not None:
            gain_grads[2 * upper] = out["gain_grad"][0]
            begin_qkv(upper, out)
        gain_grads[2 * layer + 1] = out["gain_grad"][1]
        grad_base = out["grad"]
        lefts = [state["hidden"], state["normed_two"], state["normed_two"], state["attended"]]
        rights = [out["low"], out["grad_gate"], out["grad_up"], out["branch"]]
        for name, left, right in zip(ffn, lefts, rights):
            if name in ("down", "out"):
                pairs = [weight_grad(left, part) for part in halves(right)]
            else:
                pairs = [weight_grad(part, right) for part in halves(left)]
            reach = "fsdp" if name in ("down", "gate") else "core"
            begin((name, layer), *pairs, 1 if name in ("down", "out") else 0, reach)
        sends = tick(out["sends"], [(name, layer) for name in ffn] + [("qkv", layer + 1)])
        if upper is None:
            mixed = jnp.concatenate(
                [pick(out_got, (inverse[2 * c_index + half] // 2) ^ c_index) for half in range(2)], axis=0
            )
            mixed_pieces = column_pieces(mixed)
        else:
            sends, (grads["gate", upper],) = lax.optimization_barrier((sends, background_gate))
        back_got = attend_back(
            pack, place, blk, seq_ends, state["received"], state["lse"], state["att_turned"], sends
        )
        back_got = tick(back_got, [(name, layer) for name in ffn] + [("qkv", layer + 1)])
        if upper is None:
            back_got, mixed_pieces = lax.optimization_barrier((back_got, mixed_pieces))
            mixed_out = from_local(all_columns(mixed_pieces)).astype(F32)
        if layer:
            background_down = lax.psum([grads["down", layer]], "ctx")
        upper = layer
    out = back_call(None, 0, None, back_got)
    begin_qkv(0, out)
    one_pairs = []
    for half in range(2):
        part = out["one_part"][half * block_rows : (half + 1) * block_rows]
        for step in tp_steps[:-1]:
            part = add_low(part, swap(part, "tp", tp, step))
        one_pairs.append((part, swap(part, "tp", tp, tp_steps[-1])))
    names = [(name, 0) for name in ("down", "gate")]
    arrays = [grads[name] for name in names]
    far_units = {}
    for name in [("up", 0), ("out", 0)] + [
        (name, layer) for layer in range(1, layer_count) for name in ("up", "out", "qkv")
    ] + [("qkv", 0)]:
        near, far = finished(name)
        far_units[len(arrays)] = far
        arrays.append(near)
        names.append(name)
    reduced = tail(arrays, far_units, fsdp_steps[0])
    one_pairs, reduced = lax.optimization_barrier((one_pairs, reduced))
    for name, item in zip(names, reduced):
        grads[name] = item
    grad_normed_one = jnp.concatenate(
        [left.astype(F32) + right.astype(F32) for left, right in one_pairs], axis=0
    )
    first = kept[0]["residual"]
    grad_from_one, gain_grads[0] = norm_back(grad_normed_one, first, unit_factor(first), gains[0])
    grad_tokens = from_local(grad_base + grad_from_one)

    small = jnp.concatenate(
        [from_local(jnp.stack(gain_grads)).reshape(-1), jnp.stack([item for row in stat_terms for item in row])]
        + bias_grads
    )
    used = small.shape[0]
    small = jnp.pad(small, (0, -used % 2048)).reshape(-1, 128)
    small = small_sum(small, list(reversed(fsdp_steps))).reshape(-1)
    gain_size = 2 * layer_count * model_width
    grad_gains = lax.dynamic_slice_in_dim(
        small[:gain_size].reshape(layer_count, 2, model_width), f_index * piece, piece, axis=2
    )
    stat_sums = small[gain_size : gain_size + 3 * layer_count].reshape(layer_count, 3)
    bias_sums = small[gain_size + 3 * layer_count : used].reshape(layer_count, heads_here)
    rms_values = jnp.sqrt(stat_sums / (row_count * model_width * fsdp * ctx))

    def both(pick_one):
        return jnp.stack([pick_one(layer).astype(F32) for layer in range(layer_count)])

    kept_columns = heads_here * head_size
    return (
        mixed_out,
        grad_tokens,
        grad_gains,
        both(
            lambda layer: jnp.stack(
                [grads["qkv", layer][:, j * width : j * width + kept_columns] for j in range(3)]
            )
        ),
        both(lambda layer: grads["qkv", layer][:, 3 * width : 3 * width + heads_here]),
        bias_sums,
        both(lambda layer: grads["out", layer][:kept_columns]),
        both(lambda layer: jnp.stack([grads["gate", layer], grads["up", layer]])),
        both(lambda layer: grads["down", layer]),
        rms_values,
    )


def solution(mesh):
    in_specs = (
        P(("fsdp", "ctx"), None),
        P(("fsdp", "ctx"), None),
        P("fsdp", None),
        P("fsdp", None),
        P(None, None, "fsdp"),
        P(None, None, "fsdp", "tp"),
        P(None, "fsdp", "tp"),
        P(None, "tp"),
        P(None, "tp", "fsdp"),
        P(None, None, "fsdp", "tp"),
        P(None, "tp", "fsdp"),
    )
    out_specs = (
        P(("fsdp", "ctx"), None),
        P(("fsdp", "ctx"), None),
        P(None, None, "fsdp"),
        P(None, None, "fsdp", "tp"),
        P(None, "fsdp", "tp"),
        P(None, "tp"),
        P(None, "tp", "fsdp"),
        P(None, None, "fsdp", "tp"),
        P(None, "tp", "fsdp"),
        P(),
    )
    sizes = (mesh.shape["fsdp"], mesh.shape["ctx"], mesh.shape["tp"])
    return jax.shard_map(
        functools.partial(shards, sizes),
        mesh=mesh,
        in_specs=in_specs,
        out_specs=out_specs,
        check_vma=False,
    )
```

time: 1930 us -> 1310 us (0.68)
  waiting for transfers between devices: 986 us -> 71.6 us
  Pallas kernels: 78.3 us -> 921 us
  starting transfers between devices: 226 us -> 29.7 us
  matrix products: 200 us -> 48.8 us
  other arithmetic: 222 us -> 73.9 us
  local copies, waits for them, and re-layouts: 187 us -> 119 us
    pallas_call x4 -> x13, Pallas kernels: 78.3 us -> 921 us  [the longest x7 320 us: named_call(): pl.pallas_call(body, out_shape=[jax.ShapeDtypeStruct(shape, kind) for sha...]
    ppermute x74 -> x42, waiting for transfers between devices: 599 us -> 54.6 us  [swap(): return lax.ppermute(values, axis, [(i, i ^ step) for i in range(size)])]
    ppermute x27 -> x0, waiting for transfers between devices: 387 us -> none  [the longest x9 211 us: sum_ctx(): outward = lax.ppermute(total, 'ctx', [(1, 0), (2, 3)])]
    dot_general x32 -> x20, matrix products: 200 us -> 48.8 us  [weight_grad(): lax.dot_general(left, right, (((0,), (0,)), ((), ())), preferred_element_...]
    ppermute x74 -> x42, starting transfers between devices: 148 us -> 29.7 us  [swap(): return lax.ppermute(values, axis, [(i, i ^ step) for i in range(size)])]
    ppermute x27 -> x0, starting transfers between devices: 77.9 us -> none  [the longest x9 51.3 us: sum_ctx(): lax.ppermute(values, 'ctx', [(0, 1), (3, 2)])]
    add x21 -> x4, other arithmetic: 53 us -> 3.99 us  [the longest x1 3.55 us: shards(): grad_tokens = from_local(grad_base + grad_from_one)]
    concatenate x14 -> x5, other arithmetic: 42.4 us -> 7.97 us  [the longest x2 3.37 us: to_local(): jnp.concatenate([lax.dynamic_slice_in_dim(values, (f_index ^ item) * piec...]
  transfers between devices with their start and end apart: 101 -> 43, of which waited for: 37 -> 11; matrix products, arithmetic and copies ran while one was open for 26% -> 11% of each run, Pallas kernels for 3% -> 63%
where the time goes in v2:
time: 1310 us; the launch traced here: 1300 us
  Pallas kernels  921 us (70%)
  local copies, waits for them, and re-layouts  119 us (9%)
  other arithmetic  73.9 us (6%)
  waiting for transfers between devices  71.6 us (5%)
  matrix products  48.8 us (4%)
  between operations  36.5 us (3%)
  starting transfers between devices  29.7 us (2%)
    pallas_call x7, Pallas kernels, named_call(): pl.pallas_call(body, out_shape=[jax.ShapeDtypeStruct(shape, kind) for sha...  320 us
    pallas_call x1, Pallas kernels, tail(): pl.pallas_call(functools.partial(tail_kernel, tuple(chunks), halved, fsdp...  274 us
    pallas_call x2, Pallas kernels, attend(): pl.pallas_call(functools.partial(attend_kernel, pack), out_shape=[jax.Sha...  159 us
    pallas_call x2, Pallas kernels, attend_back(): pl.pallas_call(functools.partial(attend_back_kernel, pack), out_shape=jax...  155 us
    ppermute x42, waiting for transfers between devices, swap(): return lax.ppermute(values, axis, [(i, i ^ step) for i in range(size)])  54.6 us
    dot_general x20, matrix products, weight_grad(): lax.dot_general(left, right, (((0,), (0,)), ((), ())), preferred_element_...  48.8 us
    ppermute x42, starting transfers between devices, swap(): return lax.ppermute(values, axis, [(i, i ^ step) for i in range(size)])  29.7 us
    unnamed x171, local copies, waits for them, and re-layouts  28.4 us
  transfers between devices with their start and end apart: 43, of which 11 were waited for; matrix products, arithmetic and copies ran while one was open for 11% of the time, Pallas kernels for 63%

profile of v2, /device:TPU:0, one launch (start us, length us, event | category | flops | bytes accessed | tf_op | source)
XLA Modules:
  0.0 1299.8 jit_solution(4242844205829589719)
XLA Ops:
  17.8 5.0 collective-permute-start.2
  37.6 3.8 concatenate.87.refs_3_.refs_2_
  45.1 6.7 slice_bitcast_fusion
  56.7 16.7 %collective-permute-done.3.refs_4_.refs_3_ = bf16[384,2432]{1,0:T(8,128)(2,1)} collective-permute-done((bf16[384,2432]{1,0:T(8,128)(2,1)S(1)}, bf16[384,2432]{1,0:T(8,128)(2,1)}, u32[]{:S(2)}, u32[]{:S(2)}) %collective-permute-start.3) | collective-permute-done | bytes 1867808 | tf_op jit(solution)/shard_map/ppermute | solution.py:1141
  92.3 11.9 project.2
  106.0 79.3 %attend.2 = (bf16[4,3,256,128]{3,2,1,0:T(8,128)(2,1)S(1)}, bf16[5,8,256,128]{3,2,1,0:T(8,128)(2,1)S(1)}, f32[3,1,2048]{2,1,0:T(1,128)S(1)}, f32[3,64,2048]{2,1,0:T(8,128)S(1)}) custom-call(s32[8]{0:T(128)S(1)} %fusion.28.place_ref, s32[8]{0:T(128)S(1)} %select_n.299.blk_ref, s32[6]{0:T(128)S(1)} %bitcast.132, bf16[4,5,2,256,128]{4,3,2,1,0:T(8,128)(2,1)S(1)} %copy-done.6), custom_call_target="tpu_custom_call" | custom-call | tf_op jit(solution)/shard_map/attend/pallas_call | solution.py:445
  188.9 3.9 copy.68
  200.6 76.0 %middle.2 = (bf16[512,768]{1,0:T(8,128)(2,1)}, f32[512,1536]{1,0:T(8,128)}, bf16[512,1536]{1,0:T(8,128)(2,1)}, bf16[512,2048]{1,0:T(8,128)(2,1)}, bf16[512,2048]...) custom-call(bf16[4,3,256,128]{3,2,1,0:T(8,128)(2,1)} %copy-done.13, ...), custom_call_target="tpu_custom_call" | custom-call | tf_op jit(solution)/shard_map/middle/pallas_call | solution.py:552
  280.7 4.2 collective-permute-done.13
  286.1 3.9 copy.72.refs_5_.refs_4_
  290.7 3.9 copy.71.refs_4_.refs_3_
  295.5 4.1 copy.73.refs_6_.refs_5_
  300.2 11.9 project.3
  313.9 79.3 %attend.3 = (bf16[4,3,256,128]{3,2,1,0:T(8,128)(2,1)S(1)}, bf16[5,8,256,128]{3,2,1,0:T(8,128)(2,1)S(1)}, f32[3,1,2048]{2,1,0:T(1,128)S(1)}, f32[3,64,2048]{2,1,0:T(8,128)S(1)}) custom-call(s32[8]{0:T(128)S(1)} %fusion.28.place_ref, s32[8]{0:T(128)S(1)} %select_n.299.blk_ref, s32[6]{0:T(128)S(1)} %bitcast.133, bf16[4,5,2,256,128]{4,3,2,1,0:T(8,128)(2,1)S(1)} %copy-done.7), custom_call_target="tpu_custom_call" | custom-call | tf_op jit(solution)/shard_map/attend/pallas_call | solution.py:445
  400.8 5.1 collective-permute-done.18.refs_5_.refs_7_
  409.1 75.2 %middle.3 = (bf16[512,768]{1,0:T(8,128)(2,1)}, f32[512,1536]{1,0:T(8,128)}, bf16[512,1536]{1,0:T(8,128)(2,1)}, bf16[512,2048]{1,0:T(8,128)(2,1)}, bf16[512,2048]...) custom-call(bf16[4,3,256,128]{3,2,1,0:T(8,128)(2,1)} %copy-done.12, ...), custom_call_target="tpu_custom_call" | custom-call | tf_op jit(solution)/shard_map/middle/pallas_call | solution.py:552
  493.4 55.4 %back_top.1 = (bf16[512,1536]{1,0:T(8,128)(2,1)}, bf16[512,2048]{1,0:T(8,128)(2,1)}, bf16[512,2048]{1,0:T(8,128)(2,1)}, f32[512,1536]{1,0:T(8,128)}, bf16[512,15...) custom-call(bf16[512,1536]{1,0:T(8,128)(2,1)} %pad_maximum_fusion.5.refs_0_, ...), custom_call_target="tpu_custom_call" | custom-call | tf_op jit(solution)/shard_map/back_top/pallas_call | solution.py:552
  562.5 8.5 collective-permute-done.28
  600.7 77.3 %attend_back.2.refs_0_ = bf16[4,5,2,256,128]{4,3,2,1,0:T(8,128)(2,1)S(1)} custom-call(s32[8]{0:T(128)S(1)} %fusion.28.place_ref, s32[8]{0:T(128)S(1)} %select_n.299.blk_ref, s32[6]{0:T(128)S(1)} %bitcast.134, bf16[5,8,256,128]{3,2,1,0:T(8,128)(2,1)S(1)} %copy-done.5, f32[3,1,2048]{2,1,0:T(1,128)S(1)} %get-tuple-element.177.lse_ref, ...), custom_call_target="tpu_custom_call" | custom-call | tf_op jit(solution)/shard_map/attend_back/pallas_call | solution.py:480
  678.0 4.2 add_convert_fusion.10
  699.0 6.8 collective-permute-done.31
  706.7 78.6 %back.1 = (bf16[512,2432]{1,0:T(8,128)(2,1)}, f32[8,128]{1,0:T(8,128)}, bf16[512,1536]{1,0:T(8,128)(2,1)}, bf16[512,2048]{1,0:T(8,128)(2,1)}, bf16[512,2048]{1,0...) custom-call(bf16[4,5,2,256,128]{4,3,2,1,0:T(8,128)(2,1)} %copy-done., ...), custom_call_target="tpu_custom_call" | custom-call | tf_op jit(solution)/shard_map/back/pallas_call | solution.py:552
  788.2 17.0 %all-reduce.5.cloned.1.call-done = (bf16[2048,384]{1,0:T(8,128)(2,1)}, bf16[384,2048]{1,0:T(8,128)(2,1)}) async-done(((bf16[2048,384]{1,0:T(8,128)(2,1)}, bf16[384,2048]{1,0:T(8,128)(2,1)}), (bf16[2048,384]{1,0:T(8,128)(2,1)}, bf16[384,2048]{1,0:T(8,128)(2,1)})) %all-reduce.5.cloned.1.call-update) | async-done | bytes 3145744 | tf_op jit(solution)/shard_map/psum | solution.py:1627
  805.1 4.3 convolution_convert_fusion.3
  831.9 4.2 convolution_convert_fusion.2
  846.1 78.2 %attend_back.3.refs_0_ = bf16[4,5,2,256,128]{4,3,2,1,0:T(8,128)(2,1)S(1)} custom-call(s32[8]{0:T(128)S(1)} %fusion.28.place_ref, s32[8]{0:T(128)S(1)} %select_n.299.blk_ref, s32[6]{0:T(128)S(1)} %bitcast.135, bf16[5,8,256,128]{3,2,1,0:T(8,128)(2,1)S(1)} %get-tuple-element.234.kept_ref, f32[3,1,2048]{2,1,0:T(1,128)S(1)} %get-tuple-element.235.lse_ref, ...), custom_call_target="tpu_custom_call" | custom-call | tf_op jit(solution)/shard_map/attend_back/pallas_call | solution.py:480
  930.3 10.8 back_end.1
  941.1 4.2 convolution_convert_fusion
  964.6 274.5 %tail.1 = (bf16[2048,384]{1,0:T(8,128)(2,1)}, bf16[384,2048]{1,0:T(8,128)(2,1)}, bf16[384,2048]{1,0:T(8,128)(2,1)}, bf16[768,384]{1,0:T(8,128)(2,1)}, bf16[384,2...) custom-call(bf16[2048,384]{1,0:T(8,128)(2,1)} %add_convert_fusion.9.refs_0_, ...), custom_call_target="tpu_custom_call" | custom-call | tf_op jit(solution)/shard_map/tail/pallas_call | solution.py:1057
  1248.3 3.9 concatenate.103
  1252.8 12.2 small_sum.1
  1284.0 5.1 maximum_convert_fusion
  (391 shorter events, 227.0 us)
Async XLA Ops:
  7.2 797.9 %all-reduce.5.cloned.1.call-start = ((), (), s32[]{:S(2)}) async-start(), calls=%async_computation | async-start | bytes 6291456 | tf_op jit(solution)/shard_map/psum | solution.py:1627
  17.8 36.4 %collective-permute-start.2 = (bf16[256,768]{1,0:T(8,128)(2,1)}, bf16[256,768]{1,0:T(8,128)(2,1)}, u32[]{:S(2)}, u32[]{:S(2)}) collective-permute-start(bf16[256,768]{1,0:T(8,128)(2,1)} %get-tuple-element.382), channel_id=1, source_target_pairs={{0,6},{2,4},{4,2},{6,0},{1,7},{3,5},{5,3},{7,1},{8,14},{10,12},{12... | collective-permute-start | bytes 1179656 | tf_op jit(solution)/shard_map/ppermute | solution.py:1141
  22.9 33.9 %collective-permute-start.1 = (bf16[256,768]{1,0:T(8,128)(2,1)}, bf16[256,768]{1,0:T(8,128)(2,1)}, u32[]{:S(2)}, u32[]{:S(2)}) collective-permute-start(bf16[256,768]{1,0:T(8,128)(2,1)} %get-tuple-element.383), channel_id=1, source_target_pairs={{0,4},{2,6},{4,0},{6,2},{1,5},{3,7},{5,1},{7,3},{8,12},{10,14},{12... | collective-permute-start | bytes 1179656 | tf_op jit(solution)/shard_map/ppermute | solution.py:1141
  22.9 33.9 %collective-permute-start = (bf16[256,768]{1,0:T(8,128)(2,1)}, bf16[256,768]{1,0:T(8,128)(2,1)}, u32[]{:S(2)}, u32[]{:S(2)}) collective-permute-start(bf16[256,768]{1,0:T(8,128)(2,1)} %get-tuple-element.384), channel_id=1, source_target_pairs={{0,2},{2,0},{4,6},{6,4},{1,3},{3,1},{5,7},{7,5},{8,10},{10,8},{12,... | collective-permute-start | bytes 1179656 | tf_op jit(solution)/shard_map/ppermute | solution.py:1141
  31.3 42.1 %collective-permute-start.3 = (bf16[384,2432]{1,0:T(8,128)(2,1)S(1)}, bf16[384,2432]{1,0:T(8,128)(2,1)}, u32[]{:S(2)}, u32[]{:S(2)}) collective-permute-start(bf16[384,2432]{1,0:T(8,128)(2,1)S(1)} %concatenate.89.refs_3_.refs_2_), channel_id=1, source_target_pairs={{0,16},{8,24},{16,0},{24,8},{1,17},{9,25},{17,1},{25,9},{2,18},{10... | collective-permute-start | bytes 5603336 | tf_op jit(solution)/shard_map/ppermute | solution.py:1141
  73.4 115.0 %collective-permute-start.7 = (bf16[2,384,2048]{2,1,0:T(8,128)(2,1)}, bf16[2,384,2048]{2,1,0:T(8,128)(2,1)}, u32[]{:S(2)}, u32[]{:S(2)}) collective-permute-start(bf16[2,384,2048]{2,1,0:T(8,128)(2,1)} %get-tuple-element.165.refs_7_.refs_17_), channel_id=1, source_target_pairs={{0,16},{8,24},{16,0},{24,8},{1,17},{9,25},{17,1},{25,9},{2,18},{10... | collective-permute-start | bytes 9437192 | tf_op jit(solution)/shard_map/ppermute | solution.py:1141
  83.0 105.5 %collective-permute-start.6 = (bf16[2816,384]{1,0:T(8,128)(2,1)}, bf16[2816,384]{1,0:T(8,128)(2,1)}, u32[]{:S(2)}, u32[]{:S(2)}) collective-permute-start(bf16[2816,384]{1,0:T(8,128)(2,1)} %get-tuple-element.164.refs_3_.refs_13_), channel_id=1, source_target_pairs={{0,16},{8,24},{16,0},{24,8},{1,17},{9,25},{17,1},{25,9},{2,18},{10... | collective-permute-start | bytes 6488072 | tf_op jit(solution)/shard_map/ppermute | solution.py:1141
  86.4 111.1 %collective-permute-start.10 = (bf16[2,384,2048]{2,1,0:T(8,128)(2,1)}, bf16[2,384,2048]{2,1,0:T(8,128)(2,1)}, u32[]{:S(2)}, u32[]{:S(2)}) collective-permute-start(bf16[2,384,2048]{2,1,0:T(8,128)(2,1)} %get-tuple-element.165.refs_7_.refs_17_), channel_id=1, source_target_pairs={{0,8},{8,0},{16,24},{24,16},{1,9},{9,1},{17,25},{25,17},{2,10},{10... | collective-permute-start | bytes 9437192 | tf_op jit(solution)/shard_map/ppermute | solution.py:1141
  192.8 83.8 %collective-permute-start.12 = (bf16[384,2432]{0,1:T(8,128)(2,1)}, bf16[384,2432]{0,1:T(8,128)(2,1)}, u32[]{:S(2)}, u32[]{:S(2)}) collective-permute-start(bf16[384,2432]{0,1:T(8,128)(2,1)} %copy.68), channel_id=1, source_target_pairs={{0,16},{8,24},{16,0},{24,8},{1,17},{9,25},{17,1},{25,9},{2,18},{10... | collective-permute-start | bytes 5603336 | tf_op jit(solution)/shard_map/ppermute | solution.py:1141
  276.6 120.2 %collective-permute-start.17 = (bf16[2,384,2048]{2,1,0:T(8,128)(2,1)}, bf16[2,384,2048]{2,1,0:T(8,128)(2,1)}, u32[]{:S(2)}, u32[]{:S(2)}) collective-permute-start(bf16[2,384,2048]{2,1,0:T(8,128)(2,1)} %get-tuple-element.184.refs_7_.refs_9_), channel_id=1, source_target_pairs={{0,16},{8,24},{16,0},{24,8},{1,17},{9,25},{17,1},{25,9},{2,18},{10... | collective-permute-start | bytes 9437192 | tf_op jit(solution)/shard_map/ppermute | solution.py:1141
  278.2 16.6 %collective-permute-start.14 = (bf16[384,2432]{0,1:T(8,128)(2,1)}, bf16[384,2432]{0,1:T(8,128)(2,1)}, u32[]{:S(2)}, u32[]{:S(2)}) collective-permute-start(bf16[384,2432]{0,1:T(8,128)(2,1)} %collective-permute-done.12), channel_id=1, source_target_pairs={{0,8},{8,0},{16,24},{24,16},{1,9},{9,1},{17,25},{25,17},{2,10},{10... | collective-permute-start | bytes 5603336 | tf_op jit(solution)/shard_map/ppermute | solution.py:1141
  278.7 118.1 %collective-permute-start.16 = (bf16[2816,384]{1,0:T(8,128)(2,1)}, bf16[2816,384]{1,0:T(8,128)(2,1)}, u32[]{:S(2)}, u32[]{:S(2)}) collective-permute-start(bf16[2816,384]{1,0:T(8,128)(2,1)} %get-tuple-element.170.refs_3_.refs_5_), channel_id=1, source_target_pairs={{0,16},{8,24},{16,0},{24,8},{1,17},{9,25},{17,1},{25,9},{2,18},{10... | collective-permute-start | bytes 6488072 | tf_op jit(solution)/shard_map/ppermute | solution.py:1141
  279.2 117.6 %collective-permute-start.15 = (bf16[512,768]{1,0:T(8,128)(2,1)}, bf16[512,768]{1,0:T(8,128)(2,1)}, u32[]{:S(2)}, u32[]{:S(2)}) collective-permute-start(bf16[512,768]{1,0:T(8,128)(2,1)} %pad_maximum_fusion.6), channel_id=1, source_target_pairs={{0,1},{1,0},{2,3},{3,2},{4,5},{5,4},{6,7},{7,6},{8,9},{9,8},{10,11... | collective-permute-start | bytes 2359304 | tf_op jit(solution)/shard_map/ppermute | solution.py:1141
  294.7 111.3 %collective-permute-start.20 = (bf16[2,384,2048]{2,1,0:T(8,128)(2,1)}, bf16[2,384,2048]{2,1,0:T(8,128)(2,1)}, u32[]{:S(2)}, u32[]{:S(2)}) collective-permute-start(bf16[2,384,2048]{2,1,0:T(8,128)(2,1)} %get-tuple-element.184.refs_7_.refs_9_), channel_id=1, source_target_pairs={{0,8},{8,0},{16,24},{24,16},{1,9},{9,1},{17,25},{25,17},{2,10},{10... | collective-permute-start | bytes 9437192 | tf_op jit(solution)/shard_map/ppermute | solution.py:1141
  487.1 61.7 %collective-permute-start.24 = (bf16[256,768]{1,0:T(8,128)(2,1)}, bf16[256,768]{1,0:T(8,128)(2,1)}, u32[]{:S(2)}, u32[]{:S(2)}) collective-permute-start(bf16[256,768]{1,0:T(8,128)(2,1)} %get-tuple-element.378), channel_id=1, source_target_pairs={{0,6},{2,4},{4,2},{6,0},{1,7},{3,5},{5,3},{7,1},{8,14},{10,12},{12... | collective-permute-start | bytes 1179656 | tf_op jit(solution)/shard_map/ppermute | solution.py:1141
  489.4 59.4 %collective-permute-start.23 = (bf16[256,768]{1,0:T(8,128)(2,1)}, bf16[256,768]{1,0:T(8,128)(2,1)}, u32[]{:S(2)}, u32[]{:S(2)}) collective-permute-start(bf16[256,768]{1,0:T(8,128)(2,1)} %get-tuple-element.379), channel_id=1, source_target_pairs={{0,4},{2,6},{4,0},{6,2},{1,5},{3,7},{5,1},{7,3},{8,12},{10,14},{12... | collective-permute-start | bytes 1179656 | tf_op jit(solution)/shard_map/ppermute | solution.py:1141
  489.4 59.4 %collective-permute-start.22 = (bf16[256,768]{1,0:T(8,128)(2,1)}, bf16[256,768]{1,0:T(8,128)(2,1)}, u32[]{:S(2)}, u32[]{:S(2)}) collective-permute-start(bf16[256,768]{1,0:T(8,128)(2,1)} %get-tuple-element.380), channel_id=1, source_target_pairs={{0,2},{2,0},{4,6},{6,4},{1,3},{3,1},{5,7},{7,5},{8,10},{10,8},{12,... | collective-permute-start | bytes 1179656 | tf_op jit(solution)/shard_map/ppermute | solution.py:1141
  554.6 16.4 %collective-permute-start.27 = (bf16[768,2048]{1,0:T(8,128)(2,1)S(1)}, bf16[768,2048]{1,0:T(8,128)(2,1)S(1)}, u32[]{:S(2)}, u32[]{:S(2)}) collective-permute-start(bf16[768,2048]{1,0:T(8,128)(2,1)S(1)} %convolution_convert_fusion.13), channel_id=1, source_target_pairs={{0,8},{8,0},{16,24},{24,16},{1,9},{9,1},{17,25},{25,17},{2,10},{10... | collective-permute-start | bytes 9437192 | tf_op jit(solution)/shard_map/ppermute | solution.py:1141
  554.6 16.3 %collective-permute-start.26 = (bf16[768,2048]{1,0:T(8,128)(2,1)S(1)}, bf16[768,2048]{1,0:T(8,128)(2,1)S(1)}, u32[]{:S(2)}, u32[]{:S(2)}) collective-permute-start(bf16[768,2048]{1,0:T(8,128)(2,1)S(1)} %convolution_convert_fusion.14), channel_id=1, source_target_pairs={{0,8},{8,0},{16,24},{24,16},{1,9},{9,1},{17,25},{25,17},{2,10},{10... | collective-permute-start | bytes 9437192 | tf_op jit(solution)/shard_map/ppermute | solution.py:1141
  557.0 16.0 %collective-permute-start.25 = (bf16[2048,768]{1,0:T(8,128)(2,1)S(1)}, bf16[2048,768]{1,0:T(8,128)(2,1)S(1)}, u32[]{:S(2)}, u32[]{:S(2)}) collective-permute-start(bf16[2048,768]{1,0:T(8,128)(2,1)S(1)} %convolution_convert_fusion.15), channel_id=1, source_target_pairs={{0,8},{8,0},{16,24},{24,16},{1,9},{9,1},{17,25},{25,17},{2,10},{10... | collective-permute-start | bytes 9437192 | tf_op jit(solution)/shard_map/ppermute | solution.py:1141
  579.2 98.8 %collective-permute-start.30 = (bf16[384,2048]{1,0:T(8,128)(2,1)}, bf16[384,2048]{1,0:T(8,128)(2,1)}, u32[]{:S(2)}, u32[]{:S(2)}) collective-permute-start(bf16[384,2048]{1,0:T(8,128)(2,1)} %slice.359), channel_id=1, source_target_pairs={{0,16},{8,24},{16,0},{24,8},{1,17},{9,25},{17,1},{25,9},{2,18},{10... | collective-permute-start | bytes 4718600 | tf_op jit(solution)/shard_map/ppermute | solution.py:1141
  579.8 98.3 %collective-permute-start.29 = (bf16[2048,384]{1,0:T(8,128)(2,1)}, bf16[2048,384]{1,0:T(8,128)(2,1)}, u32[]{:S(2)}, u32[]{:S(2)}) collective-permute-start(bf16[2048,384]{1,0:T(8,128)(2,1)} %slice.358), channel_id=1, source_target_pairs={{0,16},{8,24},{16,0},{24,8},{1,17},{9,25},{17,1},{25,9},{2,18},{10... | collective-permute-start | bytes 4718600 | tf_op jit(solution)/shard_map/ppermute | solution.py:1141
  687.3 18.5 %collective-permute-start.31 = (bf16[512,768]{1,0:T(8,128)(2,1)S(1)}, bf16[512,768]{1,0:T(8,128)(2,1)S(1)}, u32[]{:S(2)}, u32[]{:S(2)}) collective-permute-start(bf16[512,768]{1,0:T(8,128)(2,1)S(1)} %pad_maximum_fusion.7), channel_id=1, source_target_pairs={{0,1},{1,0},{2,3},{3,2},{4,5},{5,4},{6,7},{7,6},{8,9},{9,8},{10,11... | collective-permute-start | bytes 2359304 | tf_op jit(solution)/shard_map/ppermute | solution.py:1141
  809.4 26.7 %collective-permute-start.36 = (bf16[768,2432]{1,0:T(8,128)(2,1)S(1)}, bf16[768,2432]{1,0:T(8,128)(2,1)S(1)}, u32[]{:S(2)}, u32[]{:S(2)}) collective-permute-start(bf16[768,2432]{1,0:T(8,128)(2,1)S(1)} %convolution_convert_fusion.3), channel_id=1, source_target_pairs={{0,8},{8,0},{16,24},{24,16},{1,9},{9,1},{17,25},{25,17},{2,10},{10... | collective-permute-start | bytes 11206664 | tf_op jit(solution)/shard_map/ppermute | solution.py:1141
  813.3 22.9 %collective-permute-start.34 = (bf16[768,2048]{1,0:T(8,128)(2,1)S(1)}, bf16[768,2048]{1,0:T(8,128)(2,1)S(1)}, u32[]{:S(2)}, u32[]{:S(2)}) collective-permute-start(bf16[768,2048]{1,0:T(8,128)(2,1)S(1)} %convolution_convert_fusion.8), channel_id=1, source_target_pairs={{0,8},{8,0},{16,24},{24,16},{1,9},{9,1},{17,25},{25,17},{2,10},{10... | collective-permute-start | bytes 9437192 | tf_op jit(solution)/shard_map/ppermute | solution.py:1141
  813.8 22.3 %collective-permute-start.33 = (bf16[768,2048]{1,0:T(8,128)(2,1)S(1)}, bf16[768,2048]{1,0:T(8,128)(2,1)S(1)}, u32[]{:S(2)}, u32[]{:S(2)}) collective-permute-start(bf16[768,2048]{1,0:T(8,128)(2,1)S(1)} %convolution_convert_fusion.9), channel_id=1, source_target_pairs={{0,8},{8,0},{16,24},{24,16},{1,9},{9,1},{17,25},{25,17},{2,10},{10... | collective-permute-start | bytes 9437192 | tf_op jit(solution)/shard_map/ppermute | solution.py:1141
  817.4 18.7 %collective-permute-start.32 = (bf16[2048,768]{1,0:T(8,128)(2,1)}, bf16[2048,768]{1,0:T(8,128)(2,1)S(1)}, u32[]{:S(2)}, u32[]{:S(2)}) collective-permute-start(bf16[2048,768]{1,0:T(8,128)(2,1)} %convolution_convert_fusion.10), channel_id=1, source_target_pairs={{0,8},{8,0},{16,24},{24,16},{1,9},{9,1},{17,25},{25,17},{2,10},{10... | collective-permute-start | bytes 9437192 | tf_op jit(solution)/shard_map/ppermute | solution.py:1141
  843.5 85.6 %collective-permute-start.38 = (bf16[384,2048]{1,0:T(8,128)(2,1)S(1)}, bf16[384,2048]{1,0:T(8,128)(2,1)S(1)}, u32[]{:S(2)}, u32[]{:S(2)}) collective-permute-start(bf16[384,2048]{1,0:T(8,128)(2,1)S(1)} %slice.363), channel_id=1, source_target_pairs={{0,16},{8,24},{16,0},{24,8},{1,17},{9,25},{17,1},{25,9},{2,18},{10... | collective-permute-start | bytes 4718600 | tf_op jit(solution)/shard_map/ppermute | solution.py:1141
  845.0 85.3 %collective-permute-start.37 = (bf16[2048,384]{1,0:T(8,128)(2,1)}, bf16[2048,384]{1,0:T(8,128)(2,1)}, u32[]{:S(2)}, u32[]{:S(2)}) collective-permute-start(bf16[2048,384]{1,0:T(8,128)(2,1)} %slice.362), channel_id=1, source_target_pairs={{0,16},{8,24},{16,0},{24,8},{1,17},{9,25},{17,1},{25,9},{2,18},{10... | collective-permute-start | bytes 4718600 | tf_op jit(solution)/shard_map/ppermute | solution.py:1141
  945.3 16.0 %collective-permute-start.41 = (bf16[768,2432]{1,0:T(8,128)(2,1)S(1)}, bf16[768,2432]{1,0:T(8,128)(2,1)S(1)}, u32[]{:S(2)}, u32[]{:S(2)}) collective-permute-start(bf16[768,2432]{1,0:T(8,128)(2,1)S(1)} %convolution_convert_fusion), channel_id=1, source_target_pairs={{0,8},{8,0},{16,24},{24,16},{1,9},{9,1},{17,25},{25,17},{2,10},{10... | collective-permute-start | bytes 11206664 | tf_op jit(solution)/shard_map/ppermute | solution.py:1141
  950.8 288.2 %collective-permute-start.40 = (bf16[256,1536]{1,0:T(8,128)(2,1)S(1)}, bf16[256,1536]{1,0:T(8,128)(2,1)S(1)}, u32[]{:S(2)}, u32[]{:S(2)}) collective-permute-start(bf16[256,1536]{1,0:T(8,128)(2,1)S(1)} %get-tuple-element.274), channel_id=1, source_target_pairs={{0,1},{1,0},{2,3},{3,2},{4,5},{5,4},{6,7},{7,6},{8,9},{9,8},{10,11... | collective-permute-start | bytes 2359304 | tf_op jit(solution)/shard_map/ppermute | solution.py:1141
  952.3 286.7 %collective-permute-start.39 = (bf16[256,1536]{1,0:T(8,128)(2,1)S(1)}, bf16[256,1536]{1,0:T(8,128)(2,1)S(1)}, u32[]{:S(2)}, u32[]{:S(2)}) collective-permute-start(bf16[256,1536]{1,0:T(8,128)(2,1)S(1)} %get-tuple-element.272), channel_id=1, source_target_pairs={{0,1},{1,0},{2,3},{3,2},{4,5},{5,4},{6,7},{7,6},{8,9},{9,8},{10,11... | collective-permute-start | bytes 2359304 | tf_op jit(solution)/shard_map/ppermute | solution.py:1141
  (93 other events, 624.9 us)
Sparse Core Ops, SparseCore 0:
  685.4 119.6 all-reduce.4

commit v3 on v2

--- a/solution.py
+++ b/solution.py
@@ -603,13 +603,15 @@
         self.t = lax.axis_index("tp")
         self.started = []
 
-    def greet(self):
+    def greet(self, also=()):
         barrier = pltpu.get_barrier_semaphore()
+        for place in also:
+            pl.semaphore_signal(barrier, inc=1, device_id=place, device_id_type=pl.DeviceIdType.MESH)
         for step in self.steps:
             pl.semaphore_signal(
                 barrier, inc=1, device_id={"tp": peer(self.t, step)}, device_id_type=pl.DeviceIdType.MESH
             )
-        pl.semaphore_wait(barrier, len(self.steps))
+        pl.semaphore_wait(barrier, len(self.steps) + len(also))
 
     def copy(self, index):
         copy = pltpu.make_async_remote_copy(
@@ -720,31 +722,59 @@
     block_rows = r.packed.shape[3]
     for copy in copies.load_down(r.pieces("w_qkv"), r.w_mix):
         copy.wait()
+    turned = r.w_mix[:, 3 * width :].astype(F32).T
+    first = count * pack.hp
+    r.gains[0:2, :] = turned[first : first + 2, :]
     for half in range(2):
         rows = slice(half * block_rows, (half + 1) * block_rows)
         residual = r.residual[rows, :]
-        normed = (residual * unit_factor(residual) * r.gain[...]).astype(BF16)
+        normed = (residual * unit_factor(residual) * r.gains[0:1, :]).astype(BF16)
         r.normed[rows, :] = normed
         add = column_sums(residual * residual)
         r.stat[...] = jnp.broadcast_to(add if half == 0 else add + r.stat[0:1, :], r.stat.shape)
         project_rows(pack, r, count, width, half, rows, normed)
 
 
-def middle_kernel(pack, count, units, unit_block, steps, r):
+def middle_kernel(pack, count, units, unit_block, steps, fsdp, r):
     copies = Copies(r.sems)
     c = lax.axis_index("ctx")
     sums = pair_sums(r, 4, steps)
     block_rows = r.attended.shape[0] // 2
-    load_out = copies.load_beside([item.at[pl.ds(0, r.w_o.shape[0])] for item in r.pieces("w_back")], r.w_o)
+    f = lax.axis_index("fsdp")
+    other = {"fsdp": peer(f, 1)}
+    width = r.w_o.shape[0]
+    back, ffn = r.pieces("w_back"), r.pieces("w_units")
+    load_out = copies.load_beside([item.at[pl.ds(0, width)] for item in back], r.w_o)
     load_base = copies.load(r.residual, r.base)
-    load_units = copies.load_down([item.at[0] for item in r.pieces("w_units")], r.w_g)
-    load_units += copies.load_down([item.at[1] for item in r.pieces("w_units")], r.w_mix, units)
-    load_units += copies.load_beside(
-        [item.at[pl.ds(r.w_o.shape[0], units)] for item in r.pieces("w_back")], r.w_d
-    )
-    sums.greet()
+    load_units = copies.load_down([item.at[0] for item in ffn], r.w_g)
+    load_units += copies.load_down([item.at[1] for item in ffn], r.w_mix)
+    load_units += copies.load_beside([item.at[pl.ds(width, units)] for item in back], r.w_d)
+    sums.greet([other])
+    piece = back[0].shape[1]
+    crossing = []
+    for index in range(1, fsdp // 2):
+        place = pl.ds((fsdp // 2 + index) * piece, piece)
+        pairs = [
+            (back[index].at[pl.ds(0, width)], r.w_o.at[:, place]),
+            (ffn[index].at[0], r.w_g.at[place]),
+            (ffn[index].at[1], r.w_mix.at[place]),
+            (back[index].at[pl.ds(width, units)], r.w_d.at[:, place]),
+        ]
+        for source, target in pairs:
+            copy = pltpu.make_async_remote_copy(
+                src_ref=source,
+                dst_ref=target,
+                send_sem=r.core_send.at[len(crossing)],
+                recv_sem=r.core_recv.at[len(crossing)],
+                device_id=other,
+                device_id_type=pl.DeviceIdType.MESH,
+            )
+            copy.start()
+            crossing.append(copy)
     for copy in load_out:
         copy.wait()
+    for copy in crossing[::4]:
+        copy.wait_recv()
     halves = [slice(half * block_rows, (half + 1) * block_rows) for half in range(2)]
     size = pack.head_size
     for half, rows in enumerate(halves):
@@ -759,6 +789,9 @@
     load_base.wait()
     for copy in load_units:
         copy.wait()
+    for index, copy in enumerate(crossing):
+        if index % 4:
+            copy.wait_recv()
     for half, rows in enumerate(halves):
         branch = sums.finish(half)
         add = column_sums(branch * branch)
@@ -766,7 +799,7 @@
         middle = r.base[rows, :] + branch
         r.base[rows, :] = middle
         copies.save(r.base.at[rows], r.middle.at[rows])
-        normed = (middle * unit_factor(middle) * r.gain_two[...]).astype(BF16)
+        normed = (middle * unit_factor(middle) * r.gains[1:2, :]).astype(BF16)
         r.normed_keep[rows, :] = normed
         copies.save(r.normed_keep.at[rows], r.normed_two.at[rows])
         r.total[...] = jnp.zeros(r.total.shape, F32)
@@ -795,6 +828,8 @@
         copies.save(r.after_keep.at[rows], r.after.at[rows])
     copies.finish()
     sums.end()
+    for copy in crossing:
+        copy.wait_send()
 
 
 def back_kernel(pack, count, width, units, unit_block, steps, upper, feed, r):
@@ -867,7 +902,7 @@
             grad = r.base[rows, :].astype(F32)
             if upper:
                 load_value[half].wait()
-                back, add = norm_rows_back(sums.finish(half), r.values[rows, :], r.gain_one[...])
+                back, add = norm_rows_back(sums.finish(half), r.values[rows, :], r.upper_gains[0:1, :])
                 r.gain_grad[0:1, :] = add if half == 0 else r.gain_grad[0:1, :] + add
                 grad = grad + back
             load_middle.append(copies.load(r.middle.at[rows], r.values.at[rows]))
@@ -901,7 +936,7 @@
             copy.wait()
         for half, rows in enumerate(halves):
             load_middle[half].wait()
-            back, add = norm_rows_back(sums.finish(second + half), r.values[rows, :], r.gain_two[...])
+            back, add = norm_rows_back(sums.finish(second + half), r.values[rows, :], r.gains[1:2, :])
             r.gain_grad[1:2, :] = add if half == 0 else r.gain_grad[1:2, :] + add
             grad = r.grad_keep[rows, :] + back
             r.grad_keep[rows, :] = grad
@@ -920,18 +955,34 @@
         sums.end()
 
 
-def tail_kernel(chunks, halved, fsdp_step, fsdp_axis, counts, *refs):
-    units = counts
-    own = refs[:units]
-    far = refs[units : units + len(halved)]
-    outs = refs[units + len(halved) : 2 * units + len(halved)]
-    rest = refs[2 * units + len(halved) :]
-    inward = rest[:units]
-    crossed = rest[units : units + len(halved)]
-    x_send, x_recv, a_send, a_recv, b_send, b_recv, c_send, c_recv = rest[units + len(halved) :]
+def tail_kernel(chunks, given, halved, fsdp_step, fsdp_axis, units, *refs):
+    own, rest = refs[:units], refs[units:]
+    arrived, rest = rest[: len(given)], rest[len(given) :]
+    apart = [unit for unit, place in halved.items() if place is not None]
+    far, rest = rest[: len(apart)], rest[len(apart) :]
+    outs, rest = rest[:units], rest[units:]
+    inward, rest = rest[:units], rest[units:]
+    held, rest = rest[:units], rest[units:]
+    total_refs, rest = rest[:units], rest[units:]
+    first_refs, rest = rest[: len(given) + len(halved)], rest[len(given) + len(halved) :]
+    load_sem, save_sem, x_send, x_recv, a_send, a_recv, b_send, b_recv, c_send, c_recv = rest
+    extra = {unit: first_refs[place] for place, unit in enumerate(list(given) + list(halved))}
     c = lax.axis_index("ctx")
     f = lax.axis_index(fsdp_axis)
     mesh_id = pl.DeviceIdType.MESH
+    loads = {}
+    for unit in range(units):
+        rows = held[unit].shape[0]
+        loads[unit] = [
+            pltpu.make_async_copy(own[unit].at[pl.ds(0, rows)], held[unit], load_sem.at[unit])
+        ]
+        if unit in given:
+            place = given.index(unit)
+            loads[unit].append(
+                pltpu.make_async_copy(arrived[place], extra[unit], load_sem.at[units + place])
+            )
+        for copy in loads[unit]:
+            copy.start()
     barrier = pltpu.get_barrier_semaphore()
     pl.semaphore_signal(
         barrier, inc=1, device_id={fsdp_axis: peer(f, fsdp_step)}, device_id_type=mesh_id
@@ -952,19 +1003,19 @@
             device_id_type=mesh_id,
         )
 
-    def mine(unit):
-        return crossed[halved.index(unit)] if unit in halved else own[unit]
-
     def rows_of(index):
         unit, first, count = chunks[index]
         return unit, pl.ds(first, count)
 
     def x_copy(index):
-        unit, rows = rows_of(index)
-        place = halved.index(unit)
+        unit, first, count = chunks[index]
+        if unit in apart:
+            source = far[apart.index(unit)].at[pl.ds(first, count)]
+        else:
+            source = own[unit].at[pl.ds(held[unit].shape[0] + first, count)]
         return remote(
-            far[place].at[rows],
-            crossed[place].at[rows],
+            source,
+            extra[unit].at[pl.ds(first, count)],
             x_send.at[index],
             x_recv.at[index],
             {fsdp_axis: peer(f, fsdp_step)},
@@ -973,41 +1024,61 @@
     def a_copy(index):
         unit, rows = rows_of(index)
         return remote(
-            mine(unit).at[rows], inward[unit].at[rows], a_send.at[index], a_recv.at[index], {"ctx": 1 + c // 2}
+            held[unit].at[rows], inward[unit].at[rows], a_send.at[index], a_recv.at[index], {"ctx": 1 + c // 2}
         )
 
     def b_copy(index):
         unit, rows = rows_of(index)
         return remote(
-            inward[unit].at[rows], outs[unit].at[rows], b_send.at[index], b_recv.at[index], {"ctx": 3 - c}
+            inward[unit].at[rows], total_refs[unit].at[rows], b_send.at[index], b_recv.at[index], {"ctx": 3 - c}
         )
 
     def c_copy(index):
         unit, rows = rows_of(index)
         return remote(
-            outs[unit].at[rows], outs[unit].at[rows], c_send.at[index], c_recv.at[index], {"ctx": 3 * (c - 1)}
+            total_refs[unit].at[rows],
+            total_refs[unit].at[rows],
+            c_send.at[index],
+            c_recv.at[index],
+            {"ctx": 3 * (c - 1)},
         )
 
     def add(left, right, kind):
         return (left.astype(F32) + right.astype(F32)).astype(kind)
+
+    def is_first(index):
+        return chunks[index][1] == 0
+
+    def is_last(index):
+        return index + 1 == total or chunks[index + 1][0] != chunks[index][0]
+
+    def save(unit):
+        return pltpu.make_async_copy(total_refs[unit], outs[unit], save_sem.at[unit])
 
     total = len(chunks)
     for index in range(total):
         if chunks[index][0] in halved:
             x_copy(index).start()
 
-    def from_x(index):
+    def ready(index):
         unit, rows = rows_of(index)
+        if is_first(index):
+            for copy in loads[unit]:
+                copy.wait()
         if unit in halved:
-            place = halved.index(unit)
             x_copy(index).wait_recv()
-            crossed[place][rows, :] = add(own[unit][rows, :], crossed[place][rows, :], own[unit].dtype)
+        if unit in extra:
+            held[unit][rows, :] = add(held[unit][rows, :], extra[unit][rows, :], held[unit].dtype)
 
     @pl.when(is_end)
     def _():
         for index in range(total):
-            from_x(index)
+            ready(index)
             a_copy(index).start()
+        for index in range(total):
+            c_copy(index).wait_recv()
+            if is_last(index):
+                save(chunks[index][0]).start()
         for index in range(total):
             a_copy(index).wait_send()
 
@@ -1017,35 +1088,42 @@
         for index in range(total + lag):
             if index < total:
                 unit, rows = rows_of(index)
-                from_x(index)
+                ready(index)
                 a_copy(index).wait_recv()
-                inward[unit][rows, :] = add(mine(unit)[rows, :], inward[unit][rows, :], own[unit].dtype)
+                inward[unit][rows, :] = add(held[unit][rows, :], inward[unit][rows, :], held[unit].dtype)
                 b_copy(index).start()
             if index >= lag:
                 late = index - lag
                 unit, rows = rows_of(late)
                 b_copy(late).wait_recv()
-                outs[unit][rows, :] = add(inward[unit][rows, :], outs[unit][rows, :], outs[unit].dtype)
+                total_refs[unit][rows, :] = add(
+                    inward[unit][rows, :], total_refs[unit][rows, :], held[unit].dtype
+                )
                 c_copy(late).start()
+                if is_last(late):
+                    save(unit).start()
         for index in range(total):
             b_copy(index).wait_send()
             c_copy(index).wait_send()
 
-    @pl.when(is_end)
-    def _():
-        for index in range(total):
-            c_copy(index).wait_recv()
-
+    for unit in range(units):
+        save(unit).wait()
     for index in range(total):
         if chunks[index][0] in halved:
             x_copy(index).wait_send()
 
 
-def tail(arrays, far, fsdp_step, chunk_bytes=200 << 10):
-    halved = tuple(sorted(far))
+def tail(arrays, given, far, fsdp_step, chunk_bytes=128 << 10):
+    ready = tuple(sorted(given))
+    apart = [unit for unit in sorted(far) if far[unit] is not None]
+    halved = {unit: (apart.index(unit) if unit in apart else None) for unit in sorted(far)}
+    shapes = [
+        (item.shape[0] // (2 if unit in halved and unit not in apart else 1), item.shape[1])
+        for unit, item in enumerate(arrays)
+    ]
     chunks = []
-    for unit, item in enumerate(arrays):
-        rows, row_bytes = item.shape[0], item.shape[1] * item.dtype.itemsize
+    for unit, (rows, columns) in enumerate(shapes):
+        row_bytes = columns * arrays[unit].dtype.itemsize
         pieces = 1
         while rows % (2 * pieces) == 0 and (rows // (2 * pieces)) % 16 == 0 and (
             rows // pieces * row_bytes > chunk_bytes
@@ -1053,20 +1131,22 @@
             pieces *= 2
         chunks += [(unit, step * (rows // pieces), rows // pieces) for step in range(pieces)]
     dma = pltpu.SemaphoreType.DMA
-    buffers = [pltpu.VMEM(item.shape, item.dtype) for item in arrays]
+    buffers = [pltpu.VMEM(shape, item.dtype) for shape, item in zip(shapes, arrays)]
+    inputs = list(arrays) + [given[unit] for unit in ready] + [far[unit] for unit in apart]
     return pl.pallas_call(
-        functools.partial(tail_kernel, tuple(chunks), halved, fsdp_step, "fsdp", len(arrays)),
-        out_shape=[jax.ShapeDtypeStruct(item.shape, item.dtype) for item in arrays],
-        in_specs=[spec(pltpu.VMEM)] * (len(arrays) + len(halved)),
-        out_specs=[spec(pltpu.VMEM)] * len(arrays),
-        scratch_shapes=buffers
-        + [buffers[unit] for unit in halved]
+        functools.partial(tail_kernel, tuple(chunks), ready, halved, fsdp_step, "fsdp", len(arrays)),
+        out_shape=[jax.ShapeDtypeStruct(shape, item.dtype) for shape, item in zip(shapes, arrays)],
+        in_specs=[spec(pltpu.HBM)] * len(inputs),
+        out_specs=[spec(pltpu.HBM)] * len(arrays),
+        scratch_shapes=buffers * 3
+        + [buffers[unit] for unit in list(ready) + list(halved)]
+        + [dma((len(arrays) + len(ready),)), dma((len(arrays),))]
         + [dma((len(chunks),))] * 8,
         compiler_params=pltpu.CompilerParams(
-            vmem_limit_bytes=56 << 20, collective_id=2, has_side_effects=True
+            vmem_limit_bytes=60 << 20, collective_id=2, has_side_effects=True
         ),
         name="tail",
-    )(*arrays, *[far[unit] for unit in halved])
+    )(*inputs)
 
 
 def small_sum_kernel(steps, fsdp_axis, value_ref, out_ref, held_ref, *refs):
@@ -1198,11 +1278,14 @@
     tasks = {}
     pending = {}
 
+    def row_major(values):
+        return with_layout_constraint(values, Layout(tuple(range(values.ndim))))
+
     def gather_pieces(values):
         pieces = [values]
         for step in fsdp_steps[:-1]:
             for item in list(pieces):
-                pieces.append((yield swap(item, "fsdp", fsdp, step)))
+                pieces.append(row_major((yield swap(item, "fsdp", fsdp, step))))
         return pieces
 
     def reduce_grad(near, far, axis, until):
@@ -1210,12 +1293,16 @@
             near = add_low(near, (yield swap(far, "fsdp", fsdp, step)))
             if step != fsdp_steps[0]:
                 size = near.shape[axis] // 2
+                if until == "core" and size == piece and axis == 0:
+                    return near, None
                 near, far = (
                     lax.slice_in_dim(near, 0, size, axis=axis),
                     lax.slice_in_dim(near, size, 2 * size, axis=axis),
                 )
                 if until == "core" and size == piece:
                     return near, far
+                if until == "pair" and size == piece:
+                    return near, (yield swap(far, "fsdp", fsdp, fsdp_steps[0]))
         return near
 
     def begin(name, *args):
@@ -1225,6 +1312,7 @@
     own_first = {}
 
     def begin_gather(name, values):
+        values = row_major(values)
         tasks[name] = gather_pieces(values)
         own_first[name] = swap(values, "fsdp", fsdp, fsdp_steps[-1])
         pending[name] = next(tasks[name])
@@ -1250,6 +1338,7 @@
     def weight_pieces(name):
         pieces = finished(name)
         last = [own_first[name]] + [swap(item, "fsdp", fsdp, fsdp_steps[-1]) for item in pieces[1:]]
+        last = [row_major(item) for item in last]
         return pieces + last
 
     def exchange(sends):
@@ -1299,13 +1388,7 @@
             ],
             axis=1,
         )
-        return with_layout_constraint(jnp.concatenate(parts + [last], axis=1), Layout((0, 1)))
-
-    def gathered_gains(pieces):
-        rows = jnp.concatenate(
-            [item[:, 3 * width + heads_padded : 3 * width + heads_padded + 2] for item in pieces]
-        )
-        return [item[None] for item in rows.T.astype(F32)]
+        return row_major(jnp.concatenate(parts + [last], axis=1))
 
     share = model_width // tp
 
@@ -1337,7 +1420,9 @@
             axis=1,
         )
 
-    shard = own_qkv(0)
+    shard, cotangent, tokens, gate_up_weight, out_weight, down_weight = lax.optimization_barrier(
+        (own_qkv(0), cotangent, tokens, gate_up_weight, out_weight, down_weight)
+    )
     begin_gather(("w_qkv", 0), shard)
     cot_blocks = own_columns(cotangent)
     late_side = (c_index >= ctx // 2).astype(jnp.int32)
@@ -1368,7 +1453,7 @@
         [pick(cot_got, (deal_order[2 * c_index + half] // 2) ^ c_index) for half in range(2)], axis=0
     )
     weights = [{"w_qkv": weight_pieces(("w_qkv", 0))}]
-    gains = gathered_gains(weights[0]["w_qkv"])
+    gains = []
 
     def piece_inputs(layer, *names):
         return {
@@ -1389,7 +1474,6 @@
             "project",
             {
                 "residual": (residual, vmem),
-                "gain": (gains[2 * layer], vmem),
                 "bias": (bias_all[layer], vmem),
                 **piece_inputs(layer, "w_qkv"),
             },
@@ -1398,14 +1482,16 @@
                 "packed": packed_out(),
                 "logits": ((row_count, 128), F32, vmem),
                 "stat": ((8, model_width), F32, vmem),
+                "gains": ((8, model_width), F32, vmem),
             },
             {"w_mix": pltpu.VMEM((model_width, qkv_columns), BF16), "sems": dma((fsdp,))},
             None,
         )
-        stat_terms[layer][0] = jnp.sum(out["stat"][0])
+        stat_rows[layer][0] = out["stat"][0]
+        gains.append(out["gains"])
         return out["normed"], out["packed"], out["logits"]
 
-    stat_terms = [[None] * 3 for _ in range(layer_count)]
+    stat_rows = [[None] * 3 for _ in range(layer_count)]
     normed_one, packed, logits = project(0, residual)
     kept = []
     for layer in range(layer_count):
@@ -1429,8 +1515,12 @@
         inputs = {
             "att": (att, vmem),
             "residual": (residual, any_space),
-            "gain_two": (gains[2 * layer + 1], vmem),
-            **piece_inputs(layer, "w_back", "w_units"),
+            "gains": (gains[layer], vmem),
+            **{
+                key: value
+                for key, value in piece_inputs(layer, "w_back", "w_units").items()
+                if int(key.split("_")[-1]) <= fsdp // 2
+            },
         }
         outputs = {
             "attended": ((row_count, width), BF16, vmem),
@@ -1443,7 +1533,7 @@
             "stat": ((8, model_width), F32, vmem),
         }
         out = named_call(
-            functools.partial(middle_kernel, pack, ctx, units, unit_block, tp_steps),
+            functools.partial(middle_kernel, pack, ctx, units, unit_block, tp_steps, fsdp),
             "middle",
             inputs,
             outputs,
@@ -1460,6 +1550,8 @@
                 "hidden_keep": pltpu.VMEM((row_count, units), BF16),
                 "total": pltpu.VMEM((block_rows, model_width), F32),
                 "sems": dma((5 * fsdp + 16,)),
+                "core_send": dma((2 * fsdp,)),
+                "core_recv": dma((2 * fsdp,)),
                 **pair_scratch(4, tp_steps, block_rows, model_width),
             },
             4,
@@ -1477,14 +1569,13 @@
                 },
             )
         )
-        stat_terms[layer][1] = jnp.sum(out["stat"][0])
-        stat_terms[layer][2] = jnp.sum(out["stat"][1])
+        stat_rows[layer][1] = out["stat"][0]
+        stat_rows[layer][2] = out["stat"][1]
         residual = out["after"]
         if not last:
             residual, own_weights[later] = tick((residual, own_weights[later]), [("w_qkv", later)])
             begin_gather(("w_units", later), own_weights[later]["w_units"])
             weights.append({"w_qkv": weight_pieces(("w_qkv", later))})
-            gains += gathered_gains(weights[later]["w_qkv"])
             normed_one, packed, logits = project(later, residual)
 
     final_blocks = own_columns(residual)
@@ -1521,7 +1612,7 @@
                 outputs.update(one_part=(everything, BF16, vmem))
             else:
                 inputs.update(
-                    residual=(kept[upper]["residual"], any_space), gain_one=(gains[2 * upper], vmem)
+                    residual=(kept[upper]["residual"], any_space), upper_gains=(gains[upper], vmem)
                 )
         if layer is not None:
             state = kept[layer]
@@ -1530,7 +1621,7 @@
                 middle=(state["middle"], any_space),
                 gate=(state["gate"], any_space),
                 up=(state["up"], any_space),
-                gain_two=(gains[2 * layer + 1], vmem),
+                gains=(gains[layer], vmem),
                 **piece_inputs(layer, "w_back", "w_units"),
             )
             outputs.update(
@@ -1591,9 +1682,6 @@
         out = back_call(layer, upper, grad_base, back_got)
         if upper is None:
             out, out_got = lax.optimization_barrier((out, out_got))
-        else:
-            out, (grads["down", upper],) = lax.optimization_barrier((out, background_down))
-            background_gate = lax.psum([grads["gate", upper]], "ctx")
         if upper is not None:
             gain_grads[2 * upper] = out["gain_grad"][0]
             begin_qkv(upper, out)
@@ -1606,7 +1694,12 @@
                 pairs = [weight_grad(left, part) for part in halves(right)]
             else:
                 pairs = [weight_grad(part, right) for part in halves(left)]
-            reach = "fsdp" if name in ("down", "gate") else "core"
+            reach = "core"
+            if name in ("down", "gate"):
+                reach = "fsdp" if layer else "pair"
+            if upper is not None and name == "gate":
+                pairs, background = lax.optimization_barrier((pairs, background))
+                grads["down", upper], grads["gate", upper] = background
             begin((name, layer), *pairs, 1 if name in ("down", "out") else 0, reach)
         sends = tick(out["sends"], [(name, layer) for name in ffn] + [("qkv", layer + 1)])
         if upper is None:
@@ -1614,8 +1707,6 @@
                 [pick(out_got, (inverse[2 * c_index + half] // 2) ^ c_index) for half in range(2)], axis=0
             )
             mixed_pieces = column_pieces(mixed)
-        else:
-            sends, (grads["gate", upper],) = lax.optimization_barrier((sends, background_gate))
         back_got = attend_back(
             pack, place, blk, seq_ends, state["received"], state["lse"], state["att_turned"], sends
         )
@@ -1624,7 +1715,7 @@
             back_got, mixed_pieces = lax.optimization_barrier((back_got, mixed_pieces))
             mixed_out = from_local(all_columns(mixed_pieces)).astype(F32)
         if layer:
-            background_down = lax.psum([grads["down", layer]], "ctx")
+            background = lax.psum([grads["down", layer], grads["gate", layer]], "ctx")
         upper = layer
     out = back_call(None, 0, None, back_got)
     begin_qkv(0, out)
@@ -1635,7 +1726,8 @@
             part = add_low(part, swap(part, "tp", tp, step))
         one_pairs.append((part, swap(part, "tp", tp, tp_steps[-1])))
     names = [(name, 0) for name in ("down", "gate")]
-    arrays = [grads[name] for name in names]
+    arrays = [grads[name][0] for name in names]
+    given = {unit: grads[name][1] for unit, name in enumerate(names)}
     far_units = {}
     for name in [("up", 0), ("out", 0)] + [
         (name, layer) for layer in range(1, layer_count) for name in ("up", "out", "qkv")
@@ -1644,7 +1736,7 @@
         far_units[len(arrays)] = far
         arrays.append(near)
         names.append(name)
-    reduced = tail(arrays, far_units, fsdp_steps[0])
+    reduced = tail(arrays, given, far_units, fsdp_steps[0])
     one_pairs, reduced = lax.optimization_barrier((one_pairs, reduced))
     for name, item in zip(names, reduced):
         grads[name] = item
@@ -1652,11 +1744,11 @@
         [left.astype(F32) + right.astype(F32) for left, right in one_pairs], axis=0
     )
     first = kept[0]["residual"]
-    grad_from_one, gain_grads[0] = norm_back(grad_normed_one, first, unit_factor(first), gains[0])
+    grad_from_one, gain_grads[0] = norm_back(grad_normed_one, first, unit_factor(first), gains[0][0:1])
     grad_tokens = from_local(grad_base + grad_from_one)
 
     small = jnp.concatenate(
-        [from_local(jnp.stack(gain_grads)).reshape(-1), jnp.stack([item for row in stat_terms for item in row])]
+        [from_local(jnp.stack(gain_grads)).reshape(-1), jnp.sum(jnp.stack([item for row in stat_rows for item in row]), axis=1)]
         + bias_grads
     )
     used = small.shape[0]

time: 1310 us -> 1280 us (0.977)
  local copies, waits for them, and re-layouts: 119 us -> 91.5 us
    psum x1, waiting for transfers between devices: 17 us -> 0.01 us  [shards(): background = lax.psum([grads['down', layer], grads['gate', layer]], 'ctx')]
    convert_element_type x14 -> x12, other arithmetic: 26.3 us -> 29.9 us  [add_low(): return (left.astype(F32) + right.astype(F32)).astype(BF16)]
    unnamed x171 -> x199, local copies, waits for them, and re-layouts: 28.4 us -> 31 us
  transfers between devices with their start and end apart: 43 -> 43, of which waited for: 11 -> 9; matrix products, arithmetic and copies ran while one was open for 11% -> 11% of each run, Pallas kernels for 63% -> 71%
where the time goes in v3:
time: 1280 us; the launch traced here: 1270 us
  Pallas kernels  918 us (72%)
  local copies, waits for them, and re-layouts  91.5 us (7%)
  other arithmetic  72.1 us (6%)
  waiting for transfers between devices  62.5 us (5%)
  matrix products  57.1 us (4%)
  between operations  36.5 us (3%)
  starting transfers between devices  29.8 us (2%)
    pallas_call x7, Pallas kernels, named_call(): pl.pallas_call(body, out_shape=[jax.ShapeDtypeStruct(shape, kind) for sha...  325 us
    pallas_call x1, Pallas kernels, tail(): pl.pallas_call(functools.partial(tail_kernel, tuple(chunks), ready, halve...  267 us
    pallas_call x2, Pallas kernels, attend(): pl.pallas_call(functools.partial(attend_kernel, pack), out_shape=[jax.Sha...  158 us
    pallas_call x2, Pallas kernels, attend_back(): pl.pallas_call(functools.partial(attend_back_kernel, pack), out_shape=jax...  156 us
    ppermute x42, waiting for transfers between devices, swap(): return lax.ppermute(values, axis, [(i, i ^ step) for i in range(size)])  62.5 us
    dot_general x20, matrix products, weight_grad(): lax.dot_general(left, right, (((0,), (0,)), ((), ())), preferred_element_...  57.1 us
    unnamed x199, local copies, waits for them, and re-layouts  31 us
    convert_element_type x12, other arithmetic, add_low(): return (left.astype(F32) + right.astype(F32)).astype(BF16)  29.9 us
  transfers between devices with their start and end apart: 43, of which 9 were waited for; matrix products, arithmetic and copies ran while one was open for 11% of the time, Pallas kernels for 71%

profile of v3, /device:TPU:0, one launch (start us, length us, event | category | flops | bytes accessed | tf_op | source)
XLA Modules:
  0.0 1267.2 jit_solution(10948228503285310146)
XLA Ops:
  16.6 3.8 slice_bitcast_fusion.10
  21.4 3.8 concatenate.79.refs_2_
  40.3 3.6 concatenate.82.refs_2_
  47.4 6.7 slice_bitcast_fusion
  59.6 14.6 %collective-permute-done.3.refs_3_ = bf16[384,2432]{1,0:T(8,128)(2,1)S(1)} collective-permute-done((bf16[384,2432]{1,0:T(8,128)(2,1)}, bf16[384,2432]{1,0:T(8,128)(2,1)S(1)}, u32[]{:S(2)}, u32[]{:S(2)}) %collective-permute-start.3) | collective-permute-done | bytes 1867808 | tf_op jit(solution)/shard_map/ppermute | solution.py:1221
  86.9 12.1 project.2
  100.8 79.1 %attend.2 = (bf16[4,3,256,128]{3,2,1,0:T(8,128)(2,1)S(1)}, bf16[5,8,256,128]{3,2,1,0:T(8,128)(2,1)S(1)}, f32[3,1,2048]{2,1,0:T(1,128)S(1)}, f32[3,64,2048]{2,1,0:T(8,128)S(1)}) custom-call(s32[8]{0:T(128)S(1)} %fusion.28.place_ref, s32[8]{0:T(128)S(1)} %select_n.299.blk_ref, s32[6]{0:T(128)S(1)} %bitcast.121, bf16[4,5,2,256,128]{4,3,2,1,0:T(8,128)(2,1)S(1)} %copy-done.6), custom_call_target="tpu_custom_call" | custom-call | tf_op jit(solution)/shard_map/attend/pallas_call | solution.py:445
  181.9 7.3 collective-permute-done.6.refs_4_.refs_14_
  190.5 77.4 %middle.2 = (bf16[512,768]{1,0:T(8,128)(2,1)}, f32[512,1536]{1,0:T(8,128)}, bf16[512,1536]{1,0:T(8,128)(2,1)}, bf16[512,2048]{1,0:T(8,128)(2,1)}, bf16[512,2048]...) custom-call(bf16[4,3,256,128]{3,2,1,0:T(8,128)(2,1)} %copy-done.13, ...), custom_call_target="tpu_custom_call" | custom-call | tf_op jit(solution)/shard_map/middle/pallas_call | solution.py:552
  275.5 12.1 project.3
  289.3 78.9 %attend.3 = (bf16[4,3,256,128]{3,2,1,0:T(8,128)(2,1)S(1)}, bf16[5,8,256,128]{3,2,1,0:T(8,128)(2,1)S(1)}, f32[3,1,2048]{2,1,0:T(1,128)S(1)}, f32[3,64,2048]{2,1,0:T(8,128)S(1)}) custom-call(s32[8]{0:T(128)S(1)} %fusion.28.place_ref, s32[8]{0:T(128)S(1)} %select_n.299.blk_ref, s32[6]{0:T(128)S(1)} %bitcast.122, bf16[4,5,2,256,128]{4,3,2,1,0:T(8,128)(2,1)S(1)} %copy-done.7), custom_call_target="tpu_custom_call" | custom-call | tf_op jit(solution)/shard_map/attend/pallas_call | solution.py:445
  371.8 12.8 %collective-permute-done.14.refs_4_.refs_6_ = bf16[2816,384]{1,0:T(8,128)(2,1)} collective-permute-done((bf16[2816,384]{1,0:T(8,128)(2,1)}, bf16[2816,384]{1,0:T(8,128)(2,1)}, u32[]{:S(2)}, u32[]{:S(2)}) %collective-permute-start.14) | collective-permute-done | bytes 2162720 | tf_op jit(solution)/shard_map/ppermute | solution.py:1221
  387.6 6.1 collective-permute-done.16.refs_5_.refs_7_
  393.7 77.4 %middle.3 = (bf16[512,768]{1,0:T(8,128)(2,1)}, f32[512,1536]{1,0:T(8,128)}, bf16[512,1536]{1,0:T(8,128)(2,1)}, bf16[512,2048]{1,0:T(8,128)(2,1)}, bf16[512,2048]...) custom-call(bf16[4,3,256,128]{3,2,1,0:T(8,128)(2,1)} %copy-done.12, ...), custom_call_target="tpu_custom_call" | custom-call | tf_op jit(solution)/shard_map/middle/pallas_call | solution.py:552
  480.3 54.7 %back_top.1 = (bf16[512,1536]{1,0:T(8,128)(2,1)}, bf16[512,2048]{1,0:T(8,128)(2,1)}, bf16[512,2048]{1,0:T(8,128)(2,1)}, f32[512,1536]{1,0:T(8,128)}, bf16[512,15...) custom-call(bf16[512,1536]{1,0:T(8,128)(2,1)} %pad_maximum_fusion.5.refs_0_, ...), custom_call_target="tpu_custom_call" | custom-call | tf_op jit(solution)/shard_map/back_top/pallas_call | solution.py:552
  535.1 3.8 convolution_convert_fusion.13
  548.7 6.6 collective-permute-done.26
  579.3 78.8 %attend_back.2.refs_0_ = bf16[4,5,2,256,128]{4,3,2,1,0:T(8,128)(2,1)S(1)} custom-call(s32[8]{0:T(128)S(1)} %fusion.28.place_ref, s32[8]{0:T(128)S(1)} %select_n.299.blk_ref, s32[6]{0:T(128)S(1)} %bitcast.123, bf16[5,8,256,128]{3,2,1,0:T(8,128)(2,1)S(1)} %copy-done.5, f32[3,1,2048]{2,1,0:T(1,128)S(1)} %get-tuple-element.184.lse_ref, ...), custom_call_target="tpu_custom_call" | custom-call | tf_op jit(solution)/shard_map/attend_back/pallas_call | solution.py:480
  676.4 3.6 convolution_convert_fusion.4
  680.0 7.0 collective-permute-done.29
  688.0 80.6 %back.1 = (bf16[512,2432]{1,0:T(8,128)(2,1)}, f32[8,128]{1,0:T(8,128)}, bf16[512,1536]{1,0:T(8,128)(2,1)}, bf16[512,2048]{1,0:T(8,128)(2,1)}, bf16[512,2048]{1,0...) custom-call(bf16[4,5,2,256,128]{4,3,2,1,0:T(8,128)(2,1)} %copy-done., ...), custom_call_target="tpu_custom_call" | custom-call | tf_op jit(solution)/shard_map/back/pallas_call | solution.py:552
  768.6 6.2 convolution_convert_fusion.3
  785.9 3.6 convolution_convert_fusion.9
  821.8 4.4 convolution_convert_fusion.2
  826.1 77.6 %attend_back.3.refs_0_ = bf16[4,5,2,256,128]{4,3,2,1,0:T(8,128)(2,1)S(1)} custom-call(s32[8]{0:T(128)S(1)} %fusion.28.place_ref, s32[8]{0:T(128)S(1)} %select_n.299.blk_ref, s32[6]{0:T(128)S(1)} %bitcast.124, bf16[5,8,256,128]{3,2,1,0:T(8,128)(2,1)S(1)} %get-tuple-element.232.kept_ref, f32[3,1,2048]{2,1,0:T(1,128)S(1)} %get-tuple-element.233.lse_ref, ...), custom_call_target="tpu_custom_call" | custom-call | tf_op jit(solution)/shard_map/attend_back/pallas_call | solution.py:480
  907.6 10.9 back_end.1
  918.5 4.1 convolution_convert_fusion
  925.7 5.0 add_convert_fusion.3.refs_2_
  930.8 5.0 add_convert_fusion.1.refs_6_
  943.7 266.7 %tail.1 = (bf16[2048,384]{1,0:T(8,128)(2,1)}, bf16[384,2048]{1,0:T(8,128)(2,1)}, bf16[384,2048]{1,0:T(8,128)(2,1)}, bf16[768,384]{1,0:T(8,128)(2,1)}, bf16[384,2...) custom-call(bf16[2048,384]{1,0:T(8,128)(2,1)} %get-tuple-element.332.refs_0_,, ...), custom_call_target="tpu_custom_call" | custom-call | tf_op jit(solution)/shard_map/tail/pallas_call | solution.py:1136
  1221.1 11.3 small_sum.1
  1248.7 5.0 maximum_convert_fusion
  (396 shorter events, 200.2 us)
Async XLA Ops:
  7.2 782.2 %all-reduce.5.cloned.1.call-start = ((), (), s32[]{:S(2)}) async-start(), calls=%async_computation | async-start | bytes 6291456 | tf_op jit(solution)/shard_map/psum | solution.py:1718
  26.4 30.2 %collective-permute-start = (bf16[256,768]{1,0:T(8,128)(2,1)}, bf16[256,768]{1,0:T(8,128)(2,1)}, u32[]{:S(2)}, u32[]{:S(2)}) collective-permute-start(bf16[256,768]{1,0:T(8,128)(2,1)} %get-tuple-element.376), channel_id=1, source_target_pairs={{0,2},{2,0},{4,6},{6,4},{1,3},{3,1},{5,7},{7,5},{8,10},{10,8},{12,... | collective-permute-start | bytes 1179656 | tf_op jit(solution)/shard_map/ppermute | solution.py:1221
  29.5 30.1 %collective-permute-start.1 = (bf16[256,768]{1,0:T(8,128)(2,1)}, bf16[256,768]{1,0:T(8,128)(2,1)}, u32[]{:S(2)}, u32[]{:S(2)}) collective-permute-start(bf16[256,768]{1,0:T(8,128)(2,1)} %get-tuple-element.375), channel_id=1, source_target_pairs={{0,4},{2,6},{4,0},{6,2},{1,5},{3,7},{5,1},{7,3},{8,12},{10,14},{12... | collective-permute-start | bytes 1179656 | tf_op jit(solution)/shard_map/ppermute | solution.py:1221
  32.1 27.5 %collective-permute-start.2 = (bf16[256,768]{1,0:T(8,128)(2,1)}, bf16[256,768]{1,0:T(8,128)(2,1)}, u32[]{:S(2)}, u32[]{:S(2)}) collective-permute-start(bf16[256,768]{1,0:T(8,128)(2,1)} %get-tuple-element.374), channel_id=1, source_target_pairs={{0,6},{2,4},{4,2},{6,0},{1,7},{3,5},{5,3},{7,1},{8,14},{10,12},{12... | collective-permute-start | bytes 1179656 | tf_op jit(solution)/shard_map/ppermute | solution.py:1221
  32.1 42.1 %collective-permute-start.3 = (bf16[384,2432]{1,0:T(8,128)(2,1)}, bf16[384,2432]{1,0:T(8,128)(2,1)S(1)}, u32[]{:S(2)}, u32[]{:S(2)}) collective-permute-start(bf16[384,2432]{1,0:T(8,128)(2,1)} %concatenate.79.refs_2_), channel_id=1, source_target_pairs={{0,16},{8,24},{16,0},{24,8},{1,17},{9,25},{17,1},{25,9},{2,18},{10... | collective-permute-start | bytes 5603336 | tf_op jit(solution)/shard_map/ppermute | solution.py:1221
  74.2 115.0 %collective-permute-start.7 = (bf16[2,384,2048]{2,1,0:T(8,128)(2,1)}, bf16[2,384,2048]{2,1,0:T(8,128)(2,1)}, u32[]{:S(2)}, u32[]{:S(2)}) collective-permute-start(bf16[2,384,2048]{2,1,0:T(8,128)(2,1)} %get-tuple-element.171.refs_6_.refs_17_), channel_id=1, source_target_pairs={{0,16},{8,24},{16,0},{24,8},{1,17},{9,25},{17,1},{25,9},{2,18},{10... | collective-permute-start | bytes 9437192 | tf_op jit(solution)/shard_map/ppermute | solution.py:1221
  75.7 113.5 %collective-permute-start.6 = (bf16[2816,384]{1,0:T(8,128)(2,1)}, bf16[2816,384]{1,0:T(8,128)(2,1)}, u32[]{:S(2)}, u32[]{:S(2)}) collective-permute-start(bf16[2816,384]{1,0:T(8,128)(2,1)} %get-tuple-element.170.refs_3_.refs_13_), channel_id=1, source_target_pairs={{0,16},{8,24},{16,0},{24,8},{1,17},{9,25},{17,1},{25,9},{2,18},{10... | collective-permute-start | bytes 6488072 | tf_op jit(solution)/shard_map/ppermute | solution.py:1221
  78.3 112.2 %collective-permute-start.9 = (bf16[2,384,2048]{2,1,0:T(8,128)(2,1)}, bf16[2,384,2048]{2,1,0:T(8,128)(2,1)}, u32[]{:S(2)}, u32[]{:S(2)}) collective-permute-start(bf16[2,384,2048]{2,1,0:T(8,128)(2,1)} %get-tuple-element.171.refs_6_.refs_17_), channel_id=1, source_target_pairs={{0,8},{8,0},{16,24},{24,16},{1,9},{9,1},{17,25},{25,17},{2,10},{10... | collective-permute-start | bytes 9437192 | tf_op jit(solution)/shard_map/ppermute | solution.py:1221
  85.3 105.2 %collective-permute-start.8 = (bf16[2816,384]{1,0:T(8,128)(2,1)}, bf16[2816,384]{1,0:T(8,128)(2,1)}, u32[]{:S(2)}, u32[]{:S(2)}) collective-permute-start(bf16[2816,384]{1,0:T(8,128)(2,1)} %get-tuple-element.170.refs_3_.refs_13_), channel_id=1, source_target_pairs={{0,8},{8,0},{16,24},{24,16},{1,9},{9,1},{17,25},{25,17},{2,10},{10... | collective-permute-start | bytes 6488072 | tf_op jit(solution)/shard_map/ppermute | solution.py:1221
  189.2 78.7 %collective-permute-start.10 = (bf16[384,2432]{1,0:T(8,128)(2,1)}, bf16[384,2432]{1,0:T(8,128)(2,1)}, u32[]{:S(2)}, u32[]{:S(2)}) collective-permute-start(bf16[384,2432]{1,0:T(8,128)(2,1)} %concatenate.82.refs_2_), channel_id=1, source_target_pairs={{0,16},{8,24},{16,0},{24,8},{1,17},{9,25},{17,1},{25,9},{2,18},{10... | collective-permute-start | bytes 5603336 | tf_op jit(solution)/shard_map/ppermute | solution.py:1221
  267.9 116.7 %collective-permute-start.15 = (bf16[2,384,2048]{2,1,0:T(8,128)(2,1)}, bf16[2,384,2048]{2,1,0:T(8,128)(2,1)}, u32[]{:S(2)}, u32[]{:S(2)}) collective-permute-start(bf16[2,384,2048]{2,1,0:T(8,128)(2,1)} %get-tuple-element.191.refs_6_.refs_9_), channel_id=1, source_target_pairs={{0,16},{8,24},{16,0},{24,8},{1,17},{9,25},{17,1},{25,9},{2,18},{10... | collective-permute-start | bytes 9437192 | tf_op jit(solution)/shard_map/ppermute | solution.py:1221
  268.7 115.9 %collective-permute-start.14 = (bf16[2816,384]{1,0:T(8,128)(2,1)}, bf16[2816,384]{1,0:T(8,128)(2,1)}, u32[]{:S(2)}, u32[]{:S(2)}) collective-permute-start(bf16[2816,384]{1,0:T(8,128)(2,1)} %get-tuple-element.177.refs_3_.refs_5_), channel_id=1, source_target_pairs={{0,16},{8,24},{16,0},{24,8},{1,17},{9,25},{17,1},{25,9},{2,18},{10... | collective-permute-start | bytes 6488072 | tf_op jit(solution)/shard_map/ppermute | solution.py:1221
  270.2 101.6 %collective-permute-start.13 = (bf16[512,768]{1,0:T(8,128)(2,1)S(1)}, bf16[512,768]{1,0:T(8,128)(2,1)}, u32[]{:S(2)}, u32[]{:S(2)}) collective-permute-start(bf16[512,768]{1,0:T(8,128)(2,1)S(1)} %pad_maximum_fusion.6), channel_id=1, source_target_pairs={{0,1},{1,0},{2,3},{3,2},{4,5},{5,4},{6,7},{7,6},{8,9},{9,8},{10,11... | collective-permute-start | bytes 2359304 | tf_op jit(solution)/shard_map/ppermute | solution.py:1221
  272.8 120.8 %collective-permute-start.17 = (bf16[2,384,2048]{2,1,0:T(8,128)(2,1)}, bf16[2,384,2048]{2,1,0:T(8,128)(2,1)}, u32[]{:S(2)}, u32[]{:S(2)}) collective-permute-start(bf16[2,384,2048]{2,1,0:T(8,128)(2,1)} %get-tuple-element.191.refs_6_.refs_9_), channel_id=1, source_target_pairs={{0,8},{8,0},{16,24},{24,16},{1,9},{9,1},{17,25},{25,17},{2,10},{10... | collective-permute-start | bytes 9437192 | tf_op jit(solution)/shard_map/ppermute | solution.py:1221
  384.6 95.7 %collective-permute-start.19 = (bf16[2,384,2048]{2,1,0:T(8,128)(2,1)}, bf16[2,384,2048]{2,1,0:T(8,128)(2,1)}, u32[]{:S(2)}, u32[]{:S(2)}) collective-permute-start(bf16[2,384,2048]{2,1,0:T(8,128)(2,1)} %collective-permute-done.15.refs_7_.refs_10_), channel_id=1, source_target_pairs={{0,8},{8,0},{16,24},{24,16},{1,9},{9,1},{17,25},{25,17},{2,10},{10... | collective-permute-start | bytes 9437192 | tf_op jit(solution)/shard_map/ppermute | solution.py:1221
  385.1 95.2 %collective-permute-start.18 = (bf16[2816,384]{1,0:T(8,128)(2,1)}, bf16[2816,384]{1,0:T(8,128)(2,1)}, u32[]{:S(2)}, u32[]{:S(2)}) collective-permute-start(bf16[2816,384]{1,0:T(8,128)(2,1)} %collective-permute-done.14.refs_4_.refs_6_), channel_id=1, source_target_pairs={{0,8},{8,0},{16,24},{24,16},{1,9},{9,1},{17,25},{25,17},{2,10},{10... | collective-permute-start | bytes 6488072 | tf_op jit(solution)/shard_map/ppermute | solution.py:1221
  474.0 61.0 %collective-permute-start.20 = (bf16[256,768]{1,0:T(8,128)(2,1)}, bf16[256,768]{1,0:T(8,128)(2,1)S(1)}, u32[]{:S(2)}, u32[]{:S(2)}) collective-permute-start(bf16[256,768]{1,0:T(8,128)(2,1)} %get-tuple-element.372), channel_id=1, source_target_pairs={{0,2},{2,0},{4,6},{6,4},{1,3},{3,1},{5,7},{7,5},{8,10},{10,8},{12,... | collective-permute-start | bytes 1179656 | tf_op jit(solution)/shard_map/ppermute | solution.py:1221
  474.6 60.5 %collective-permute-start.21 = (bf16[256,768]{1,0:T(8,128)(2,1)}, bf16[256,768]{1,0:T(8,128)(2,1)}, u32[]{:S(2)}, u32[]{:S(2)}) collective-permute-start(bf16[256,768]{1,0:T(8,128)(2,1)} %get-tuple-element.371), channel_id=1, source_target_pairs={{0,4},{2,6},{4,0},{6,2},{1,5},{3,7},{5,1},{7,3},{8,12},{10,14},{12... | collective-permute-start | bytes 1179656 | tf_op jit(solution)/shard_map/ppermute | solution.py:1221
  478.0 57.0 %collective-permute-start.22 = (bf16[256,768]{1,0:T(8,128)(2,1)}, bf16[256,768]{1,0:T(8,128)(2,1)}, u32[]{:S(2)}, u32[]{:S(2)}) collective-permute-start(bf16[256,768]{1,0:T(8,128)(2,1)} %get-tuple-element.370), channel_id=1, source_target_pairs={{0,6},{2,4},{4,2},{6,0},{1,7},{3,5},{5,3},{7,1},{8,14},{10,12},{12... | collective-permute-start | bytes 1179656 | tf_op jit(solution)/shard_map/ppermute | solution.py:1221
  560.4 99.3 %collective-permute-start.28 = (bf16[384,2048]{1,0:T(8,128)(2,1)}, bf16[384,2048]{1,0:T(8,128)(2,1)}, u32[]{:S(2)}, u32[]{:S(2)}) collective-permute-start(bf16[384,2048]{1,0:T(8,128)(2,1)} %slice.290), channel_id=1, source_target_pairs={{0,16},{8,24},{16,0},{24,8},{1,17},{9,25},{17,1},{25,9},{2,18},{10... | collective-permute-start | bytes 4718600 | tf_op jit(solution)/shard_map/ppermute | solution.py:1221
  564.2 95.6 %collective-permute-start.27 = (bf16[2048,384]{1,0:T(8,128)(2,1)}, bf16[2048,384]{1,0:T(8,128)(2,1)}, u32[]{:S(2)}, u32[]{:S(2)}) collective-permute-start(bf16[2048,384]{1,0:T(8,128)(2,1)} %slice.289), channel_id=1, source_target_pairs={{0,16},{8,24},{16,0},{24,8},{1,17},{9,25},{17,1},{25,9},{2,18},{10... | collective-permute-start | bytes 4718600 | tf_op jit(solution)/shard_map/ppermute | solution.py:1221
  565.6 122.4 %collective-permute-start.31 = (bf16[2,384,2048]{2,1,0:T(8,128)(2,1)}, bf16[2,384,2048]{2,1,0:T(8,128)(2,1)}, u32[]{:S(2)}, u32[]{:S(2)}) collective-permute-start(bf16[2,384,2048]{2,1,0:T(8,128)(2,1)} %collective-permute-done.7.refs_7_.refs_18_), channel_id=1, source_target_pairs={{0,8},{8,0},{16,24},{24,16},{1,9},{9,1},{17,25},{25,17},{2,10},{10... | collective-permute-start | bytes 9437192 | tf_op jit(solution)/shard_map/ppermute | solution.py:1221
  574.7 113.3 %collective-permute-start.30 = (bf16[2816,384]{1,0:T(8,128)(2,1)}, bf16[2816,384]{1,0:T(8,128)(2,1)}, u32[]{:S(2)}, u32[]{:S(2)}) collective-permute-start(bf16[2816,384]{1,0:T(8,128)(2,1)} %collective-permute-done.6.refs_4_.refs_14_), channel_id=1, source_target_pairs={{0,8},{8,0},{16,24},{24,16},{1,9},{9,1},{17,25},{25,17},{2,10},{10... | collective-permute-start | bytes 6488072 | tf_op jit(solution)/shard_map/ppermute | solution.py:1221
  667.5 19.5 %collective-permute-start.29 = (bf16[512,768]{1,0:T(8,128)(2,1)S(1)}, bf16[512,768]{1,0:T(8,128)(2,1)S(1)}, u32[]{:S(2)}, u32[]{:S(2)}) collective-permute-start(bf16[512,768]{1,0:T(8,128)(2,1)S(1)} %pad_maximum_fusion.7), channel_id=1, source_target_pairs={{0,1},{1,0},{2,3},{3,2},{4,5},{5,4},{6,7},{7,6},{8,9},{9,8},{10,11... | collective-permute-start | bytes 2359304 | tf_op jit(solution)/shard_map/ppermute | solution.py:1221
  774.8 30.2 %collective-permute-start.36 = (bf16[768,2432]{1,0:T(8,128)(2,1)}, bf16[768,2432]{1,0:T(8,128)(2,1)}, u32[]{:S(2)}, u32[]{:S(2)}) collective-permute-start(bf16[768,2432]{1,0:T(8,128)(2,1)} %convolution_convert_fusion.3), channel_id=1, source_target_pairs={{0,8},{8,0},{16,24},{24,16},{1,9},{9,1},{17,25},{25,17},{2,10},{10... | collective-permute-start | bytes 11206664 | tf_op jit(solution)/shard_map/ppermute | solution.py:1221
  778.3 26.7 %collective-permute-start.34 = (bf16[768,2048]{1,0:T(8,128)(2,1)}, bf16[768,2048]{1,0:T(8,128)(2,1)}, u32[]{:S(2)}, u32[]{:S(2)}) collective-permute-start(bf16[768,2048]{1,0:T(8,128)(2,1)} %convolution_convert_fusion.7), channel_id=1, source_target_pairs={{0,8},{8,0},{16,24},{24,16},{1,9},{9,1},{17,25},{25,17},{2,10},{10... | collective-permute-start | bytes 9437192 | tf_op jit(solution)/shard_map/ppermute | solution.py:1221
  785.8 19.2 %collective-permute-start.32 = (bf16[2048,768]{1,0:T(8,128)(2,1)}, bf16[2048,768]{1,0:T(8,128)(2,1)}, u32[]{:S(2)}, u32[]{:S(2)}) collective-permute-start(bf16[2048,768]{1,0:T(8,128)(2,1)} %convolution_convert_fusion.10), channel_id=1, source_target_pairs={{0,8},{8,0},{16,24},{24,16},{1,9},{9,1},{17,25},{25,17},{2,10},{10... | collective-permute-start | bytes 9437192 | tf_op jit(solution)/shard_map/ppermute | solution.py:1221
  809.1 96.1 %collective-permute-start.38 = (bf16[384,2048]{1,0:T(8,128)(2,1)S(1)}, bf16[384,2048]{1,0:T(8,128)(2,1)S(1)}, u32[]{:S(2)}, u32[]{:S(2)}) collective-permute-start(bf16[384,2048]{1,0:T(8,128)(2,1)S(1)} %get-tuple-element.331), channel_id=1, source_target_pairs={{0,16},{8,24},{16,0},{24,8},{1,17},{9,25},{17,1},{25,9},{2,18},{10... | collective-permute-start | bytes 4718600 | tf_op jit(solution)/shard_map/ppermute | solution.py:1221
  813.9 91.3 %collective-permute-start.37 = (bf16[2048,384]{1,0:T(8,128)(2,1)S(1)}, bf16[2048,384]{1,0:T(8,128)(2,1)S(1)}, u32[]{:S(2)}, u32[]{:S(2)}) collective-permute-start(bf16[2048,384]{1,0:T(8,128)(2,1)S(1)} %get-tuple-element.333), channel_id=1, source_target_pairs={{0,16},{8,24},{16,0},{24,8},{1,17},{9,25},{17,1},{25,9},{2,18},{10... | collective-permute-start | bytes 4718600 | tf_op jit(solution)/shard_map/ppermute | solution.py:1221
  922.6 18.3 %collective-permute-start.41 = (bf16[768,2432]{1,0:T(8,128)(2,1)S(1)}, bf16[768,2432]{1,0:T(8,128)(2,1)S(1)}, u32[]{:S(2)}, u32[]{:S(2)}) collective-permute-start(bf16[768,2432]{1,0:T(8,128)(2,1)S(1)} %convolution_convert_fusion), channel_id=1, source_target_pairs={{0,8},{8,0},{16,24},{24,16},{1,9},{9,1},{17,25},{25,17},{2,10},{10... | collective-permute-start | bytes 11206664 | tf_op jit(solution)/shard_map/ppermute | solution.py:1221
  935.9 274.5 %collective-permute-start.39 = (bf16[256,1536]{1,0:T(8,128)(2,1)S(1)}, bf16[256,1536]{1,0:T(8,128)(2,1)S(1)}, u32[]{:S(2)}, u32[]{:S(2)}) collective-permute-start(bf16[256,1536]{1,0:T(8,128)(2,1)S(1)} %get-tuple-element.272), channel_id=1, source_target_pairs={{0,1},{1,0},{2,3},{3,2},{4,5},{5,4},{6,7},{7,6},{8,9},{9,8},{10,11... | collective-permute-start | bytes 2359304 | tf_op jit(solution)/shard_map/ppermute | solution.py:1221
  936.4 274.0 %collective-permute-start.40 = (bf16[256,1536]{1,0:T(8,128)(2,1)S(1)}, bf16[256,1536]{1,0:T(8,128)(2,1)S(1)}, u32[]{:S(2)}, u32[]{:S(2)}) collective-permute-start(bf16[256,1536]{1,0:T(8,128)(2,1)S(1)} %get-tuple-element.274), channel_id=1, source_target_pairs={{0,1},{1,0},{2,3},{3,2},{4,5},{5,4},{6,7},{7,6},{8,9},{9,8},{10,11... | collective-permute-start | bytes 2359304 | tf_op jit(solution)/shard_map/ppermute | solution.py:1221
  (107 other events, 633.4 us)
Sparse Core Ops, SparseCore 0:
  666.3 120.7 all-reduce.4

commit v4 on v3

--- a/solution.py
+++ b/solution.py
@@ -577,7 +577,7 @@
         for index, item in enumerate(pieces):
             place = target.at[pl.ds(index * rows, rows)]
             if columns is not None:
-                place = target.at[pl.ds(index * rows, rows), pl.ds(0, columns)]
+                place = target.at[pl.ds(index * rows, rows), pl.ds(*columns)]
             out.append(self.load(item, place))
         return out
 
@@ -716,11 +716,19 @@
     write_tiles(pack, count, r.packed, half, query, key, value, forget)
 
 
-def first_kernel(pack, count, width, r):
+def load_projections(copies, r, width, layer):
+    out = []
+    for j in range(3):
+        out += copies.load_down([item.at[j] for item in r.pieces("w_qkv")], r.w_mix, (j * width, width))
+    last = [item.at[:, pl.ds(128 * layer, 128)] for item in r.pieces("w_last")]
+    return out + copies.load_down(last, r.w_mix, (3 * width, 128))
+
+
+def first_kernel(pack, count, width, layer, r):
     copies = Copies(r.sems)
     c = lax.axis_index("ctx")
     block_rows = r.packed.shape[3]
-    for copy in copies.load_down(r.pieces("w_qkv"), r.w_mix):
+    for copy in load_projections(copies, r, width, layer):
         copy.wait()
     turned = r.w_mix[:, 3 * width :].astype(F32).T
     first = count * pack.hp
@@ -832,10 +840,11 @@
         copy.wait_send()
 
 
-def back_kernel(pack, count, width, units, unit_block, steps, upper, feed, r):
+def back_kernel(pack, count, width, units, unit_block, steps, upper_layer, feed, r):
     copies = Copies(r.sems)
     c = lax.axis_index("ctx")
     size = pack.head_size
+    upper = upper_layer is not None
     forget_tile, forget_lane = pack.value_place(pack.hp)
     if feed:
         sums = pair_sums(r, 4 if upper else 2, steps)
@@ -843,7 +852,7 @@
     block_rows = r.total.shape[0]
     halves = [slice(half * block_rows, (half + 1) * block_rows) for half in range(2)]
     if upper:
-        load_qkv = copies.load_down(r.pieces("w_qkv"), r.w_mix, 3 * width + 128)
+        load_qkv = load_projections(copies, r, width, upper_layer)
     if feed:
         if upper:
             load_value = [copies.load(r.residual.at[rows], r.values.at[rows]) for rows in halves]
@@ -895,7 +904,7 @@
             else:
                 r.one_part[rows, :] = part
     if feed:
-        waits += copies.load_down([item.at[1] for item in r.pieces("w_units")], r.w_mix, units)
+        waits += copies.load_down([item.at[1] for item in r.pieces("w_units")], r.w_mix, (0, units))
         load_base.wait()
         load_middle = []
         for half, rows in enumerate(halves):
@@ -1379,16 +1388,17 @@
     place = 2 * jnp.bitwise_xor(inverse // 2, c_index) + inverse % 2
 
     def own_qkv(layer):
-        parts = [jnp.pad(query_key_value[layer, j], ((0, 0), (0, more_columns))) for j in range(3)]
-        last = jnp.concatenate(
-            [
+        return jnp.pad(query_key_value[layer], ((0, 0), (0, 0), (0, more_columns)))
+
+    def own_last():
+        parts = []
+        for layer in range(layer_count):
+            parts += [
                 jnp.pad(forget_weight[layer], ((0, 0), (0, heads_padded - heads_here))),
                 norm_gains[layer].T,
                 jnp.zeros((piece, 128 - heads_padded - 2), BF16),
-            ],
-            axis=1,
-        )
-        return row_major(jnp.concatenate(parts + [last], axis=1))
+            ]
+        return jnp.concatenate(parts, axis=1)
 
     share = model_width // tp
 
@@ -1424,6 +1434,9 @@
         (own_qkv(0), cotangent, tokens, gate_up_weight, out_weight, down_weight)
     )
     begin_gather(("w_qkv", 0), shard)
+    begin_gather(("w_last", 0), own_last())
+    output_places = [(inverse[2 * c_index + half] // 2) ^ c_index for half in range(2)]
+    cot_places = [(deal_order[2 * c_index + half] // 2) ^ c_index for half in range(2)]
     cot_blocks = own_columns(cotangent)
     late_side = (c_index >= ctx // 2).astype(jnp.int32)
     cot_sends = []
@@ -1446,13 +1459,15 @@
         own_weights[layer]["w_qkv"] = own_qkv(layer)
 
     residual = to_local(tokens)
-    own_weights, residual, cot_got = tick((own_weights, residual, cot_got), [("w_qkv", 0)])
+    own_weights, residual, cot_got, output_places, cot_places = tick(
+        (own_weights, residual, cot_got, output_places, cot_places), [("w_qkv", 0), ("w_last", 0)]
+    )
     for name in ("w_back", "w_units"):
         begin_gather((name, 0), own_weights[0][name])
     cot_mine = jnp.concatenate(
-        [pick(cot_got, (deal_order[2 * c_index + half] // 2) ^ c_index) for half in range(2)], axis=0
+        [pick(cot_got, cot_places[half]) for half in range(2)], axis=0
     )
-    weights = [{"w_qkv": weight_pieces(("w_qkv", 0))}]
+    weights = [{"w_qkv": weight_pieces(("w_qkv", 0)), "w_last": weight_pieces(("w_last", 0))}]
     gains = []
 
     def piece_inputs(layer, *names):
@@ -1470,12 +1485,12 @@
 
     def project(layer, residual):
         out = named_call(
-            functools.partial(first_kernel, pack, ctx, width),
+            functools.partial(first_kernel, pack, ctx, width, layer),
             "project",
             {
                 "residual": (residual, vmem),
                 "bias": (bias_all[layer], vmem),
-                **piece_inputs(layer, "w_qkv"),
+                **piece_inputs(layer, "w_qkv", "w_last"),
             },
             {
                 "normed": (everything, BF16, vmem),
@@ -1484,7 +1499,7 @@
                 "stat": ((8, model_width), F32, vmem),
                 "gains": ((8, model_width), F32, vmem),
             },
-            {"w_mix": pltpu.VMEM((model_width, qkv_columns), BF16), "sems": dma((fsdp,))},
+            {"w_mix": pltpu.VMEM((model_width, qkv_columns), BF16), "sems": dma((4 * fsdp,))},
             None,
         )
         stat_rows[layer][0] = out["stat"][0]
@@ -1573,9 +1588,13 @@
         stat_rows[layer][2] = out["stat"][1]
         residual = out["after"]
         if not last:
-            residual, own_weights[later] = tick((residual, own_weights[later]), [("w_qkv", later)])
+            residual, own_weights[later] = tick(
+                (residual, own_weights[later]), [("w_qkv", later), ("w_back", later)]
+            )
             begin_gather(("w_units", later), own_weights[later]["w_units"])
-            weights.append({"w_qkv": weight_pieces(("w_qkv", later))})
+            weights.append(
+                {"w_qkv": weight_pieces(("w_qkv", later)), "w_last": weights[0]["w_last"]}
+            )
             normed_one, packed, logits = project(later, residual)
 
     final_blocks = own_columns(residual)
@@ -1598,11 +1617,11 @@
     bias_grads = [None] * layer_count
 
     def back_call(layer, upper, grad_base, back_got):
-        inputs, outputs, scratch = {}, {}, {"w_mix": mix, "sems": dma((5 * fsdp + 20,))}
+        inputs, outputs, scratch = {}, {}, {"w_mix": mix, "sems": dma((8 * fsdp + 24,))}
         scratch["total"] = pltpu.VMEM((block_rows, model_width), F32)
         if upper is not None:
             inputs.update(
-                back=(back_got, vmem), logits=(kept[upper]["logits"], vmem), **piece_inputs(upper, "w_qkv")
+                back=(back_got, vmem), logits=(kept[upper]["logits"], vmem), **piece_inputs(upper, "w_qkv", "w_last")
             )
             outputs.update(
                 grads=((row_count, qkv_columns), BF16, any_space), bias_grad=((8, 128), F32, vmem)
@@ -1655,7 +1674,7 @@
                 units,
                 unit_block,
                 tp_steps,
-                upper is not None,
+                upper,
                 layer is not None,
             ),
             "back_top" if upper is None else "back_end" if layer is None else "back",
@@ -1701,17 +1720,19 @@
                 pairs, background = lax.optimization_barrier((pairs, background))
                 grads["down", upper], grads["gate", upper] = background
             begin((name, layer), *pairs, 1 if name in ("down", "out") else 0, reach)
-        sends = tick(out["sends"], [(name, layer) for name in ffn] + [("qkv", layer + 1)])
+        sends = tick(out["sends"], [(name, layer) for name in ("down", "gate")])
         if upper is None:
             mixed = jnp.concatenate(
-                [pick(out_got, (inverse[2 * c_index + half] // 2) ^ c_index) for half in range(2)], axis=0
-            )
+                [pick(out_got, output_places[half]) for half in range(2)], axis=0
+            )
+        if layer == 0:
+            sends, mixed = lax.optimization_barrier((sends, mixed))
             mixed_pieces = column_pieces(mixed)
         back_got = attend_back(
             pack, place, blk, seq_ends, state["received"], state["lse"], state["att_turned"], sends
         )
         back_got = tick(back_got, [(name, layer) for name in ffn] + [("qkv", layer + 1)])
-        if upper is None:
+        if layer == 0:
             back_got, mixed_pieces = lax.optimization_barrier((back_got, mixed_pieces))
             mixed_out = from_local(all_columns(mixed_pieces)).astype(F32)
         if layer:

time: 1280 us -> 1250 us (0.977)
  waiting for transfers between devices: 62.5 us -> 43.4 us
    ppermute x42 -> x45, waiting for transfers between devices: 62.5 us -> 35.8 us  [swap(): return lax.ppermute(values, axis, [(i, i ^ step) for i in range(size)])]
    unnamed x199 -> x203, local copies, waits for them, and re-layouts: 31 us -> 21.6 us
    ppermute x42 -> x45, starting transfers between devices: 29.7 us -> 32 us  [swap(): return lax.ppermute(values, axis, [(i, i ^ step) for i in range(size)])]
  transfers between devices with their start and end apart: 43 -> 46, of which waited for: 9 -> 10; matrix products, arithmetic and copies ran while one was open for 11% -> 12% of each run, Pallas kernels for 71% -> 72%
where the time goes in v4:
time: 1250 us; the launch traced here: 1240 us
  Pallas kernels  918 us (73%)
  local copies, waits for them, and re-layouts  80.2 us (6%)
  other arithmetic  74.9 us (6%)
  matrix products  59.3 us (5%)
  waiting for transfers between devices  43.4 us (3%)
  between operations  36.6 us (3%)
  starting transfers between devices  32 us (3%)
    pallas_call x7, Pallas kernels, named_call(): pl.pallas_call(body, out_shape=[jax.ShapeDtypeStruct(shape, kind) for sha...  325 us
    pallas_call x1, Pallas kernels, tail(): pl.pallas_call(functools.partial(tail_kernel, tuple(chunks), ready, halve...  268 us
    pallas_call x2, Pallas kernels, attend(): pl.pallas_call(functools.partial(attend_kernel, pack), out_shape=[jax.Sha...  158 us
    pallas_call x2, Pallas kernels, attend_back(): pl.pallas_call(functools.partial(attend_back_kernel, pack), out_shape=jax...  155 us
    dot_general x20, matrix products, weight_grad(): lax.dot_general(left, right, (((0,), (0,)), ((), ())), preferred_element_...  59.3 us
    ppermute x45, waiting for transfers between devices, swap(): return lax.ppermute(values, axis, [(i, i ^ step) for i in range(size)])  35.8 us
    ppermute x45, starting transfers between devices, swap(): return lax.ppermute(values, axis, [(i, i ^ step) for i in range(size)])  32 us
    convert_element_type x12, other arithmetic, add_low(): return (left.astype(F32) + right.astype(F32)).astype(BF16)  28.1 us
  transfers between devices with their start and end apart: 46, of which 10 were waited for; matrix products, arithmetic and copies ran while one was open for 12% of the time, Pallas kernels for 72%

profile of v4, /device:TPU:0, one launch (start us, length us, event | category | flops | bytes accessed | tf_op | source)
XLA Modules:
  0.0 1244.5 jit_solution(11933497572513930650)
XLA Ops:
  16.6 4.0 slice_bitcast_fusion.2
  33.0 3.9 slice_bitcast_fusion.4
  37.9 4.5 pad_maximum_fusion.3
  42.4 6.8 slice_bitcast_fusion
  62.2 3.7 pad_maximum_fusion.refs_0_.refs_1_
  65.9 8.0 collective-permute-done.4.refs_7_
  82.7 3.7 collective-permute-done.8.refs_9_
  87.1 12.1 project.2
  100.9 79.2 %attend.2 = (bf16[4,3,256,128]{3,2,1,0:T(8,128)(2,1)S(1)}, bf16[5,8,256,128]{3,2,1,0:T(8,128)(2,1)S(1)}, f32[3,1,2048]{2,1,0:T(1,128)S(1)}, f32[3,64,2048]{2,1,0:T(8,128)S(1)}) custom-call(s32[8]{0:T(128)S(1)} %fusion.28.place_ref, s32[8]{0:T(128)S(1)} %select_n.299.blk_ref, s32[6]{0:T(128)S(1)} %bitcast.113, bf16[4,5,2,256,128]{4,3,2,1,0:T(8,128)(2,1)S(1)} %copy-done.6), custom_call_target="tpu_custom_call" | custom-call | tf_op jit(solution)/shard_map/attend/pallas_call | solution.py:445
  182.2 6.8 collective-permute-done.9.refs_4_.refs_18_
  191.1 77.3 %middle.2 = (bf16[512,768]{1,0:T(8,128)(2,1)}, f32[512,1536]{1,0:T(8,128)}, bf16[512,1536]{1,0:T(8,128)(2,1)}, bf16[512,2048]{1,0:T(8,128)(2,1)}, bf16[512,2048]...) custom-call(bf16[4,3,256,128]{3,2,1,0:T(8,128)(2,1)} %copy-done.13, ...), custom_call_target="tpu_custom_call" | custom-call | tf_op jit(solution)/shard_map/middle/pallas_call | solution.py:552
  268.4 5.7 collective-permute-done.13.refs_3_
  282.0 12.1 project.3
  295.8 78.9 %attend.3 = (bf16[4,3,256,128]{3,2,1,0:T(8,128)(2,1)S(1)}, bf16[5,8,256,128]{3,2,1,0:T(8,128)(2,1)S(1)}, f32[3,1,2048]{2,1,0:T(1,128)S(1)}, f32[3,64,2048]{2,1,0:T(8,128)S(1)}) custom-call(s32[8]{0:T(128)S(1)} %fusion.28.place_ref, s32[8]{0:T(128)S(1)} %select_n.299.blk_ref, s32[6]{0:T(128)S(1)} %bitcast.114, bf16[4,5,2,256,128]{4,3,2,1,0:T(8,128)(2,1)S(1)} %copy-done.7), custom_call_target="tpu_custom_call" | custom-call | tf_op jit(solution)/shard_map/attend/pallas_call | solution.py:445
  382.3 5.1 collective-permute-done.19.refs_5_.refs_7_
  387.4 77.4 %middle.3 = (bf16[512,768]{1,0:T(8,128)(2,1)}, f32[512,1536]{1,0:T(8,128)}, bf16[512,1536]{1,0:T(8,128)(2,1)}, bf16[512,2048]{1,0:T(8,128)(2,1)}, bf16[512,2048]...) custom-call(bf16[4,3,256,128]{3,2,1,0:T(8,128)(2,1)} %copy-done.12, ...), custom_call_target="tpu_custom_call" | custom-call | tf_op jit(solution)/shard_map/middle/pallas_call | solution.py:552
  473.9 56.0 %back_top.1 = (bf16[512,1536]{1,0:T(8,128)(2,1)}, bf16[512,2048]{1,0:T(8,128)(2,1)}, bf16[512,2048]{1,0:T(8,128)(2,1)}, f32[512,1536]{1,0:T(8,128)}, bf16[512,15...) custom-call(bf16[512,1536]{1,0:T(8,128)(2,1)} %pad_maximum_fusion.5.refs_0_, ...), custom_call_target="tpu_custom_call" | custom-call | tf_op jit(solution)/shard_map/back_top/pallas_call | solution.py:552
  530.0 3.7 convolution_convert_fusion.15
  551.5 77.8 %attend_back.2.refs_0_ = bf16[4,5,2,256,128]{4,3,2,1,0:T(8,128)(2,1)S(1)} custom-call(s32[8]{0:T(128)S(1)} %fusion.28.place_ref, s32[8]{0:T(128)S(1)} %select_n.299.blk_ref, s32[6]{0:T(128)S(1)} %bitcast.115, bf16[5,8,256,128]{3,2,1,0:T(8,128)(2,1)S(1)} %copy-done.5, f32[3,1,2048]{2,1,0:T(1,128)S(1)} %get-tuple-element.197.lse_ref, ...), custom_call_target="tpu_custom_call" | custom-call | tf_op jit(solution)/shard_map/attend_back/pallas_call | solution.py:480
  652.7 3.6 convolution_convert_fusion.4
  656.3 79.4 %back.1 = (bf16[512,2432]{1,0:T(8,128)(2,1)}, f32[8,128]{1,0:T(8,128)}, bf16[512,1536]{1,0:T(8,128)(2,1)}, bf16[512,2048]{1,0:T(8,128)(2,1)}, bf16[512,2048]{1,0...) custom-call(bf16[4,5,2,256,128]{4,3,2,1,0:T(8,128)(2,1)} %copy-done., ...), custom_call_target="tpu_custom_call" | custom-call | tf_op jit(solution)/shard_map/back/pallas_call | solution.py:552
  735.8 5.4 convolution_convert_fusion.10
  748.2 7.6 all-reduce.5.cloned.1.call-done
  756.0 5.5 convolution_convert_fusion.6
  788.7 4.1 convolution_convert_fusion.2
  798.6 77.4 %attend_back.3.refs_0_ = bf16[4,5,2,256,128]{4,3,2,1,0:T(8,128)(2,1)S(1)} custom-call(s32[8]{0:T(128)S(1)} %fusion.28.place_ref, s32[8]{0:T(128)S(1)} %select_n.299.blk_ref, s32[6]{0:T(128)S(1)} %bitcast.116, bf16[5,8,256,128]{3,2,1,0:T(8,128)(2,1)S(1)} %get-tuple-element.176.kept_ref, f32[3,1,2048]{2,1,0:T(1,128)S(1)} %get-tuple-element.177.lse_ref, ...), custom_call_target="tpu_custom_call" | custom-call | tf_op jit(solution)/shard_map/attend_back/pallas_call | solution.py:480
  880.4 10.9 back_end.1
  910.8 4.8 add_convert_fusion.1.refs_6_
  918.6 268.0 %tail.1 = (bf16[2048,384]{1,0:T(8,128)(2,1)}, bf16[384,2048]{1,0:T(8,128)(2,1)}, bf16[384,2048]{1,0:T(8,128)(2,1)}, bf16[768,384]{1,0:T(8,128)(2,1)}, bf16[384,2...) custom-call(bf16[2048,384]{1,0:T(8,128)(2,1)} %get-tuple-element.342.refs_0_,, ...), custom_call_target="tpu_custom_call" | custom-call | tf_op jit(solution)/shard_map/tail/pallas_call | solution.py:1145
  1197.9 11.5 small_sum.1
  1211.6 3.6 multiply_add_fusion
  1228.7 5.1 maximum_convert_fusion
  (405 shorter events, 194.0 us)
Async XLA Ops:
  7.2 748.7 %all-reduce.5.cloned.1.call-start = ((), (), s32[]{:S(2)}) async-start(), calls=%async_computation | async-start | bytes 6291456 | tf_op jit(solution)/shard_map/psum | solution.py:1739
  24.3 49.6 %collective-permute-start = (bf16[256,768]{1,0:T(8,128)(2,1)}, bf16[256,768]{1,0:T(8,128)(2,1)S(1)}, u32[]{:S(2)}, u32[]{:S(2)}) collective-permute-start(bf16[256,768]{1,0:T(8,128)(2,1)} %get-tuple-element.386), channel_id=1, source_target_pairs={{0,2},{2,0},{4,6},{6,4},{1,3},{3,1},{5,7},{7,5},{8,10},{10,8},{12,... | collective-permute-start | bytes 1179656 | tf_op jit(solution)/shard_map/ppermute | solution.py:1230
  27.3 46.6 %collective-permute-start.1 = (bf16[256,768]{1,0:T(8,128)(2,1)}, bf16[256,768]{1,0:T(8,128)(2,1)}, u32[]{:S(2)}, u32[]{:S(2)}) collective-permute-start(bf16[256,768]{1,0:T(8,128)(2,1)} %get-tuple-element.385), channel_id=1, source_target_pairs={{0,4},{2,6},{4,0},{6,2},{1,5},{3,7},{5,1},{7,3},{8,12},{10,14},{12... | collective-permute-start | bytes 1179656 | tf_op jit(solution)/shard_map/ppermute | solution.py:1230
  29.9 44.0 %collective-permute-start.2 = (bf16[256,768]{1,0:T(8,128)(2,1)}, bf16[256,768]{1,0:T(8,128)(2,1)}, u32[]{:S(2)}, u32[]{:S(2)}) collective-permute-start(bf16[256,768]{1,0:T(8,128)(2,1)} %get-tuple-element.384), channel_id=1, source_target_pairs={{0,6},{2,4},{4,2},{6,0},{1,7},{3,5},{5,3},{7,1},{8,14},{10,12},{12... | collective-permute-start | bytes 1179656 | tf_op jit(solution)/shard_map/ppermute | solution.py:1230
  29.9 44.0 %collective-permute-start.3 = (bf16[3,384,768]{2,1,0:T(8,128)(2,1)S(1)}, bf16[3,384,768]{2,1,0:T(8,128)(2,1)}, u32[]{:S(2)}, u32[]{:S(2)}) collective-permute-start(bf16[3,384,768]{2,1,0:T(8,128)(2,1)S(1)} %copy-done.17), channel_id=1, source_target_pairs={{0,16},{8,24},{16,0},{24,8},{1,17},{9,25},{17,1},{25,9},{2,18},{10... | collective-permute-start | bytes 5308424 | tf_op jit(solution)/shard_map/ppermute | solution.py:1230
  32.6 41.3 %collective-permute-start.4 = (bf16[384,256]{1,0:T(8,128)(2,1)S(1)}, bf16[384,256]{1,0:T(8,128)(2,1)S(1)}, u32[]{:S(2)}, u32[]{:S(2)}) collective-permute-start(bf16[384,256]{1,0:T(8,128)(2,1)S(1)} %concatenate.79.refs_6_), channel_id=1, source_target_pairs={{0,16},{8,24},{16,0},{24,8},{1,17},{9,25},{17,1},{25,9},{2,18},{10... | collective-permute-start | bytes 589832 | tf_op jit(solution)/shard_map/ppermute | solution.py:1230
  73.9 115.1 %collective-permute-start.10 = (bf16[2,384,2048]{2,1,0:T(8,128)(2,1)}, bf16[2,384,2048]{2,1,0:T(8,128)(2,1)}, u32[]{:S(2)}, u32[]{:S(2)}) collective-permute-start(bf16[2,384,2048]{2,1,0:T(8,128)(2,1)} %get-tuple-element.184.refs_6_.refs_21_), channel_id=1, source_target_pairs={{0,16},{8,24},{16,0},{24,8},{1,17},{9,25},{17,1},{25,9},{2,18},{10... | collective-permute-start | bytes 9437192 | tf_op jit(solution)/shard_map/ppermute | solution.py:1230
  75.5 113.5 %collective-permute-start.9 = (bf16[2816,384]{1,0:T(8,128)(2,1)}, bf16[2816,384]{1,0:T(8,128)(2,1)}, u32[]{:S(2)}, u32[]{:S(2)}) collective-permute-start(bf16[2816,384]{1,0:T(8,128)(2,1)} %get-tuple-element.183.refs_3_.refs_17_), channel_id=1, source_target_pairs={{0,16},{8,24},{16,0},{24,8},{1,17},{9,25},{17,1},{25,9},{2,18},{10... | collective-permute-start | bytes 6488072 | tf_op jit(solution)/shard_map/ppermute | solution.py:1230
  79.8 111.3 %collective-permute-start.12 = (bf16[2,384,2048]{2,1,0:T(8,128)(2,1)}, bf16[2,384,2048]{2,1,0:T(8,128)(2,1)}, u32[]{:S(2)}, u32[]{:S(2)}) collective-permute-start(bf16[2,384,2048]{2,1,0:T(8,128)(2,1)} %get-tuple-element.184.refs_6_.refs_21_), channel_id=1, source_target_pairs={{0,8},{8,0},{16,24},{24,16},{1,9},{9,1},{17,25},{25,17},{2,10},{10... | collective-permute-start | bytes 9437192 | tf_op jit(solution)/shard_map/ppermute | solution.py:1230
  86.4 104.6 %collective-permute-start.11 = (bf16[2816,384]{1,0:T(8,128)(2,1)}, bf16[2816,384]{1,0:T(8,128)(2,1)}, u32[]{:S(2)}, u32[]{:S(2)}) collective-permute-start(bf16[2816,384]{1,0:T(8,128)(2,1)} %get-tuple-element.183.refs_3_.refs_17_), channel_id=1, source_target_pairs={{0,8},{8,0},{16,24},{24,16},{1,9},{9,1},{17,25},{25,17},{2,10},{10... | collective-permute-start | bytes 6488072 | tf_op jit(solution)/shard_map/ppermute | solution.py:1230
  189.0 85.1 %collective-permute-start.14 = (bf16[2816,384]{1,0:T(8,128)(2,1)}, bf16[2816,384]{1,0:T(8,128)(2,1)}, u32[]{:S(2)}, u32[]{:S(2)}) collective-permute-start(bf16[2816,384]{1,0:T(8,128)(2,1)} %get-tuple-element.190.refs_3_.refs_5_), channel_id=1, source_target_pairs={{0,16},{8,24},{16,0},{24,8},{1,17},{9,25},{17,1},{25,9},{2,18},{10... | collective-permute-start | bytes 6488072 | tf_op jit(solution)/shard_map/ppermute | solution.py:1230
  190.3 83.8 %collective-permute-start.13 = (bf16[3,384,768]{2,1,0:T(8,128)(2,1)}, bf16[3,384,768]{2,1,0:T(8,128)(2,1)}, u32[]{:S(2)}, u32[]{:S(2)}) collective-permute-start(bf16[3,384,768]{2,1,0:T(8,128)(2,1)} %get-tuple-element.191.refs_2_), channel_id=1, source_target_pairs={{0,16},{8,24},{16,0},{24,8},{1,17},{9,25},{17,1},{25,9},{2,18},{10... | collective-permute-start | bytes 5308424 | tf_op jit(solution)/shard_map/ppermute | solution.py:1230
  274.1 104.2 %collective-permute-start.18 = (bf16[2,384,2048]{2,1,0:T(8,128)(2,1)}, bf16[2,384,2048]{2,1,0:T(8,128)(2,1)}, u32[]{:S(2)}, u32[]{:S(2)}) collective-permute-start(bf16[2,384,2048]{2,1,0:T(8,128)(2,1)} %get-tuple-element.204.refs_6_.refs_9_), channel_id=1, source_target_pairs={{0,16},{8,24},{16,0},{24,8},{1,17},{9,25},{17,1},{25,9},{2,18},{10... | collective-permute-start | bytes 9437192 | tf_op jit(solution)/shard_map/ppermute | solution.py:1230
  275.9 102.4 %collective-permute-start.17 = (bf16[512,768]{1,0:T(8,128)(2,1)S(1)}, bf16[512,768]{1,0:T(8,128)(2,1)}, u32[]{:S(2)}, u32[]{:S(2)}) collective-permute-start(bf16[512,768]{1,0:T(8,128)(2,1)S(1)} %pad_maximum_fusion.6), channel_id=1, source_target_pairs={{0,1},{1,0},{2,3},{3,2},{4,5},{5,4},{6,7},{7,6},{8,9},{9,8},{10,11... | collective-permute-start | bytes 2359304 | tf_op jit(solution)/shard_map/ppermute | solution.py:1230
  277.5 110.0 %collective-permute-start.20 = (bf16[2,384,2048]{2,1,0:T(8,128)(2,1)}, bf16[2,384,2048]{2,1,0:T(8,128)(2,1)}, u32[]{:S(2)}, u32[]{:S(2)}) collective-permute-start(bf16[2,384,2048]{2,1,0:T(8,128)(2,1)} %get-tuple-element.204.refs_6_.refs_9_), channel_id=1, source_target_pairs={{0,8},{8,0},{16,24},{24,16},{1,9},{9,1},{17,25},{25,17},{2,10},{10... | collective-permute-start | bytes 9437192 | tf_op jit(solution)/shard_map/ppermute | solution.py:1230
  378.3 95.6 %collective-permute-start.22 = (bf16[2,384,2048]{2,1,0:T(8,128)(2,1)}, bf16[2,384,2048]{2,1,0:T(8,128)(2,1)}, u32[]{:S(2)}, u32[]{:S(2)}) collective-permute-start(bf16[2,384,2048]{2,1,0:T(8,128)(2,1)} %collective-permute-done.18.refs_7_.refs_10_), channel_id=1, source_target_pairs={{0,8},{8,0},{16,24},{24,16},{1,9},{9,1},{17,25},{25,17},{2,10},{10... | collective-permute-start | bytes 9437192 | tf_op jit(solution)/shard_map/ppermute | solution.py:1230
  378.9 95.1 %collective-permute-start.21 = (bf16[2816,384]{1,0:T(8,128)(2,1)}, bf16[2816,384]{1,0:T(8,128)(2,1)}, u32[]{:S(2)}, u32[]{:S(2)}) collective-permute-start(bf16[2816,384]{1,0:T(8,128)(2,1)} %collective-permute-done.14.refs_4_.refs_6_), channel_id=1, source_target_pairs={{0,8},{8,0},{16,24},{24,16},{1,9},{9,1},{17,25},{25,17},{2,10},{10... | collective-permute-start | bytes 6488072 | tf_op jit(solution)/shard_map/ppermute | solution.py:1230
  467.6 62.3 %collective-permute-start.23 = (bf16[256,768]{1,0:T(8,128)(2,1)}, bf16[256,768]{1,0:T(8,128)(2,1)}, u32[]{:S(2)}, u32[]{:S(2)}) collective-permute-start(bf16[256,768]{1,0:T(8,128)(2,1)} %get-tuple-element.382), channel_id=1, source_target_pairs={{0,2},{2,0},{4,6},{6,4},{1,3},{3,1},{5,7},{7,5},{8,10},{10,8},{12,... | collective-permute-start | bytes 1179656 | tf_op jit(solution)/shard_map/ppermute | solution.py:1230
  467.6 62.3 %collective-permute-start.24 = (bf16[256,768]{1,0:T(8,128)(2,1)}, bf16[256,768]{1,0:T(8,128)(2,1)}, u32[]{:S(2)}, u32[]{:S(2)}) collective-permute-start(bf16[256,768]{1,0:T(8,128)(2,1)} %get-tuple-element.381), channel_id=1, source_target_pairs={{0,4},{2,6},{4,0},{6,2},{1,5},{3,7},{5,1},{7,3},{8,12},{10,14},{12... | collective-permute-start | bytes 1179656 | tf_op jit(solution)/shard_map/ppermute | solution.py:1230
  470.6 59.3 %collective-permute-start.25 = (bf16[256,768]{1,0:T(8,128)(2,1)}, bf16[256,768]{1,0:T(8,128)(2,1)}, u32[]{:S(2)}, u32[]{:S(2)}) collective-permute-start(bf16[256,768]{1,0:T(8,128)(2,1)} %get-tuple-element.380), channel_id=1, source_target_pairs={{0,6},{2,4},{4,2},{6,0},{1,7},{3,5},{5,3},{7,1},{8,14},{10,12},{12... | collective-permute-start | bytes 1179656 | tf_op jit(solution)/shard_map/ppermute | solution.py:1230
  539.8 89.6 %collective-permute-start.30 = (bf16[768,2048]{1,0:T(8,128)(2,1)}, bf16[768,2048]{1,0:T(8,128)(2,1)S(1)}, u32[]{:S(2)}, u32[]{:S(2)}) collective-permute-start(bf16[768,2048]{1,0:T(8,128)(2,1)} %convolution_convert_fusion.11), channel_id=1, source_target_pairs={{0,8},{8,0},{16,24},{24,16},{1,9},{9,1},{17,25},{25,17},{2,10},{10... | collective-permute-start | bytes 9437192 | tf_op jit(solution)/shard_map/ppermute | solution.py:1230
  545.3 84.1 %collective-permute-start.28 = (bf16[2048,384]{1,0:T(8,128)(2,1)S(1)}, bf16[2048,384]{1,0:T(8,128)(2,1)S(1)}, u32[]{:S(2)}, u32[]{:S(2)}) collective-permute-start(bf16[2048,384]{1,0:T(8,128)(2,1)S(1)} %slice.273), channel_id=1, source_target_pairs={{0,16},{8,24},{16,0},{24,8},{1,17},{9,25},{17,1},{25,9},{2,18},{10... | collective-permute-start | bytes 4718600 | tf_op jit(solution)/shard_map/ppermute | solution.py:1230
  547.6 81.9 %collective-permute-start.29 = (bf16[384,2048]{1,0:T(8,128)(2,1)S(1)}, bf16[384,2048]{1,0:T(8,128)(2,1)}, u32[]{:S(2)}, u32[]{:S(2)}) collective-permute-start(bf16[384,2048]{1,0:T(8,128)(2,1)S(1)} %slice.274), channel_id=1, source_target_pairs={{0,16},{8,24},{16,0},{24,8},{1,17},{9,25},{17,1},{25,9},{2,18},{10... | collective-permute-start | bytes 4718600 | tf_op jit(solution)/shard_map/ppermute | solution.py:1230
  551.0 78.4 %collective-permute-start.31 = (bf16[768,768]{1,0:T(8,128)(2,1)}, bf16[768,768]{1,0:T(8,128)(2,1)}, u32[]{:S(2)}, u32[]{:S(2)}) collective-permute-start(bf16[768,768]{1,0:T(8,128)(2,1)} %convolution_convert_fusion.19), channel_id=1, source_target_pairs={{0,8},{8,0},{16,24},{24,16},{1,9},{9,1},{17,25},{25,17},{2,10},{10... | collective-permute-start | bytes 3538952 | tf_op jit(solution)/shard_map/ppermute | solution.py:1230
  551.0 105.4 %collective-permute-start.33 = (bf16[2,384,2048]{2,1,0:T(8,128)(2,1)}, bf16[2,384,2048]{2,1,0:T(8,128)(2,1)}, u32[]{:S(2)}, u32[]{:S(2)}) collective-permute-start(bf16[2,384,2048]{2,1,0:T(8,128)(2,1)} %collective-permute-done.10.refs_7_.refs_22_), channel_id=1, source_target_pairs={{0,8},{8,0},{16,24},{24,16},{1,9},{9,1},{17,25},{25,17},{2,10},{10... | collective-permute-start | bytes 9437192 | tf_op jit(solution)/shard_map/ppermute | solution.py:1230
  761.5 116.1 %collective-permute-start.38 = (bf16[768,2048]{1,0:T(8,128)(2,1)}, bf16[768,2048]{1,0:T(8,128)(2,1)S(1)}, u32[]{:S(2)}, u32[]{:S(2)}) collective-permute-start(bf16[768,2048]{1,0:T(8,128)(2,1)} %convolution_convert_fusion.6), channel_id=1, source_target_pairs={{0,8},{8,0},{16,24},{24,16},{1,9},{9,1},{17,25},{25,17},{2,10},{10... | collective-permute-start | bytes 9437192 | tf_op jit(solution)/shard_map/ppermute | solution.py:1230
  766.3 111.3 %collective-permute-start.40 = (bf16[768,2432]{1,0:T(8,128)(2,1)S(1)}, bf16[768,2432]{1,0:T(8,128)(2,1)}, u32[]{:S(2)}, u32[]{:S(2)}) collective-permute-start(bf16[768,2432]{1,0:T(8,128)(2,1)S(1)} %convolution_convert_fusion.3), channel_id=1, source_target_pairs={{0,8},{8,0},{16,24},{24,16},{1,9},{9,1},{17,25},{25,17},{2,10},{10... | collective-permute-start | bytes 11206664 | tf_op jit(solution)/shard_map/ppermute | solution.py:1230
  782.0 95.5 %collective-permute-start.36 = (bf16[2048,384]{1,0:T(8,128)(2,1)S(1)}, bf16[2048,384]{1,0:T(8,128)(2,1)S(1)}, u32[]{:S(2)}, u32[]{:S(2)}) collective-permute-start(bf16[2048,384]{1,0:T(8,128)(2,1)S(1)} %get-tuple-element.343), channel_id=1, source_target_pairs={{0,16},{8,24},{16,0},{24,8},{1,17},{9,25},{17,1},{25,9},{2,18},{10... | collective-permute-start | bytes 4718600 | tf_op jit(solution)/shard_map/ppermute | solution.py:1230
  786.5 91.0 %collective-permute-start.37 = (bf16[384,2048]{1,0:T(8,128)(2,1)S(1)}, bf16[384,2048]{1,0:T(8,128)(2,1)S(1)}, u32[]{:S(2)}, u32[]{:S(2)}) collective-permute-start(bf16[384,2048]{1,0:T(8,128)(2,1)S(1)} %get-tuple-element.341), channel_id=1, source_target_pairs={{0,16},{8,24},{16,0},{24,8},{1,17},{9,25},{17,1},{25,9},{2,18},{10... | collective-permute-start | bytes 4718600 | tf_op jit(solution)/shard_map/ppermute | solution.py:1230
  792.8 84.8 %collective-permute-start.41 = (bf16[512,768]{1,0:T(8,128)(2,1)S(1)}, bf16[512,768]{1,0:T(8,128)(2,1)S(1)}, u32[]{:S(2)}, u32[]{:S(2)}) collective-permute-start(bf16[512,768]{1,0:T(8,128)(2,1)S(1)} %pad_maximum_fusion.7), channel_id=1, source_target_pairs={{0,1},{1,0},{2,3},{3,2},{4,5},{5,4},{6,7},{7,6},{8,9},{9,8},{10,11... | collective-permute-start | bytes 2359304 | tf_op jit(solution)/shard_map/ppermute | solution.py:1230
  893.8 292.8 %collective-permute-start.42 = (bf16[256,1536]{1,0:T(8,128)(2,1)S(1)}, bf16[256,1536]{1,0:T(8,128)(2,1)}, u32[]{:S(2)}, u32[]{:S(2)}) collective-permute-start(bf16[256,1536]{1,0:T(8,128)(2,1)S(1)} %get-tuple-element.286), channel_id=1, source_target_pairs={{0,1},{1,0},{2,3},{3,2},{4,5},{5,4},{6,7},{7,6},{8,9},{9,8},{10,11... | collective-permute-start | bytes 2359304 | tf_op jit(solution)/shard_map/ppermute | solution.py:1230
  894.4 292.2 %collective-permute-start.43 = (bf16[256,1536]{1,0:T(8,128)(2,1)}, bf16[256,1536]{1,0:T(8,128)(2,1)}, u32[]{:S(2)}, u32[]{:S(2)}) collective-permute-start(bf16[256,1536]{1,0:T(8,128)(2,1)} %get-tuple-element.288), channel_id=1, source_target_pairs={{0,1},{1,0},{2,3},{3,2},{4,5},{5,4},{6,7},{7,6},{8,9},{9,8},{10,11... | collective-permute-start | bytes 2359304 | tf_op jit(solution)/shard_map/ppermute | solution.py:1230
  (112 other events, 850.8 us)
Sparse Core Ops, SparseCore 0:
  635.7 120.1 all-reduce.4

commit v5 on v4

--- a/solution.py
+++ b/solution.py
@@ -717,18 +717,20 @@
 
 
 def load_projections(copies, r, width, layer):
-    out = []
+    last = [item.at[:, pl.ds(128 * layer, 128)] for item in r.pieces("w_last")]
+    out = copies.load_down(last, r.w_mix, (3 * width, 128))
     for j in range(3):
         out += copies.load_down([item.at[j] for item in r.pieces("w_qkv")], r.w_mix, (j * width, width))
-    last = [item.at[:, pl.ds(128 * layer, 128)] for item in r.pieces("w_last")]
-    return out + copies.load_down(last, r.w_mix, (3 * width, 128))
+    return out
 
 
 def first_kernel(pack, count, width, layer, r):
     copies = Copies(r.sems)
     c = lax.axis_index("ctx")
     block_rows = r.packed.shape[3]
-    for copy in load_projections(copies, r, width, layer):
+    loads = load_projections(copies, r, width, layer)
+    last_count = len(r.pieces("w_last"))
+    for copy in loads[:last_count]:
         copy.wait()
     turned = r.w_mix[:, 3 * width :].astype(F32).T
     first = count * pack.hp
@@ -740,6 +742,9 @@
         r.normed[rows, :] = normed
         add = column_sums(residual * residual)
         r.stat[...] = jnp.broadcast_to(add if half == 0 else add + r.stat[0:1, :], r.stat.shape)
+        if half == 0:
+            for copy in loads[last_count:]:
+                copy.wait()
         project_rows(pack, r, count, width, half, rows, normed)
 
 
@@ -1093,7 +1098,7 @@
 
     @pl.when(is_middle)
     def _():
-        lag = 2
+        lag = 4
         for index in range(total + lag):
             if index < total:
                 unit, rows = rows_of(index)

time: 1250 us -> 1260 us (level)
  transfers between devices with their start and end apart: 46 -> 46, of which waited for: 10 -> 10; matrix products, arithmetic and copies ran while one was open for 12% -> 11% of each run, Pallas kernels for 72% -> 72%
where the time goes in v5:
time: 1260 us; the launch traced here: 1250 us
  Pallas kernels  928 us (74%)
  local copies, waits for them, and re-layouts  80.2 us (6%)
  other arithmetic  74.9 us (6%)
  matrix products  59.3 us (5%)
  waiting for transfers between devices  43.6 us (3%)
  between operations  36.6 us (3%)
  starting transfers between devices  32 us (3%)
    pallas_call x7, Pallas kernels, named_call(): pl.pallas_call(body, out_shape=[jax.ShapeDtypeStruct(shape, kind) for sha...  325 us
    pallas_call x1, Pallas kernels, tail(): pl.pallas_call(functools.partial(tail_kernel, tuple(chunks), ready, halve...  278 us
    pallas_call x2, Pallas kernels, attend(): pl.pallas_call(functools.partial(attend_kernel, pack), out_shape=[jax.Sha...  158 us
    pallas_call x2, Pallas kernels, attend_back(): pl.pallas_call(functools.partial(attend_back_kernel, pack), out_shape=jax...  155 us
    dot_general x20, matrix products, weight_grad(): lax.dot_general(left, right, (((0,), (0,)), ((), ())), preferred_element_...  59.3 us
    ppermute x45, waiting for transfers between devices, swap(): return lax.ppermute(values, axis, [(i, i ^ step) for i in range(size)])  36 us
    ppermute x45, starting transfers between devices, swap(): return lax.ppermute(values, axis, [(i, i ^ step) for i in range(size)])  32 us
    convert_element_type x12, other arithmetic, add_low(): return (left.astype(F32) + right.astype(F32)).astype(BF16)  28.1 us
  transfers between devices with their start and end apart: 46, of which 10 were waited for; matrix products, arithmetic and copies ran while one was open for 11% of the time, Pallas kernels for 72%

profile of v5, /device:TPU:0, one launch (start us, length us, event | category | flops | bytes accessed | tf_op | source)
XLA Modules:
  0.0 1254.4 jit_solution(8678807563673282315)
XLA Ops:
  16.6 4.0 slice_bitcast_fusion.2
  33.0 3.9 slice_bitcast_fusion.4
  37.9 4.5 pad_maximum_fusion.3
  42.4 6.8 slice_bitcast_fusion
  62.2 3.7 pad_maximum_fusion.refs_0_.refs_1_
  65.9 8.0 collective-permute-done.4.refs_7_
  82.7 3.7 collective-permute-done.8.refs_9_
  87.1 11.9 project.2
  100.7 79.2 %attend.2 = (bf16[4,3,256,128]{3,2,1,0:T(8,128)(2,1)S(1)}, bf16[5,8,256,128]{3,2,1,0:T(8,128)(2,1)S(1)}, f32[3,1,2048]{2,1,0:T(1,128)S(1)}, f32[3,64,2048]{2,1,0:T(8,128)S(1)}) custom-call(s32[8]{0:T(128)S(1)} %fusion.28.place_ref, s32[8]{0:T(128)S(1)} %select_n.299.blk_ref, s32[6]{0:T(128)S(1)} %bitcast.113, bf16[4,5,2,256,128]{4,3,2,1,0:T(8,128)(2,1)S(1)} %copy-done.6), custom_call_target="tpu_custom_call" | custom-call | tf_op jit(solution)/shard_map/attend/pallas_call | solution.py:445
  182.0 7.1 collective-permute-done.9.refs_4_.refs_18_
  191.1 77.3 %middle.2 = (bf16[512,768]{1,0:T(8,128)(2,1)}, f32[512,1536]{1,0:T(8,128)}, bf16[512,1536]{1,0:T(8,128)(2,1)}, bf16[512,2048]{1,0:T(8,128)(2,1)}, bf16[512,2048]...) custom-call(bf16[4,3,256,128]{3,2,1,0:T(8,128)(2,1)} %copy-done.13, ...), custom_call_target="tpu_custom_call" | custom-call | tf_op jit(solution)/shard_map/middle/pallas_call | solution.py:552
  268.4 5.7 collective-permute-done.13.refs_3_
  282.0 11.9 project.3
  295.6 78.9 %attend.3 = (bf16[4,3,256,128]{3,2,1,0:T(8,128)(2,1)S(1)}, bf16[5,8,256,128]{3,2,1,0:T(8,128)(2,1)S(1)}, f32[3,1,2048]{2,1,0:T(1,128)S(1)}, f32[3,64,2048]{2,1,0:T(8,128)S(1)}) custom-call(s32[8]{0:T(128)S(1)} %fusion.28.place_ref, s32[8]{0:T(128)S(1)} %select_n.299.blk_ref, s32[6]{0:T(128)S(1)} %bitcast.114, bf16[4,5,2,256,128]{4,3,2,1,0:T(8,128)(2,1)S(1)} %copy-done.7), custom_call_target="tpu_custom_call" | custom-call | tf_op jit(solution)/shard_map/attend/pallas_call | solution.py:445
  382.1 5.1 collective-permute-done.19.refs_5_.refs_7_
  387.2 77.4 %middle.3 = (bf16[512,768]{1,0:T(8,128)(2,1)}, f32[512,1536]{1,0:T(8,128)}, bf16[512,1536]{1,0:T(8,128)(2,1)}, bf16[512,2048]{1,0:T(8,128)(2,1)}, bf16[512,2048]...) custom-call(bf16[4,3,256,128]{3,2,1,0:T(8,128)(2,1)} %copy-done.12, ...), custom_call_target="tpu_custom_call" | custom-call | tf_op jit(solution)/shard_map/middle/pallas_call | solution.py:552
  473.7 56.0 %back_top.1 = (bf16[512,1536]{1,0:T(8,128)(2,1)}, bf16[512,2048]{1,0:T(8,128)(2,1)}, bf16[512,2048]{1,0:T(8,128)(2,1)}, f32[512,1536]{1,0:T(8,128)}, bf16[512,15...) custom-call(bf16[512,1536]{1,0:T(8,128)(2,1)} %pad_maximum_fusion.5.refs_0_, ...), custom_call_target="tpu_custom_call" | custom-call | tf_op jit(solution)/shard_map/back_top/pallas_call | solution.py:552
  529.8 3.7 convolution_convert_fusion.15
  551.3 77.8 %attend_back.2.refs_0_ = bf16[4,5,2,256,128]{4,3,2,1,0:T(8,128)(2,1)S(1)} custom-call(s32[8]{0:T(128)S(1)} %fusion.28.place_ref, s32[8]{0:T(128)S(1)} %select_n.299.blk_ref, s32[6]{0:T(128)S(1)} %bitcast.115, bf16[5,8,256,128]{3,2,1,0:T(8,128)(2,1)S(1)} %copy-done.5, f32[3,1,2048]{2,1,0:T(1,128)S(1)} %get-tuple-element.197.lse_ref, ...), custom_call_target="tpu_custom_call" | custom-call | tf_op jit(solution)/shard_map/attend_back/pallas_call | solution.py:480
  652.5 3.6 convolution_convert_fusion.4
  656.1 79.6 %back.1 = (bf16[512,2432]{1,0:T(8,128)(2,1)}, f32[8,128]{1,0:T(8,128)}, bf16[512,1536]{1,0:T(8,128)(2,1)}, bf16[512,2048]{1,0:T(8,128)(2,1)}, bf16[512,2048]{1,0...) custom-call(bf16[4,5,2,256,128]{4,3,2,1,0:T(8,128)(2,1)} %copy-done., ...), custom_call_target="tpu_custom_call" | custom-call | tf_op jit(solution)/shard_map/back/pallas_call | solution.py:552
  735.7 5.4 convolution_convert_fusion.10
  748.1 7.5 all-reduce.5.cloned.1.call-done
  755.8 5.5 convolution_convert_fusion.6
  788.4 4.1 convolution_convert_fusion.2
  798.4 77.4 %attend_back.3.refs_0_ = bf16[4,5,2,256,128]{4,3,2,1,0:T(8,128)(2,1)S(1)} custom-call(s32[8]{0:T(128)S(1)} %fusion.28.place_ref, s32[8]{0:T(128)S(1)} %select_n.299.blk_ref, s32[6]{0:T(128)S(1)} %bitcast.116, bf16[5,8,256,128]{3,2,1,0:T(8,128)(2,1)S(1)} %get-tuple-element.176.kept_ref, f32[3,1,2048]{2,1,0:T(1,128)S(1)} %get-tuple-element.177.lse_ref, ...), custom_call_target="tpu_custom_call" | custom-call | tf_op jit(solution)/shard_map/attend_back/pallas_call | solution.py:480
  880.2 11.0 back_end.1
  910.7 4.8 add_convert_fusion.1.refs_6_
  918.5 278.0 %tail.1 = (bf16[2048,384]{1,0:T(8,128)(2,1)}, bf16[384,2048]{1,0:T(8,128)(2,1)}, bf16[384,2048]{1,0:T(8,128)(2,1)}, bf16[768,384]{1,0:T(8,128)(2,1)}, bf16[384,2...) custom-call(bf16[2048,384]{1,0:T(8,128)(2,1)} %get-tuple-element.342.refs_0_,, ...), custom_call_target="tpu_custom_call" | custom-call | tf_op jit(solution)/shard_map/tail/pallas_call | solution.py:1150
  1207.8 11.5 small_sum.1
  1221.5 3.6 multiply_add_fusion
  1238.5 5.1 maximum_convert_fusion
  (405 shorter events, 194.0 us)
Async XLA Ops:
  7.2 748.5 %all-reduce.5.cloned.1.call-start = ((), (), s32[]{:S(2)}) async-start(), calls=%async_computation | async-start | bytes 6291456 | tf_op jit(solution)/shard_map/psum | solution.py:1744
  24.3 49.6 %collective-permute-start = (bf16[256,768]{1,0:T(8,128)(2,1)}, bf16[256,768]{1,0:T(8,128)(2,1)S(1)}, u32[]{:S(2)}, u32[]{:S(2)}) collective-permute-start(bf16[256,768]{1,0:T(8,128)(2,1)} %get-tuple-element.386), channel_id=1, source_target_pairs={{0,2},{2,0},{4,6},{6,4},{1,3},{3,1},{5,7},{7,5},{8,10},{10,8},{12,... | collective-permute-start | bytes 1179656 | tf_op jit(solution)/shard_map/ppermute | solution.py:1235
  27.3 46.6 %collective-permute-start.1 = (bf16[256,768]{1,0:T(8,128)(2,1)}, bf16[256,768]{1,0:T(8,128)(2,1)}, u32[]{:S(2)}, u32[]{:S(2)}) collective-permute-start(bf16[256,768]{1,0:T(8,128)(2,1)} %get-tuple-element.385), channel_id=1, source_target_pairs={{0,4},{2,6},{4,0},{6,2},{1,5},{3,7},{5,1},{7,3},{8,12},{10,14},{12... | collective-permute-start | bytes 1179656 | tf_op jit(solution)/shard_map/ppermute | solution.py:1235
  29.9 44.0 %collective-permute-start.2 = (bf16[256,768]{1,0:T(8,128)(2,1)}, bf16[256,768]{1,0:T(8,128)(2,1)}, u32[]{:S(2)}, u32[]{:S(2)}) collective-permute-start(bf16[256,768]{1,0:T(8,128)(2,1)} %get-tuple-element.384), channel_id=1, source_target_pairs={{0,6},{2,4},{4,2},{6,0},{1,7},{3,5},{5,3},{7,1},{8,14},{10,12},{12... | collective-permute-start | bytes 1179656 | tf_op jit(solution)/shard_map/ppermute | solution.py:1235
  29.9 44.0 %collective-permute-start.3 = (bf16[3,384,768]{2,1,0:T(8,128)(2,1)S(1)}, bf16[3,384,768]{2,1,0:T(8,128)(2,1)}, u32[]{:S(2)}, u32[]{:S(2)}) collective-permute-start(bf16[3,384,768]{2,1,0:T(8,128)(2,1)S(1)} %copy-done.17), channel_id=1, source_target_pairs={{0,16},{8,24},{16,0},{24,8},{1,17},{9,25},{17,1},{25,9},{2,18},{10... | collective-permute-start | bytes 5308424 | tf_op jit(solution)/shard_map/ppermute | solution.py:1235
  32.6 41.3 %collective-permute-start.4 = (bf16[384,256]{1,0:T(8,128)(2,1)S(1)}, bf16[384,256]{1,0:T(8,128)(2,1)S(1)}, u32[]{:S(2)}, u32[]{:S(2)}) collective-permute-start(bf16[384,256]{1,0:T(8,128)(2,1)S(1)} %concatenate.79.refs_6_), channel_id=1, source_target_pairs={{0,16},{8,24},{16,0},{24,8},{1,17},{9,25},{17,1},{25,9},{2,18},{10... | collective-permute-start | bytes 589832 | tf_op jit(solution)/shard_map/ppermute | solution.py:1235
  73.9 115.1 %collective-permute-start.10 = (bf16[2,384,2048]{2,1,0:T(8,128)(2,1)}, bf16[2,384,2048]{2,1,0:T(8,128)(2,1)}, u32[]{:S(2)}, u32[]{:S(2)}) collective-permute-start(bf16[2,384,2048]{2,1,0:T(8,128)(2,1)} %get-tuple-element.184.refs_6_.refs_21_), channel_id=1, source_target_pairs={{0,16},{8,24},{16,0},{24,8},{1,17},{9,25},{17,1},{25,9},{2,18},{10... | collective-permute-start | bytes 9437192 | tf_op jit(solution)/shard_map/ppermute | solution.py:1235
  75.5 113.5 %collective-permute-start.9 = (bf16[2816,384]{1,0:T(8,128)(2,1)}, bf16[2816,384]{1,0:T(8,128)(2,1)}, u32[]{:S(2)}, u32[]{:S(2)}) collective-permute-start(bf16[2816,384]{1,0:T(8,128)(2,1)} %get-tuple-element.183.refs_3_.refs_17_), channel_id=1, source_target_pairs={{0,16},{8,24},{16,0},{24,8},{1,17},{9,25},{17,1},{25,9},{2,18},{10... | collective-permute-start | bytes 6488072 | tf_op jit(solution)/shard_map/ppermute | solution.py:1235
  79.8 111.3 %collective-permute-start.12 = (bf16[2,384,2048]{2,1,0:T(8,128)(2,1)}, bf16[2,384,2048]{2,1,0:T(8,128)(2,1)}, u32[]{:S(2)}, u32[]{:S(2)}) collective-permute-start(bf16[2,384,2048]{2,1,0:T(8,128)(2,1)} %get-tuple-element.184.refs_6_.refs_21_), channel_id=1, source_target_pairs={{0,8},{8,0},{16,24},{24,16},{1,9},{9,1},{17,25},{25,17},{2,10},{10... | collective-permute-start | bytes 9437192 | tf_op jit(solution)/shard_map/ppermute | solution.py:1235
  86.4 104.6 %collective-permute-start.11 = (bf16[2816,384]{1,0:T(8,128)(2,1)}, bf16[2816,384]{1,0:T(8,128)(2,1)}, u32[]{:S(2)}, u32[]{:S(2)}) collective-permute-start(bf16[2816,384]{1,0:T(8,128)(2,1)} %get-tuple-element.183.refs_3_.refs_17_), channel_id=1, source_target_pairs={{0,8},{8,0},{16,24},{24,16},{1,9},{9,1},{17,25},{25,17},{2,10},{10... | collective-permute-start | bytes 6488072 | tf_op jit(solution)/shard_map/ppermute | solution.py:1235
  189.0 85.1 %collective-permute-start.14 = (bf16[2816,384]{1,0:T(8,128)(2,1)}, bf16[2816,384]{1,0:T(8,128)(2,1)}, u32[]{:S(2)}, u32[]{:S(2)}) collective-permute-start(bf16[2816,384]{1,0:T(8,128)(2,1)} %get-tuple-element.190.refs_3_.refs_5_), channel_id=1, source_target_pairs={{0,16},{8,24},{16,0},{24,8},{1,17},{9,25},{17,1},{25,9},{2,18},{10... | collective-permute-start | bytes 6488072 | tf_op jit(solution)/shard_map/ppermute | solution.py:1235
  190.3 83.8 %collective-permute-start.13 = (bf16[3,384,768]{2,1,0:T(8,128)(2,1)}, bf16[3,384,768]{2,1,0:T(8,128)(2,1)}, u32[]{:S(2)}, u32[]{:S(2)}) collective-permute-start(bf16[3,384,768]{2,1,0:T(8,128)(2,1)} %get-tuple-element.191.refs_2_), channel_id=1, source_target_pairs={{0,16},{8,24},{16,0},{24,8},{1,17},{9,25},{17,1},{25,9},{2,18},{10... | collective-permute-start | bytes 5308424 | tf_op jit(solution)/shard_map/ppermute | solution.py:1235
  274.1 104.0 %collective-permute-start.18 = (bf16[2,384,2048]{2,1,0:T(8,128)(2,1)}, bf16[2,384,2048]{2,1,0:T(8,128)(2,1)}, u32[]{:S(2)}, u32[]{:S(2)}) collective-permute-start(bf16[2,384,2048]{2,1,0:T(8,128)(2,1)} %get-tuple-element.204.refs_6_.refs_9_), channel_id=1, source_target_pairs={{0,16},{8,24},{16,0},{24,8},{1,17},{9,25},{17,1},{25,9},{2,18},{10... | collective-permute-start | bytes 9437192 | tf_op jit(solution)/shard_map/ppermute | solution.py:1235
  275.9 102.2 %collective-permute-start.17 = (bf16[512,768]{1,0:T(8,128)(2,1)S(1)}, bf16[512,768]{1,0:T(8,128)(2,1)}, u32[]{:S(2)}, u32[]{:S(2)}) collective-permute-start(bf16[512,768]{1,0:T(8,128)(2,1)S(1)} %pad_maximum_fusion.6), channel_id=1, source_target_pairs={{0,1},{1,0},{2,3},{3,2},{4,5},{5,4},{6,7},{7,6},{8,9},{9,8},{10,11... | collective-permute-start | bytes 2359304 | tf_op jit(solution)/shard_map/ppermute | solution.py:1235
  277.5 109.8 %collective-permute-start.20 = (bf16[2,384,2048]{2,1,0:T(8,128)(2,1)}, bf16[2,384,2048]{2,1,0:T(8,128)(2,1)}, u32[]{:S(2)}, u32[]{:S(2)}) collective-permute-start(bf16[2,384,2048]{2,1,0:T(8,128)(2,1)} %get-tuple-element.204.refs_6_.refs_9_), channel_id=1, source_target_pairs={{0,8},{8,0},{16,24},{24,16},{1,9},{9,1},{17,25},{25,17},{2,10},{10... | collective-permute-start | bytes 9437192 | tf_op jit(solution)/shard_map/ppermute | solution.py:1235
  378.1 95.6 %collective-permute-start.22 = (bf16[2,384,2048]{2,1,0:T(8,128)(2,1)}, bf16[2,384,2048]{2,1,0:T(8,128)(2,1)}, u32[]{:S(2)}, u32[]{:S(2)}) collective-permute-start(bf16[2,384,2048]{2,1,0:T(8,128)(2,1)} %collective-permute-done.18.refs_7_.refs_10_), channel_id=1, source_target_pairs={{0,8},{8,0},{16,24},{24,16},{1,9},{9,1},{17,25},{25,17},{2,10},{10... | collective-permute-start | bytes 9437192 | tf_op jit(solution)/shard_map/ppermute | solution.py:1235
  378.6 95.1 %collective-permute-start.21 = (bf16[2816,384]{1,0:T(8,128)(2,1)}, bf16[2816,384]{1,0:T(8,128)(2,1)}, u32[]{:S(2)}, u32[]{:S(2)}) collective-permute-start(bf16[2816,384]{1,0:T(8,128)(2,1)} %collective-permute-done.14.refs_4_.refs_6_), channel_id=1, source_target_pairs={{0,8},{8,0},{16,24},{24,16},{1,9},{9,1},{17,25},{25,17},{2,10},{10... | collective-permute-start | bytes 6488072 | tf_op jit(solution)/shard_map/ppermute | solution.py:1235
  467.4 62.3 %collective-permute-start.23 = (bf16[256,768]{1,0:T(8,128)(2,1)}, bf16[256,768]{1,0:T(8,128)(2,1)}, u32[]{:S(2)}, u32[]{:S(2)}) collective-permute-start(bf16[256,768]{1,0:T(8,128)(2,1)} %get-tuple-element.382), channel_id=1, source_target_pairs={{0,2},{2,0},{4,6},{6,4},{1,3},{3,1},{5,7},{7,5},{8,10},{10,8},{12,... | collective-permute-start | bytes 1179656 | tf_op jit(solution)/shard_map/ppermute | solution.py:1235
  467.4 62.3 %collective-permute-start.24 = (bf16[256,768]{1,0:T(8,128)(2,1)}, bf16[256,768]{1,0:T(8,128)(2,1)}, u32[]{:S(2)}, u32[]{:S(2)}) collective-permute-start(bf16[256,768]{1,0:T(8,128)(2,1)} %get-tuple-element.381), channel_id=1, source_target_pairs={{0,4},{2,6},{4,0},{6,2},{1,5},{3,7},{5,1},{7,3},{8,12},{10,14},{12... | collective-permute-start | bytes 1179656 | tf_op jit(solution)/shard_map/ppermute | solution.py:1235
  470.4 59.3 %collective-permute-start.25 = (bf16[256,768]{1,0:T(8,128)(2,1)}, bf16[256,768]{1,0:T(8,128)(2,1)}, u32[]{:S(2)}, u32[]{:S(2)}) collective-permute-start(bf16[256,768]{1,0:T(8,128)(2,1)} %get-tuple-element.380), channel_id=1, source_target_pairs={{0,6},{2,4},{4,2},{6,0},{1,7},{3,5},{5,3},{7,1},{8,14},{10,12},{12... | collective-permute-start | bytes 1179656 | tf_op jit(solution)/shard_map/ppermute | solution.py:1235
  539.6 89.6 %collective-permute-start.30 = (bf16[768,2048]{1,0:T(8,128)(2,1)}, bf16[768,2048]{1,0:T(8,128)(2,1)S(1)}, u32[]{:S(2)}, u32[]{:S(2)}) collective-permute-start(bf16[768,2048]{1,0:T(8,128)(2,1)} %convolution_convert_fusion.11), channel_id=1, source_target_pairs={{0,8},{8,0},{16,24},{24,16},{1,9},{9,1},{17,25},{25,17},{2,10},{10... | collective-permute-start | bytes 9437192 | tf_op jit(solution)/shard_map/ppermute | solution.py:1235
  545.1 84.1 %collective-permute-start.28 = (bf16[2048,384]{1,0:T(8,128)(2,1)S(1)}, bf16[2048,384]{1,0:T(8,128)(2,1)S(1)}, u32[]{:S(2)}, u32[]{:S(2)}) collective-permute-start(bf16[2048,384]{1,0:T(8,128)(2,1)S(1)} %slice.273), channel_id=1, source_target_pairs={{0,16},{8,24},{16,0},{24,8},{1,17},{9,25},{17,1},{25,9},{2,18},{10... | collective-permute-start | bytes 4718600 | tf_op jit(solution)/shard_map/ppermute | solution.py:1235
  547.4 81.8 %collective-permute-start.29 = (bf16[384,2048]{1,0:T(8,128)(2,1)S(1)}, bf16[384,2048]{1,0:T(8,128)(2,1)}, u32[]{:S(2)}, u32[]{:S(2)}) collective-permute-start(bf16[384,2048]{1,0:T(8,128)(2,1)S(1)} %slice.274), channel_id=1, source_target_pairs={{0,16},{8,24},{16,0},{24,8},{1,17},{9,25},{17,1},{25,9},{2,18},{10... | collective-permute-start | bytes 4718600 | tf_op jit(solution)/shard_map/ppermute | solution.py:1235
  550.7 78.4 %collective-permute-start.31 = (bf16[768,768]{1,0:T(8,128)(2,1)}, bf16[768,768]{1,0:T(8,128)(2,1)}, u32[]{:S(2)}, u32[]{:S(2)}) collective-permute-start(bf16[768,768]{1,0:T(8,128)(2,1)} %convolution_convert_fusion.19), channel_id=1, source_target_pairs={{0,8},{8,0},{16,24},{24,16},{1,9},{9,1},{17,25},{25,17},{2,10},{10... | collective-permute-start | bytes 3538952 | tf_op jit(solution)/shard_map/ppermute | solution.py:1235
  550.7 105.4 %collective-permute-start.33 = (bf16[2,384,2048]{2,1,0:T(8,128)(2,1)}, bf16[2,384,2048]{2,1,0:T(8,128)(2,1)}, u32[]{:S(2)}, u32[]{:S(2)}) collective-permute-start(bf16[2,384,2048]{2,1,0:T(8,128)(2,1)} %collective-permute-done.10.refs_7_.refs_22_), channel_id=1, source_target_pairs={{0,8},{8,0},{16,24},{24,16},{1,9},{9,1},{17,25},{25,17},{2,10},{10... | collective-permute-start | bytes 9437192 | tf_op jit(solution)/shard_map/ppermute | solution.py:1235
  761.2 116.0 %collective-permute-start.38 = (bf16[768,2048]{1,0:T(8,128)(2,1)}, bf16[768,2048]{1,0:T(8,128)(2,1)S(1)}, u32[]{:S(2)}, u32[]{:S(2)}) collective-permute-start(bf16[768,2048]{1,0:T(8,128)(2,1)} %convolution_convert_fusion.6), channel_id=1, source_target_pairs={{0,8},{8,0},{16,24},{24,16},{1,9},{9,1},{17,25},{25,17},{2,10},{10... | collective-permute-start | bytes 9437192 | tf_op jit(solution)/shard_map/ppermute | solution.py:1235
  766.0 111.3 %collective-permute-start.40 = (bf16[768,2432]{1,0:T(8,128)(2,1)S(1)}, bf16[768,2432]{1,0:T(8,128)(2,1)}, u32[]{:S(2)}, u32[]{:S(2)}) collective-permute-start(bf16[768,2432]{1,0:T(8,128)(2,1)S(1)} %convolution_convert_fusion.3), channel_id=1, source_target_pairs={{0,8},{8,0},{16,24},{24,16},{1,9},{9,1},{17,25},{25,17},{2,10},{10... | collective-permute-start | bytes 11206664 | tf_op jit(solution)/shard_map/ppermute | solution.py:1235
  781.8 95.5 %collective-permute-start.36 = (bf16[2048,384]{1,0:T(8,128)(2,1)S(1)}, bf16[2048,384]{1,0:T(8,128)(2,1)S(1)}, u32[]{:S(2)}, u32[]{:S(2)}) collective-permute-start(bf16[2048,384]{1,0:T(8,128)(2,1)S(1)} %get-tuple-element.343), channel_id=1, source_target_pairs={{0,16},{8,24},{16,0},{24,8},{1,17},{9,25},{17,1},{25,9},{2,18},{10... | collective-permute-start | bytes 4718600 | tf_op jit(solution)/shard_map/ppermute | solution.py:1235
  786.3 91.0 %collective-permute-start.37 = (bf16[384,2048]{1,0:T(8,128)(2,1)S(1)}, bf16[384,2048]{1,0:T(8,128)(2,1)S(1)}, u32[]{:S(2)}, u32[]{:S(2)}) collective-permute-start(bf16[384,2048]{1,0:T(8,128)(2,1)S(1)} %get-tuple-element.341), channel_id=1, source_target_pairs={{0,16},{8,24},{16,0},{24,8},{1,17},{9,25},{17,1},{25,9},{2,18},{10... | collective-permute-start | bytes 4718600 | tf_op jit(solution)/shard_map/ppermute | solution.py:1235
  792.6 84.8 %collective-permute-start.41 = (bf16[512,768]{1,0:T(8,128)(2,1)S(1)}, bf16[512,768]{1,0:T(8,128)(2,1)S(1)}, u32[]{:S(2)}, u32[]{:S(2)}) collective-permute-start(bf16[512,768]{1,0:T(8,128)(2,1)S(1)} %pad_maximum_fusion.7), channel_id=1, source_target_pairs={{0,1},{1,0},{2,3},{3,2},{4,5},{5,4},{6,7},{7,6},{8,9},{9,8},{10,11... | collective-permute-start | bytes 2359304 | tf_op jit(solution)/shard_map/ppermute | solution.py:1235
  893.7 302.8 %collective-permute-start.42 = (bf16[256,1536]{1,0:T(8,128)(2,1)S(1)}, bf16[256,1536]{1,0:T(8,128)(2,1)}, u32[]{:S(2)}, u32[]{:S(2)}) collective-permute-start(bf16[256,1536]{1,0:T(8,128)(2,1)S(1)} %get-tuple-element.286), channel_id=1, source_target_pairs={{0,1},{1,0},{2,3},{3,2},{4,5},{5,4},{6,7},{7,6},{8,9},{9,8},{10,11... | collective-permute-start | bytes 2359304 | tf_op jit(solution)/shard_map/ppermute | solution.py:1235
  894.3 302.2 %collective-permute-start.43 = (bf16[256,1536]{1,0:T(8,128)(2,1)}, bf16[256,1536]{1,0:T(8,128)(2,1)}, u32[]{:S(2)}, u32[]{:S(2)}) collective-permute-start(bf16[256,1536]{1,0:T(8,128)(2,1)} %get-tuple-element.288), channel_id=1, source_target_pairs={{0,1},{1,0},{2,3},{3,2},{4,5},{5,4},{6,7},{7,6},{8,9},{9,8},{10,11... | collective-permute-start | bytes 2359304 | tf_op jit(solution)/shard_map/ppermute | solution.py:1235
  (112 other events, 850.5 us)
Sparse Core Ops, SparseCore 0:
  635.5 120.1 all-reduce.4
